TPU v7x, 32 devices: a whole 2x2x4 slice. The times are simulated.
32 devices in a mesh: dp: 8 (over z, x), tensor: 4 (over y, core).
Axes of the slice: x: 2, y: 2, z: 4, core: 2. Of those that a mesh axis runs over, the one named last changes fastest.
Arguments:
- residual_in: float32 [4096, 2048], P('dp', 'tensor'), may hold values from -6 to 6
- lengths: int32 [8, 4], P('dp'), may hold values from 1 to 384, 512 in all within a row
- head_bucket: int32 [8, 4], P('dp'), may hold values from 0 to 3, as said below
- width_bucket: int32 [8, 4], P('dp'), may hold values from 0 to 3, as said below
- norm1_gain: float32 [2048], replicated, may hold values from 0.25 to 1.75
- norm1_shift: float32 [2048], replicated, may hold values from -3 to 3
- w_qkv: bfloat16 [2048, 3, 2048], P('dp', None, 'tensor'), may hold values from -0.125 to 0.125
- w_out: bfloat16 [2048, 2048], P('tensor', 'dp'), may hold values from -1 to 1
- norm2_gain: float32 [2048], replicated, may hold values from 0.25 to 1.75
- norm2_shift: float32 [2048], replicated, may hold values from -3 to 3
- w_up: bfloat16 [2048, 8192], P('dp', 'tensor'), may hold values from -0.125 to 0.125
- w_down: bfloat16 [8192, 2048], P('tensor', 'dp'), may hold values from -0.0625 to 0.0625
- cotangent: float32 [4096, 2048], P('dp', 'tensor'), may hold values from -6 to 6
Outputs:
- output: float32 [4096, 2048], P('dp', 'tensor')
- grad_input: float32 [4096, 2048], P('dp', 'tensor')
- grad_norm1_gain: float32 [2048], replicated
- grad_norm1_shift: float32 [2048], replicated
- grad_w_qkv: float32 [2048, 3, 2048], P('dp', None, 'tensor')
- grad_w_out: float32 [2048, 2048], P('tensor', 'dp')
- grad_norm2_gain: float32 [2048], replicated
- grad_norm2_shift: float32 [2048], replicated
- grad_w_up: float32 [2048, 8192], P('dp', 'tensor')
- grad_w_down: float32 [8192, 2048], P('tensor', 'dp')
- bucket_counts: int32 [4], replicated
Inputs may be any that keep to these rules, and one draw needn't show every extreme that they name: `lengths`: each row sums to 512; its largest entry is 384. `head_bucket`: every row of 4 sequences holds at least one bucket 4 - 1. `width_bucket`: every row of 4 sequences holds at least one bucket 4 - 1.
All inputs are finite; a program needn't handle non-finite values.
Results may differ from a plain program's by a relative error of at most 0.033.
Values may be sent and summed in bfloat16 or wider, within the bound.
A program may use at most 192 MiB of HBM per device.

v0:
```python
import math

import jax
import jax.numpy as jnp
from jax import lax
from jax.sharding import PartitionSpec as P

HD = 128


epsilon = 1e-05


def token_info(length_row, head_row, width_row, row_count):
    seq_ends = jnp.cumsum(length_row)
    seq_starts = seq_ends - length_row
    places = jnp.arange(row_count, dtype=jnp.int32)
    segment = jnp.sum((places[:, None] >= seq_ends[None, :]).astype(jnp.int32), axis=1)
    labels = jnp.arange(length_row.shape[0], dtype=jnp.int32)
    onehot = (segment[:, None] == labels[None, :]).astype(jnp.int32)
    offset = places - jnp.sum(onehot * seq_starts[None, :], axis=1)
    head_tok = jnp.sum(onehot * head_row[None, :], axis=1)
    width_tok = jnp.sum(onehot * width_row[None, :], axis=1)
    return (segment, offset, head_tok, width_tok)


def rotary_tables(offset, head_size):
    half_size = head_size // 2
    ladder = jnp.arange(half_size, dtype=jnp.float32)
    inverse = jnp.exp(ladder * (-2.0 * math.log(10000.0) / head_size))
    angles = offset.astype(jnp.float32)[:, None] * inverse[None, :]
    return (jnp.cos(angles)[:, None, :], jnp.sin(angles)[:, None, :])


def rotate(values, cosine, sine_part):
    half_size = values.shape[-1] // 2
    front_half = values[..., :half_size]
    back_half = values[..., half_size:]
    return jnp.concatenate(
        [front_half * cosine - back_half * sine_part, back_half * cosine + front_half * sine_part],
        axis=-1,
    )


def norm_forward(values, norm_gain, norm_shift):
    center = values - jnp.mean(values, axis=-1, keepdims=True)
    spread = jnp.mean(center * center, axis=-1, keepdims=True)
    inverse = lax.rsqrt(spread + epsilon)
    unit_rows = center * inverse
    return (unit_rows * norm_gain + norm_shift, unit_rows, inverse)


def norm_backward(grad_rows, unit_rows, inverse, norm_gain):
    scaled = grad_rows * norm_gain
    grad_in = inverse * (
        scaled
        - jnp.mean(scaled, axis=-1, keepdims=True)
        - unit_rows * jnp.mean(scaled * unit_rows, axis=-1, keepdims=True)
    )
    return (grad_in, jnp.sum(grad_rows * unit_rows, axis=0), jnp.sum(grad_rows, axis=0))


def head_forward(query_rows, key_rows, value_rows, allowed, score_scale):
    scores = jnp.dot(query_rows, key_rows.T, preferred_element_type=jnp.float32) * score_scale
    scores = jnp.where(allowed, scores, -1000000000.0)
    row_max = jnp.max(scores, axis=-1, keepdims=True)
    exp_scores = jnp.exp(scores - row_max)
    row_total = jnp.sum(exp_scores, axis=-1, keepdims=True)
    weights = exp_scores / row_total
    mixed = jnp.dot(weights.astype(jnp.bfloat16), value_rows, preferred_element_type=jnp.float32)
    return (mixed, row_max + jnp.log(row_total))


def head_backward(query_rows, key_rows, value_rows, grad_mixed, log_total, allowed, score_scale):
    scores = jnp.dot(query_rows, key_rows.T, preferred_element_type=jnp.float32) * score_scale
    scores = jnp.where(allowed, scores, -1000000000.0)
    weights = jnp.exp(scores - log_total)
    grad_weights = jnp.dot(grad_mixed, value_rows.T, preferred_element_type=jnp.float32)
    grad_values = jnp.dot(
        weights.astype(jnp.bfloat16).T, grad_mixed, preferred_element_type=jnp.float32
    )
    grad_scores = weights * (grad_weights - jnp.sum(grad_weights * weights, axis=-1, keepdims=True))
    grad_raw = (grad_scores * score_scale).astype(jnp.bfloat16)
    grad_queries = jnp.dot(grad_raw, key_rows, preferred_element_type=jnp.float32)
    grad_keys = jnp.dot(grad_raw.T, query_rows, preferred_element_type=jnp.float32)
    return (grad_queries, grad_keys, grad_values)


def whole_stream(part_rows):
    return lax.all_gather(part_rows.astype(jnp.bfloat16), "tensor", axis=1, tiled=True).astype(
        part_rows.dtype
    )


def stream_sum(part_rows):
    return lax.psum_scatter(
        part_rows.astype(jnp.bfloat16), "tensor", scatter_dimension=1, tiled=True
    ).astype(jnp.float32)


def branch_sum(part_rows):
    return lax.psum_scatter(
        part_rows.astype(jnp.bfloat16), "tensor", scatter_dimension=1, tiled=True
    ).astype(jnp.float32)


def whole_grad(part_rows):
    return lax.all_gather(part_rows, "tensor", axis=1, tiled=True)


def local(
    residual_in,
    lengths,
    head_bucket,
    width_bucket,
    norm1_gain,
    norm1_shift,
    w_qkv,
    w_out,
    norm2_gain,
    norm2_shift,
    w_up,
    w_down,
    cotangent,
):
    tensor_index = lax.axis_index("tensor")
    bucket_total = lax.axis_size("tensor")
    row_count = residual_in.shape[0]
    segment, offset, head_tok, width_tok = token_info(
        lengths[0], head_bucket[0], width_bucket[0], row_count
    )
    matches = (
        width_bucket[0][:, None] == jnp.arange(bucket_total, dtype=jnp.int32)[None, :]
    ).astype(jnp.int32)
    local_counts = jnp.sum(lengths[0][:, None] * matches, axis=0)
    bucket_counts = lax.psum(local_counts, "dp")
    head_mask = (head_tok >= tensor_index).astype(jnp.float32)[:, None, None]
    width_mask = (width_tok >= tensor_index).astype(jnp.float32)[:, None]
    places = jnp.arange(row_count, dtype=jnp.int32)
    allowed = (segment[:, None] == segment[None, :]) & (places[:, None] >= places[None, :])
    cosine, sine_part = rotary_tables(offset, HD)
    score_scale = HD ** (-0.5)
    full_qkv, full_out, full_up, full_down = (
        lax.all_gather(w_qkv, "dp", axis=0, tiled=True),
        lax.all_gather(w_out, "dp", axis=1, tiled=True),
        lax.all_gather(w_up, "dp", axis=0, tiled=True),
        lax.all_gather(w_down, "dp", axis=1, tiled=True),
    )
    model_width = full_qkv.shape[0]
    head_count = full_qkv.shape[2] // HD
    inputs = whole_stream(residual_in)
    normed1, unit1, inverse1 = norm_forward(inputs, norm1_gain, norm1_shift)
    normed1 = normed1.astype(jnp.bfloat16)
    projected = jnp.dot(
        normed1, full_qkv.reshape(model_width, -1), preferred_element_type=jnp.float32
    ).reshape(row_count, 3, head_count, HD)
    query_heads = jnp.swapaxes(
        rotate(projected[:, 0], cosine, sine_part).astype(jnp.bfloat16), 0, 1
    )
    key_heads = jnp.swapaxes(rotate(projected[:, 1], cosine, sine_part).astype(jnp.bfloat16), 0, 1)
    value_heads = jnp.swapaxes(projected[:, 2].astype(jnp.bfloat16), 0, 1)

    def attend(triple):
        return head_forward(triple[0], triple[1], triple[2], allowed, score_scale)

    head_out, log_total = lax.map(attend, (query_heads, key_heads, value_heads))
    mixed = (jnp.swapaxes(head_out, 0, 1) * head_mask).astype(jnp.bfloat16).reshape(row_count, -1)
    middle = residual_in + branch_sum(jnp.dot(mixed, full_out, preferred_element_type=jnp.float32))
    middle_rows = whole_stream(middle)
    normed2, unit2, inverse2 = norm_forward(middle_rows, norm2_gain, norm2_shift)
    normed2 = normed2.astype(jnp.bfloat16)
    upper = jnp.dot(normed2, full_up, preferred_element_type=jnp.float32)
    active = (jnp.square(jnp.maximum(upper, 0.0)) * width_mask).astype(jnp.bfloat16)
    output = middle + branch_sum(jnp.dot(active, full_down, preferred_element_type=jnp.float32))
    back_qkv, back_out, back_up, back_down = (full_qkv, full_out, full_up, full_down)
    grad_top = whole_grad(cotangent.astype(jnp.bfloat16))
    grad_down = jnp.dot(active.T, grad_top, preferred_element_type=jnp.float32)
    grad_active = jnp.dot(grad_top, back_down.T, preferred_element_type=jnp.float32)
    grad_upper = (grad_active * width_mask * 2.0 * jnp.maximum(upper, 0.0)).astype(jnp.bfloat16)
    grad_up = jnp.dot(normed2.T, grad_upper, preferred_element_type=jnp.float32)
    grad_normed2 = jnp.dot(grad_upper, back_up.T, preferred_element_type=jnp.float32)
    part_middle, gain2_grad, shift2_grad = norm_backward(grad_normed2, unit2, inverse2, norm2_gain)
    grad_middle = cotangent + stream_sum(part_middle)
    grad_branch = whole_grad(grad_middle.astype(jnp.bfloat16))
    grad_wout = jnp.dot(mixed.T, grad_branch, preferred_element_type=jnp.float32)
    grad_mixed = jnp.dot(grad_branch, back_out.T, preferred_element_type=jnp.float32).astype(
        jnp.bfloat16
    )
    grad_mixed = grad_mixed.reshape(row_count, head_count, HD) * head_mask.astype(jnp.bfloat16)
    grad_heads = jnp.swapaxes(grad_mixed, 0, 1)

    def attend_back(group):
        return head_backward(group[0], group[1], group[2], group[3], group[4], allowed, score_scale)

    grad_query, grad_key, grad_value = lax.map(
        attend_back, (query_heads, key_heads, value_heads, grad_heads, log_total)
    )
    grad_query = rotate(jnp.swapaxes(grad_query, 0, 1), cosine, -sine_part)
    grad_key = rotate(jnp.swapaxes(grad_key, 0, 1), cosine, -sine_part)
    grad_value = jnp.swapaxes(grad_value, 0, 1)
    grad_projected = (
        jnp.stack([grad_query, grad_key, grad_value], axis=1)
        .astype(jnp.bfloat16)
        .reshape(row_count, -1)
    )
    grad_qkv = jnp.dot(normed1.T, grad_projected, preferred_element_type=jnp.float32).reshape(
        model_width, 3, head_count * HD
    )
    grad_normed1 = jnp.dot(
        grad_projected, back_qkv.reshape(model_width, -1).T, preferred_element_type=jnp.float32
    )
    part_input, gain1_grad, shift1_grad = norm_backward(grad_normed1, unit1, inverse1, norm1_gain)
    grad_input = grad_middle + stream_sum(part_input)
    grad_qkv, grad_wout, grad_up, grad_down = (
        lax.psum_scatter(
            grad_qkv.astype(jnp.bfloat16), "dp", scatter_dimension=0, tiled=True
        ).astype(jnp.float32),
        lax.psum_scatter(
            grad_wout.astype(jnp.bfloat16), "dp", scatter_dimension=1, tiled=True
        ).astype(jnp.float32),
        lax.psum_scatter(
            grad_up.astype(jnp.bfloat16), "dp", scatter_dimension=0, tiled=True
        ).astype(jnp.float32),
        lax.psum_scatter(
            grad_down.astype(jnp.bfloat16), "dp", scatter_dimension=1, tiled=True
        ).astype(jnp.float32),
    )
    gain1_grad, shift1_grad, gain2_grad, shift2_grad = lax.psum(
        (gain1_grad, shift1_grad, gain2_grad, shift2_grad), ("dp", "tensor")
    )
    return (
        output,
        grad_input,
        gain1_grad,
        shift1_grad,
        grad_qkv,
        grad_wout,
        gain2_grad,
        shift2_grad,
        grad_up,
        grad_down,
        bucket_counts,
    )


def solution(mesh):
    placed = (
        P("dp", "tensor"),
        P("dp", None),
        P("dp", None),
        P("dp", None),
        P(),
        P(),
        P("dp", None, "tensor"),
        P("tensor", "dp"),
        P(),
        P(),
        P("dp", "tensor"),
        P("tensor", "dp"),
        P("dp", "tensor"),
    )
    return jax.shard_map(
        local,
        mesh=mesh,
        in_specs=placed,
        out_specs=(
            P("dp", "tensor"),
            P("dp", "tensor"),
            P(),
            P(),
            P("dp", None, "tensor"),
            P("tensor", "dp"),
            P(),
            P(),
            P("dp", "tensor"),
            P("tensor", "dp"),
            P(),
        ),
        check_vma=False,
    )
```

profile of v0, /device:TPU:0, one launch (start us, length us, event | category | flops | bytes accessed | tf_op | source)
XLA Modules:
  0.0 1178.2 jit_solution(16343150201479456839)
XLA Ops:
  14.6 20.9 %all-gather.9.cloned.1.call-done = bf16[512,2048]{1,0:T(8,128)(2,1)} async-done(((bf16[512,512]{1,0:T(8,128)(2,1)}), bf16[512,2048]{1,0:T(8,128)(2,1)}) %all-gather.9.cloned.1.call-update) | async-done | bytes 2097168 | tf_op jit(solution)/shard_map/all_gather | solution.py:90
  39.9 98.2 %all-gather.11.cloned.1.call-done = bf16[2048,3,512]{0,2,1:T(8,128)(2,1)} async-done(((bf16[256,3,512]{0,2,1:T(8,128)(2,1)}), bf16[2048,3,512]{0,2,1:T(8,128)(2,1)}) %all-gather.11.cloned.1.call-update) | async-done | bytes 6291472 | tf_op jit(solution)/shard_map/all_gather | solution.py:144
  138.1 5.9 fusion.74
  151.5 13.9 %while.28 = (s32[]{:T(128)}, f32[4,512,128]{1,2,0:T(8,128)}, f32[4,512,1]{1,2,0:T(1,128)S(1)}, bf16[4,512,128]{2,1,0:T(8,128)(2,1)}, bf16[4,512,128]{2,1,0:T(8,1...) while((s32[]{:T(128)}, f32[4,512,128]{1,2,0:T(8,128)}, ...), condition=%wide.region_8.9_spmd.clone, body=%wide.region_5.0_spmd.clone.sunk | while | flops 137100800 | bytes 3827809 | solution.py:166
  167.6 21.9 %all-gather.13.cloned.1.call-done = bf16[512,2048]{1,0:T(8,128)(2,1)} async-done(((bf16[512,256]{1,0:T(8,128)(2,1)}), bf16[512,2048]{1,0:T(8,128)(2,1)}) %all-gather.13.cloned.1.call-update) | async-done | bytes 2097168 | tf_op jit(solution)/shard_map/all_gather | solution.py:145
  189.4 4.4 convolution_convert_fusion.5
  193.9 29.7 %reduce-scatter.9.cloned.1.call-done = bf16[512,512]{1,0:T(8,128)(2,1)} async-done(((bf16[512,2048]{1,0:T(8,128)(2,1)}), bf16[512,512]{1,0:T(8,128)(2,1)}) %reduce-scatter.9.cloned.1.call-update) | async-done | bytes 524304 | tf_op jit(solution)/shard_map/reduce_scatter | solution.py:102
  229.4 19.0 %all-gather.15.cloned.1.call-done = bf16[512,2048]{1,0:T(8,128)(2,1)} async-done(((bf16[512,512]{1,0:T(8,128)(2,1)}), bf16[512,2048]{1,0:T(8,128)(2,1)}) %all-gather.15.cloned.1.call-update) | async-done | bytes 2097168 | tf_op jit(solution)/shard_map/all_gather | solution.py:90
  252.6 122.9 %all-gather.17.cloned.1.call-done = bf16[2048,2048]{1,0:T(8,128)(2,1)} async-done(((bf16[256,2048]{1,0:T(8,128)(2,1)}), bf16[2048,2048]{1,0:T(8,128)(2,1)}) %all-gather.17.cloned.1.call-update) | async-done | bytes 8388624 | tf_op jit(solution)/shard_map/all_gather | solution.py:146
  375.5 10.6 fusion.85
  386.1 12.4 %all-gather.21.cloned.1.call-done = bf16[512,2048]{1,0:T(8,128)(2,1)} async-done(((bf16[512,512]{1,0:T(8,128)(2,1)}), bf16[512,2048]{1,0:T(8,128)(2,1)}) %all-gather.21.cloned.1.call-update) | async-done | bytes 2097168 | tf_op jit(solution)/shard_map/all_gather | solution.py:108
  398.5 127.7 %all-gather.19.cloned.1.call-done = bf16[2048,2048]{1,0:T(8,128)(2,1)} async-done(((bf16[2048,256]{1,0:T(8,128)(2,1)}), bf16[2048,2048]{1,0:T(8,128)(2,1)}) %all-gather.19.cloned.1.call-update) | async-done | bytes 8388624 | tf_op jit(solution)/shard_map/all_gather | solution.py:147
  526.2 10.0 multiply_convert_fusion.1
  536.2 8.8 fusion.64
  545.0 2.5 fusion.63
  547.6 29.7 %reduce-scatter.13.cloned.1.call-done = bf16[512,512]{1,0:T(8,128)(2,1)} async-done(((bf16[512,2048]{1,0:T(8,128)(2,1)}), bf16[512,512]{1,0:T(8,128)(2,1)}) %reduce-scatter.13.cloned.1.call-update) | async-done | bytes 524304 | tf_op jit(solution)/shard_map/reduce_scatter | solution.py:96
  579.9 10.5 convolution_convert_fusion.4
  591.3 11.0 all-gather.23.cloned.1.call-done
  602.4 4.3 convolution_convert_fusion.6
  610.7 4.4 convolution_convert_fusion.3
  617.4 35.3 %while.29 = (s32[]{:T(128)}, f32[4,512,128]{1,2,0:T(8,128)}, f32[4,512,128]{1,2,0:T(8,128)}, bf16[4,512,128]{1,2,0:T(8,128)(2,1)}, bf16[4,512,128]{2,1,0:T(8,128...) while((s32[]{:T(128)}, f32[4,512,128]{1,2,0:T(8,128)}, ...), condition=%wide.region_20.21_spmd.clone, body=%wide.region_18.20_spmd.clone.sunk | while | flops 338951680 | bytes 13782193 | solution.py:195
  654.9 7.1 fusion.72
  664.9 10.2 convolution_convert_fusion.1
  675.2 10.7 convolution_convert_fusion
  686.6 7.3 convolution_convert_fusion.2
  694.6 12.2 %psum.39 = s32[4]{0:T(128)} all-reduce(s32[4]{0:T(128)S(1)} %select_reduce_fusion.3), channel_id=1, replica_groups=mesh['dp'=8,'tensor'=4] {'dp'}, use_global_device_ids=true, to_apply=%region_37.38 | all-reduce | flops 4 | bytes 32 | tf_op jit(solution)/shard_map/psum | solution.py:136
  709.1 39.1 %all-reduce = (f32[2048]{0:T(1024)}, f32[2048]{0:T(1024)}, f32[2048]{0:T(1024)}, f32[2048]{0:T(1024)}) all-reduce(f32[2048]{0:T(1024)S(1)} %get-tuple-element.201, f32[2048]{0:T(1024)S(1)} %get-tuple-element.206, f32[2048]{0:T(1024)S(1)} %get-tuple-element.199, ...), channel_id=1, replica_groups=mesh['dp'=8,'tensor'=4] {'dp','tensor'}, use_global_device_ids=true, to_apply=%region_25.26 | all-reduce | flops 8192 | bytes 65536 | tf_op jit(solution)/shard_map/psum | solution.py:228
  752.2 143.3 %reduce-scatter.21.cloned.1.call-done = bf16[256,2048]{1,0:T(8,128)(2,1)} async-done(((bf16[2048,2048]{1,0:T(8,128)(2,1)}), bf16[256,2048]{1,0:T(8,128)(2,1)}) %reduce-scatter.21.cloned.1.call-update) | async-done | bytes 1048592 | tf_op jit(solution)/shard_map/reduce_scatter | solution.py:221
  895.5 2.8 convert_element_type.187
  898.3 149.6 %reduce-scatter.23.cloned.1.call-done = bf16[2048,256]{1,0:T(8,128)(2,1)} async-done(((bf16[2048,2048]{1,0:T(8,128)(2,1)}), bf16[2048,256]{1,0:T(8,128)(2,1)}) %reduce-scatter.23.cloned.1.call-update) | async-done | bytes 1048592 | tf_op jit(solution)/shard_map/reduce_scatter | solution.py:224
  1047.9 2.7 convert_element_type.189
  1050.6 118.1 %reduce-scatter.17.cloned.1.call-done = bf16[256,3,512]{2,0,1:T(8,128)(2,1)} async-done(((bf16[2048,3,512]{2,0,1:T(8,128)(2,1)}), bf16[256,3,512]{2,0,1:T(8,128)(2,1)}) %reduce-scatter.17.cloned.1.call-update) | async-done | bytes 786448 | tf_op jit(solution)/shard_map/reduce_scatter | solution.py:215
  (204 shorter events, 105.4 us)
Async XLA Ops:
  7.2 28.3 %all-gather.9.cloned.1.call-start = ((), (), s32[]{:S(2)}) async-start(), calls=%async_computation.8 | async-start | bytes 2621440 | tf_op jit(solution)/shard_map/all_gather | solution.py:90
  9.3 128.7 %copy-start.15 = (f32[2048]{0:T(1024)S(1)}, f32[2048]{0:T(1024)}, u32[]{:S(2)}) copy-start(f32[2048]{0:T(1024)} %param.21) | copy-start | bytes 24580
  9.3 128.8 %copy-start.24 = (f32[2048]{0:T(1024)S(1)}, f32[2048]{0:T(1024)}, u32[]{:S(2)}) copy-start(f32[2048]{0:T(1024)} %param.22) | copy-start | bytes 24580
  9.4 128.7 %all-gather.11.cloned.1.call-start = ((), (), s32[]{:S(2)}) async-start(), calls=%async_computation.9 | async-start | bytes 7077888 | tf_op jit(solution)/shard_map/all_gather | solution.py:144
  11.7 177.7 %all-gather.13.cloned.1.call-start = ((), (), s32[]{:S(2)}) async-start(), calls=%async_computation.10 | async-start | bytes 2359296 | tf_op jit(solution)/shard_map/all_gather | solution.py:145
  12.5 211.1 %reduce-scatter.9.cloned.1.call-start = ((), (), s32[]{:S(2)}) async-start(), calls=%async_computation.11 | async-start | bytes 2621440 | tf_op jit(solution)/shard_map/reduce_scatter | solution.py:102
  35.5 102.6 %copy-start = (bf16[512,2048]{1,0:T(8,128)(2,1)S(1)}, bf16[512,2048]{1,0:T(8,128)(2,1)}, u32[]{:S(2)}) copy-start(bf16[512,2048]{1,0:T(8,128)(2,1)} %all-gather.9.cloned.1.call-done) | copy-start | bytes 6291460
  39.9 98.2 %copy-start.17 = (f32[512]{0:T(512)}, f32[512]{0:T(512)S(1)}, u32[]{:S(2)}) copy-start(f32[512]{0:T(512)S(1)} %add_rsqrt_fusion.1) | copy-start | bytes 6148
  167.6 56.0 %copy-start.2 = (f32[512,512]{1,0:T(8,128)S(1)}, f32[512,512]{1,0:T(8,128)}, u32[]{:S(2)}) copy-start(f32[512,512]{1,0:T(8,128)} %param.17) | copy-start | bytes 3145732
  193.8 35.5 %copy-start.13 = (s32[512]{0:T(512)S(1)}, s32[512]{0:T(512)}, u32[]{:S(2)}) copy-start(s32[512]{0:T(512)} %get-tuple-element.207) | copy-start | bytes 6148
  193.8 54.5 %all-gather.15.cloned.1.call-start = ((), (), s32[]{:S(2)}) async-start(), calls=%async_computation.12 | async-start | bytes 2621440 | tf_op jit(solution)/shard_map/all_gather | solution.py:90
  225.6 149.9 %copy-start.14 = (f32[2048]{0:T(1024)S(1)}, f32[2048]{0:T(1024)}, u32[]{:S(2)}) copy-start(f32[2048]{0:T(1024)} %param.25) | copy-start | bytes 24580
  225.6 149.9 %copy-start.23 = (f32[2048]{0:T(1024)S(1)}, f32[2048]{0:T(1024)}, u32[]{:S(2)}) copy-start(f32[2048]{0:T(1024)} %param.26) | copy-start | bytes 24580
  225.6 149.9 %all-gather.17.cloned.1.call-start = ((), (), s32[]{:S(2)}) async-start(), calls=%async_computation.13 | async-start | bytes 9437184 | tf_op jit(solution)/shard_map/all_gather | solution.py:146
  226.2 172.3 %all-gather.21.cloned.1.call-start = ((), (), s32[]{:S(2)}) async-start(), calls=%async_computation.16 | async-start | bytes 2621440 | tf_op jit(solution)/shard_map/all_gather | solution.py:108
  228.4 297.8 %all-gather.19.cloned.1.call-start = ((), (), s32[]{:S(2)}) async-start(), calls=%async_computation.14 | async-start | bytes 9437184 | tf_op jit(solution)/shard_map/all_gather | solution.py:147
  229.1 348.2 %reduce-scatter.13.cloned.1.call-start = ((), (), s32[]{:S(2)}) async-start(), calls=%async_computation.17 | async-start | bytes 2621440 | tf_op jit(solution)/shard_map/reduce_scatter | solution.py:96
  526.2 10.0 copy-start.1
  536.2 8.8 copy-start.28
  547.5 54.8 %all-gather.23.cloned.1.call-start = ((), (), s32[]{:S(2)}) async-start(), calls=%async_computation.18 | async-start | bytes 2621440 | tf_op jit(solution)/shard_map/all_gather | solution.py:108
  579.6 127.2 %reduce-scatter.11.cloned.1.call-start = ((), (), s32[]{:S(2)}) async-start(), calls=%async_computation.15 | async-start | bytes 2621440 | tf_op jit(solution)/shard_map/reduce_scatter | solution.py:102
  590.4 157.8 %reduce-scatter.19.cloned.1.call-start = ((), (), s32[]{:S(2)}) async-start(), calls=%async_computation.21 | async-start | bytes 2359296 | tf_op jit(solution)/shard_map/reduce_scatter | solution.py:218
  591.3 17.4 %copy-start.19 = (bf16[512]{0:T(512)(128)(2,1)S(1)}, bf16[512]{0:T(512)(128)(2,1)}, u32[]{:S(2)}) copy-start(bf16[512]{0:T(512)(128)(2,1)} %get-tuple-element.248) | copy-start | bytes 3076
  615.1 134.9 %reduce-scatter.15.cloned.1.call-start = ((), (), s32[]{:S(2)}) async-start(), calls=%async_computation.19 | async-start | bytes 2621440 | tf_op jit(solution)/shard_map/reduce_scatter | solution.py:96
  617.4 6.8 copy-start.5
  654.8 7.1 copy-start.10
  664.6 231.0 %reduce-scatter.21.cloned.1.call-start = ((), (), s32[]{:S(2)}) async-start(), calls=%async_computation.22 | async-start | bytes 9437184 | tf_op jit(solution)/shard_map/reduce_scatter | solution.py:221
  675.1 372.8 %reduce-scatter.23.cloned.1.call-start = ((), (), s32[]{:S(2)}) async-start(), calls=%async_computation.23 | async-start | bytes 9437184 | tf_op jit(solution)/shard_map/reduce_scatter | solution.py:224
  685.9 482.8 %reduce-scatter.17.cloned.1.call-start = ((), (), s32[]{:S(2)}) async-start(), calls=%async_computation.20 | async-start | bytes 7077888 | tf_op jit(solution)/shard_map/reduce_scatter | solution.py:215
  693.9 13.0 %copy-start.8 = (bf16[512,512]{1,0:T(8,128)(2,1)S(1)}, bf16[512,512]{1,0:T(8,128)(2,1)}, u32[]{:S(2)}) copy-start(bf16[512,512]{1,0:T(8,128)(2,1)} %reduce-scatter.9.cloned.1.call-done) | copy-start | bytes 1572868
  693.9 56.1 %copy-start.3 = (f32[512,512]{1,0:T(8,128)S(1)}, f32[512,512]{1,0:T(8,128)}, u32[]{:S(2)}) copy-start(f32[512,512]{1,0:T(8,128)} %param.29) | copy-start | bytes 3145732
  693.9 56.1 %copy-start.9 = (bf16[512,512]{1,0:T(8,128)(2,1)S(1)}, bf16[512,512]{1,0:T(8,128)(2,1)}, u32[]{:S(2)}) copy-start(bf16[512,512]{1,0:T(8,128)(2,1)} %reduce-scatter.13.cloned.1.call-done) | copy-start | bytes 1572868
  (19 other events, 60.6 us)
Sparse Core Ops, SparseCore 0:
  10.2 25.2 all-gather.8
  38.1 99.9 all-gather.10
  140.1 49.2 all-gather.12
  193.9 29.5 reduce-scatter.8
  225.7 22.5 all-gather.14
  250.6 124.9 all-gather.16
  377.7 20.7 all-gather.20
  400.8 125.3 all-gather.18
  547.7 29.5 reduce-scatter.12
  579.7 22.5 all-gather.22
  605.5 31.4 reduce-scatter.10
  640.7 68.1 reduce-scatter.18
  712.2 30.6 reduce-scatter.14
  746.4 149.0 reduce-scatter.20
  899.4 148.3 reduce-scatter.22
  1051.3 117.3 reduce-scatter.16
where the time goes:
time: 1190 us; the launch traced here: 1180 us
  waiting for transfers between devices  906 us (76%)
  matrix products  138 us (12%)
  blocking collectives  51.3 us (4%)
  other arithmetic  48.7 us (4%)
  local copies, waits for them, and re-layouts  17.5 us (1%)
  between operations  14.8 us (1%)
    reduce_scatter x1, waiting for transfers between devices, local(): lax.psum_scatter(grad_down.astype(jnp.bfloat16), 'dp', scatter_dimension=...  150 us
    reduce_scatter x1, waiting for transfers between devices, local(): lax.psum_scatter(grad_up.astype(jnp.bfloat16), 'dp', scatter_dimension=0,...  143 us
    all_gather x1, waiting for transfers between devices, local(): lax.all_gather(w_down, 'dp', axis=1, tiled=True)  128 us
    all_gather x1, waiting for transfers between devices, local(): lax.all_gather(w_up, 'dp', axis=0, tiled=True)  123 us
    reduce_scatter x1, waiting for transfers between devices, local(): lax.psum_scatter(grad_qkv.astype(jnp.bfloat16), 'dp', scatter_dimension=0...  118 us
    all_gather x1, waiting for transfers between devices, local(): lax.all_gather(w_qkv, 'dp', axis=0, tiled=True)  98.2 us
    all_gather x2, waiting for transfers between devices, whole_stream(): lax.all_gather(part_rows.astype(jnp.bfloat16), 'tensor', axis=1, tiled=True)  39.9 us
    psum x1, blocking collectives, local(): lax.psum((gain1_grad, shift1_grad, gain2_grad, shift2_grad), ('dp', 'tens...  39.1 us
  transfers between devices with their start and end apart: 16, of which 13 were waited for; matrix products, arithmetic and copies ran while one was open for 14% of the time, Pallas kernels for 0%

commit v1 on v0

v1 whole, which is shorter than its diff:
```python
import functools
import math

import jax
import jax.numpy as jnp
from jax import lax
from jax.experimental import pallas as pl
from jax.experimental.pallas import tpu as pltpu
from jax.sharding import PartitionSpec as P

HD = 128
HIDDEN_BIT = 2

epsilon = 1e-05


def dp_swap(value, bit):
    count = lax.axis_size("dp")
    return lax.ppermute(value, "dp", [(i, i ^ bit) for i in range(count)])


def tensor_swap(value, bit):
    count = lax.axis_size("tensor")
    return lax.ppermute(value, "tensor", [(i, i ^ bit) for i in range(count)])


def bits_of(count):
    return [1 << i for i in range(count.bit_length() - 1)]


def replica_bits():
    bits = bits_of(lax.axis_size("dp"))
    return [b for b in bits if b > HIDDEN_BIT] + [b for b in bits if b < HIDDEN_BIT]


def gather_weight(mine, other):
    blocks = {0: mine, HIDDEN_BIT: dp_swap(other, HIDDEN_BIT)}
    for bit in replica_bits():
        blocks.update({m | bit: dp_swap(blocks[m], bit) for m in list(blocks)})
    return blocks


def add_low(left, right):
    return (left.astype(jnp.float32) + right.astype(jnp.float32)).astype(jnp.bfloat16)


def scatter_weight(blocks):
    for bit in reversed(replica_bits()):
        arrived = {m ^ bit: dp_swap(blocks[m], bit) for m in blocks if m & bit}
        blocks = {m: add_low(blocks[m], arrived[m]) for m in arrived}
    return blocks[0], dp_swap(blocks[HIDDEN_BIT], HIDDEN_BIT)


def gather_act(rows):
    blocks = {(0, 0): rows, (1, 0): dp_swap(rows, HIDDEN_BIT)}
    for bit in reversed(bits_of(lax.axis_size("tensor"))):
        blocks.update({(b, m | bit): tensor_swap(v, bit) for (b, m), v in list(blocks.items())})
    return blocks


def scatter_act(blocks):
    for bit in bits_of(lax.axis_size("tensor")):
        arrived = {(b, m ^ bit): tensor_swap(v, bit) for (b, m), v in blocks.items() if m & bit}
        blocks = {k: add_low(blocks[k], arrived[k]) for k in arrived}
    return blocks[(0, 0)].astype(jnp.float32) + dp_swap(blocks[(1, 0)], HIDDEN_BIT).astype(
        jnp.float32
    )


def lay(blocks, shape, spots):
    count = len(blocks)

    def kernel(*refs):
        ins, out, sems = refs[:count], refs[count], refs[count + 1]
        copies = []
        for i, spot in enumerate(spots()):
            r, c = blocks[i].shape
            copies.append(
                pltpu.make_async_copy(
                    ins[i],
                    out.at[pl.ds(pl.multiple_of(spot[0], 16), r), pl.ds(pl.multiple_of(spot[1], 128), c)],
                    sems.at[i],
                )
            )
        for copy in copies:
            copy.start()
        for copy in copies:
            copy.wait()

    return pl.pallas_call(
        kernel,
        out_shape=jax.ShapeDtypeStruct(shape, jnp.bfloat16),
        in_specs=[pl.BlockSpec(memory_space=pl.ANY)] * count,
        out_specs=pl.BlockSpec(memory_space=pltpu.VMEM),
        scratch_shapes=[pltpu.SemaphoreType.DMA((count,))],
        compiler_params=pltpu.CompilerParams(vmem_limit_bytes=24 << 20),
    )(*blocks)


def cut(whole, block_shape, count, spots):
    def kernel(*refs):
        src, outs, sems = refs[0], refs[1 : 1 + count], refs[1 + count]
        r, c = block_shape
        copies = []
        for i, spot in enumerate(spots()):
            copies.append(
                pltpu.make_async_copy(
                    src.at[pl.ds(pl.multiple_of(spot[0], 16), r), pl.ds(pl.multiple_of(spot[1], 128), c)],
                    outs[i],
                    sems.at[i],
                )
            )
        for copy in copies:
            copy.start()
        for copy in copies:
            copy.wait()

    return pl.pallas_call(
        kernel,
        out_shape=[jax.ShapeDtypeStruct(block_shape, jnp.bfloat16)] * count,
        in_specs=[pl.BlockSpec(memory_space=pltpu.VMEM)],
        out_specs=[pl.BlockSpec(memory_space=pl.ANY)] * count,
        scratch_shapes=[pltpu.SemaphoreType.DMA((count,))],
        compiler_params=pltpu.CompilerParams(vmem_limit_bytes=24 << 20),
    )(whole)


def lay_weight(blocks, axis):
    count = len(blocks)
    r, c = blocks[0].shape
    if axis == 1 and c % 128:
        order = jnp.bitwise_xor(lax.axis_index("dp"), jnp.arange(count))
        stacked = jnp.stack([blocks[m] for m in range(count)])[order]
        return jnp.swapaxes(stacked, 0, 1).reshape(r, count * c)

    def spots():
        place = lax.axis_index("dp")
        at = [jnp.bitwise_xor(place, m) for m in range(count)]
        return [(d * r, 0) if axis == 0 else (0, d * c) for d in at]

    shape = (r * count, c) if axis == 0 else (r, c * count)
    return lay([blocks[m] for m in range(count)], shape, spots)


def cut_weight(whole, axis):
    count = lax.axis_size("dp")
    r, c = whole.shape
    r, c = (r // count, c) if axis == 0 else (r, c // count)
    if axis == 1 and c % 128:
        order = jnp.bitwise_xor(lax.axis_index("dp"), jnp.arange(count))
        stacked = jnp.swapaxes(whole.reshape(r, count, c), 0, 1)[order]
        return {m: stacked[m] for m in range(count)}

    def spots():
        place = lax.axis_index("dp")
        at = [jnp.bitwise_xor(place, m) for m in range(count)]
        return [(d * r, 0) if axis == 0 else (0, d * c) for d in at]

    return dict(enumerate(cut(whole, (r, c), count, spots)))


def act_keys():
    return [(b, m) for b in range(2) for m in range(lax.axis_size("tensor"))]


def act_spots(r, c):
    place = lax.axis_index("tensor")
    return [(b * r, jnp.bitwise_xor(place, m) * c) for b, m in act_keys()]


def lay_act(blocks):
    r, c = blocks[(0, 0)].shape
    shape = (2 * r, c * lax.axis_size("tensor"))
    return lay([blocks[k] for k in act_keys()], shape, lambda: act_spots(r, c))


def cut_act(whole):
    r, c = whole.shape[0] // 2, whole.shape[1] // lax.axis_size("tensor")
    keys = act_keys()
    return dict(zip(keys, cut(whole, (r, c), len(keys), lambda: act_spots(r, c))))


def whole_stream(rows):
    return lay_act(gather_act(rows.astype(jnp.bfloat16)))


def stream_sum(rows):
    return scatter_act(cut_act(rows.astype(jnp.bfloat16)))


def sum_all(value, axes):
    if "dp" in axes:
        for bit in bits_of(lax.axis_size("dp")):
            value = value + dp_swap(value, bit)
    if "tensor" in axes:
        for bit in bits_of(lax.axis_size("tensor")):
            value = value + tensor_swap(value, bit)
    return value


def token_info(length_row, head_row, width_row, row_count):
    seq_ends = jnp.cumsum(length_row)
    seq_starts = seq_ends - length_row
    places = jnp.arange(row_count, dtype=jnp.int32)
    segment = jnp.sum((places[:, None] >= seq_ends[None, :]).astype(jnp.int32), axis=1)
    labels = jnp.arange(length_row.shape[0], dtype=jnp.int32)
    onehot = (segment[:, None] == labels[None, :]).astype(jnp.int32)
    offset = places - jnp.sum(onehot * seq_starts[None, :], axis=1)
    head_tok = jnp.sum(onehot * head_row[None, :], axis=1)
    width_tok = jnp.sum(onehot * width_row[None, :], axis=1)
    return (segment, offset, head_tok, width_tok)


def rotary_tables(offset, head_size):
    half_size = head_size // 2
    ladder = jnp.arange(half_size, dtype=jnp.float32)
    inverse = jnp.exp(ladder * (-2.0 * math.log(10000.0) / head_size))
    angles = offset.astype(jnp.float32)[:, None] * inverse[None, :]
    return (jnp.cos(angles)[:, None, :], jnp.sin(angles)[:, None, :])


def rotate(values, cosine, sine_part):
    half_size = values.shape[-1] // 2
    front_half = values[..., :half_size]
    back_half = values[..., half_size:]
    return jnp.concatenate(
        [front_half * cosine - back_half * sine_part, back_half * cosine + front_half * sine_part],
        axis=-1,
    )


def norm_forward(values, norm_gain, norm_shift):
    values = values.astype(jnp.float32)
    center = values - jnp.mean(values, axis=-1, keepdims=True)
    spread = jnp.mean(center * center, axis=-1, keepdims=True)
    inverse = lax.rsqrt(spread + epsilon)
    unit_rows = center * inverse
    return (unit_rows * norm_gain + norm_shift, unit_rows, inverse)


def norm_backward(grad_rows, unit_rows, inverse, norm_gain):
    scaled = grad_rows * norm_gain
    grad_in = inverse * (
        scaled
        - jnp.mean(scaled, axis=-1, keepdims=True)
        - unit_rows * jnp.mean(scaled * unit_rows, axis=-1, keepdims=True)
    )
    return (grad_in, jnp.sum(grad_rows * unit_rows, axis=0), jnp.sum(grad_rows, axis=0))


def heads_of(rows, blocks):
    rows = rows.reshape(blocks, rows.shape[0] // blocks, -1, HD)
    return jnp.transpose(rows, (2, 0, 1, 3)).reshape(-1, rows.shape[1], HD)


def rows_of(heads, blocks):
    heads = heads.reshape(-1, blocks, heads.shape[1], HD)
    return jnp.transpose(heads, (1, 2, 0, 3)).reshape(blocks * heads.shape[2], -1)


def local(
    residual_in,
    lengths,
    head_bucket,
    width_bucket,
    norm1_gain,
    norm1_shift,
    w_qkv,
    w_out,
    norm2_gain,
    norm2_shift,
    w_up,
    w_down,
    cotangent,
):
    f32, bf16 = jnp.float32, jnp.bfloat16
    dot = functools.partial(jnp.dot, preferred_element_type=f32)
    tensor_index = lax.axis_index("tensor")
    bucket_total = lax.axis_size("tensor")
    tokens = residual_in.shape[0]
    side = (lax.axis_index("dp") // HIDDEN_BIT) % 2

    def halves(weight, axis):
        left, right = jnp.split(weight, 2, axis=axis)
        return jnp.where(side == 0, left, right), jnp.where(side == 0, right, left)

    info = jnp.stack([lengths[0], head_bucket[0], width_bucket[0]])
    far_info = dp_swap(info, HIDDEN_BIT)
    pair = [token_info(i[0], i[1], i[2], tokens) for i in (info, far_info)]
    segment, offset, head_tok, width_tok = [jnp.stack([a, b]) for a, b in zip(*pair)]
    matches = (
        width_bucket[0][:, None] == jnp.arange(bucket_total, dtype=jnp.int32)[None, :]
    ).astype(jnp.int32)
    bucket_counts = sum_all(jnp.sum(lengths[0][:, None] * matches, axis=0), ("dp",))
    head_mask = (head_tok.reshape(-1) >= tensor_index).astype(f32)[:, None]
    width_mask = (width_tok.reshape(-1) >= tensor_index).astype(f32)[:, None]
    places = jnp.arange(tokens, dtype=jnp.int32)
    allowed = (segment[:, :, None] == segment[:, None, :]) & (
        places[:, None] >= places[None, :]
    )
    cosine, sine_part = rotary_tables(offset.reshape(-1), HD)
    score_scale = HD ** (-0.5)

    qkv_halves = [h.reshape(h.shape[0], -1) for h in halves(w_qkv, 2)]
    full_qkv = lay_weight(gather_weight(*qkv_halves), 0)
    full_out = lay_weight(gather_weight(*halves(w_out, 0)), 1)
    full_up = lay_weight(gather_weight(*halves(w_up, 1)), 0)
    full_down = lay_weight(gather_weight(*halves(w_down, 0)), 1)

    inputs = whole_stream(residual_in)
    normed1, unit1, inverse1 = norm_forward(inputs, norm1_gain, norm1_shift)
    normed1 = normed1.astype(bf16)
    projected = dot(normed1, full_qkv).reshape(2 * tokens, 3, -1, HD)
    width = projected.shape[2] * HD
    query = rotate(projected[:, 0], cosine, sine_part).astype(bf16).reshape(-1, width)
    key = rotate(projected[:, 1], cosine, sine_part).astype(bf16).reshape(-1, width)
    value = projected[:, 2].astype(bf16).reshape(-1, width)
    query, key, value = heads_of(query, 2), heads_of(key, 2), heads_of(value, 2)
    allowed = jnp.tile(allowed, (query.shape[0] // 2, 1, 1))
    scores = jnp.einsum("nqd,nkd->nqk", query, key, preferred_element_type=f32) * score_scale
    scores = jnp.where(allowed, scores, -1000000000.0)
    scores = jnp.exp(scores - jnp.max(scores, axis=-1, keepdims=True))
    weights = (scores / jnp.sum(scores, axis=-1, keepdims=True)).astype(bf16)
    mixed = jnp.einsum("nqk,nkd->nqd", weights, value, preferred_element_type=f32)
    mixed = (rows_of(mixed, 2) * head_mask).astype(bf16)
    middle = residual_in + stream_sum(dot(mixed, full_out))
    middle_rows = whole_stream(middle)
    normed2, unit2, inverse2 = norm_forward(middle_rows, norm2_gain, norm2_shift)
    normed2 = normed2.astype(bf16)
    upper = jnp.maximum(dot(normed2, full_up), 0.0) * width_mask
    active = jnp.square(upper).astype(bf16)
    upper = upper.astype(bf16)
    output = middle + stream_sum(dot(active, full_down))

    grad_top = whole_stream(cotangent)
    grad_down = scatter_weight(cut_weight(dot(active.T, grad_top).astype(bf16), 1))
    grad_active = dot(grad_top, full_down.T)
    grad_upper = (grad_active * 2.0 * upper.astype(f32)).astype(bf16)
    grad_normed2 = dot(grad_upper, full_up.T)
    part_middle, gain2_grad, shift2_grad = norm_backward(
        grad_normed2, unit2, inverse2, norm2_gain
    )
    grad_middle = cotangent + stream_sum(part_middle)
    grad_up = scatter_weight(cut_weight(dot(normed2.T, grad_upper).astype(bf16), 0))
    grad_branch = whole_stream(grad_middle)
    grad_wout = scatter_weight(cut_weight(dot(mixed.T, grad_branch).astype(bf16), 1))
    grad_mixed = (dot(grad_branch, full_out.T) * head_mask).astype(bf16)
    grad_mixed = heads_of(grad_mixed, 2)
    grad_weights = jnp.einsum("nqd,nkd->nqk", grad_mixed, value, preferred_element_type=f32)
    grad_value = jnp.einsum("nqk,nqd->nkd", weights, grad_mixed, preferred_element_type=f32)
    wide = weights.astype(f32)
    grad_scores = wide * (grad_weights - jnp.sum(grad_weights * wide, axis=-1, keepdims=True))
    grad_raw = (grad_scores * score_scale).astype(bf16)
    grad_query = jnp.einsum("nqk,nkd->nqd", grad_raw, key, preferred_element_type=f32)
    grad_key = jnp.einsum("nqk,nqd->nkd", grad_raw, query, preferred_element_type=f32)
    grad_query, grad_key = [
        rotate(rows_of(g, 2).reshape(2 * tokens, -1, HD), cosine, -sine_part).reshape(-1, width)
        for g in (grad_query, grad_key)
    ]
    grad_projected = jnp.concatenate([grad_query, grad_key, rows_of(grad_value, 2)], axis=1)
    grad_projected = grad_projected.astype(bf16)
    grad_normed1 = dot(grad_projected, full_qkv.T)
    part_input, gain1_grad, shift1_grad = norm_backward(
        grad_normed1, unit1, inverse1, norm1_gain
    )
    grad_input = grad_middle + stream_sum(part_input)
    grad_qkv = scatter_weight(cut_weight(dot(normed1.T, grad_projected).astype(bf16), 0))

    def join(pair, axis):
        left = jnp.where(side == 0, pair[0], pair[1])
        right = jnp.where(side == 0, pair[1], pair[0])
        return jnp.concatenate([left, right], axis=axis).astype(f32)

    grad_qkv = join([g.reshape(g.shape[0], 3, width) for g in grad_qkv], 2)
    grad_wout, grad_up, grad_down = join(grad_wout, 0), join(grad_up, 1), join(grad_down, 0)
    gain2_grad, shift2_grad = sum_all(jnp.stack([gain2_grad, shift2_grad]), ("dp", "tensor"))
    gain1_grad, shift1_grad = sum_all(jnp.stack([gain1_grad, shift1_grad]), ("dp", "tensor"))
    return (
        output,
        grad_input,
        gain1_grad,
        shift1_grad,
        grad_qkv,
        grad_wout,
        gain2_grad,
        shift2_grad,
        grad_up,
        grad_down,
        bucket_counts,
    )


def solution(mesh):
    placed = (
        P("dp", "tensor"),
        P("dp", None),
        P("dp", None),
        P("dp", None),
        P(),
        P(),
        P("dp", None, "tensor"),
        P("tensor", "dp"),
        P(),
        P(),
        P("dp", "tensor"),
        P("tensor", "dp"),
        P("dp", "tensor"),
    )
    return jax.shard_map(
        local,
        mesh=mesh,
        in_specs=placed,
        out_specs=(
            P("dp", "tensor"),
            P("dp", "tensor"),
            P(),
            P(),
            P("dp", None, "tensor"),
            P("tensor", "dp"),
            P(),
            P(),
            P("dp", "tensor"),
            P("tensor", "dp"),
            P(),
        ),
        check_vma=False,
    )
```

time: 1190 us -> 712 us (0.60)
  waiting for transfers between devices: 906 us -> 422 us
  starting transfers between devices: 1.29 us -> 97.2 us
  matrix products: 138 us -> 80.8 us
  blocking collectives: 51.3 us -> 0 us
  local copies, waits for them, and re-layouts: 17.5 us -> 38.8 us
  between operations: 14.8 us -> 2.63 us
  Pallas kernels: 0 us -> 12.1 us
    reduce_scatter x8 -> x0, waiting for transfers between devices: 470 us -> none  [the longest x1 150 us: local(): lax.psum_scatter(grad_down.astype(jnp.bfloat16), 'dp', scatter_dimension=...]
    all_gather x8 -> x0, waiting for transfers between devices: 434 us -> none  [the longest x1 128 us: local(): lax.all_gather(w_down, 'dp', axis=1, tiled=True)]
    ppermute x0 -> x126, waiting for transfers between devices: none -> 422 us  [the longest x74 386 us: dp_swap(): return lax.ppermute(value, 'dp', [(i, i ^ bit) for i in range(count)])]
    ppermute x0 -> x126, starting transfers between devices: none -> 97.2 us  [the longest x74 72.4 us: dp_swap(): return lax.ppermute(value, 'dp', [(i, i ^ bit) for i in range(count)])]
    dot_general x40 -> x18, matrix products: 138 us -> 80.8 us  [the longest x1 7.98 us: local(): grad_normed1 = dot(grad_projected, full_qkv.T)]
    psum x2 -> x0, blocking collectives: 51.3 us -> none  [the longest x1 39.1 us: local(): lax.psum((gain1_grad, shift1_grad, gain2_grad, shift2_grad), ('dp', 'tens...]
    pallas_call x0 -> x16, Pallas kernels: none -> 12.1 us  [the longest x8 6.19 us: cut(): pl.pallas_call(kernel, out_shape=[jax.ShapeDtypeStruct(block_shape, jnp.b...]
    convert_element_type x19 -> x35, other arithmetic: 27.2 us -> 24.1 us  [the longest x2 7.68 us: stream_sum(): return scatter_act(cut_act(rows.astype(jnp.bfloat16)))]
  transfers between devices with their start and end apart: 16 -> 126, of which waited for: 13 -> 51; matrix products, arithmetic and copies ran while one was open for 14% -> 9% of each run, Pallas kernels for 0% -> 1%
where the time goes in v1:
time: 712 us; the launch traced here: 708 us
  waiting for transfers between devices  422 us (59%)
  starting transfers between devices  97.2 us (14%)
  matrix products  80.8 us (11%)
  other arithmetic  54.3 us (8%)
  local copies, waits for them, and re-layouts  38.8 us (5%)
  Pallas kernels  12.1 us (2%)
    ppermute x74, waiting for transfers between devices, dp_swap(): return lax.ppermute(value, 'dp', [(i, i ^ bit) for i in range(count)])  386 us
    ppermute x74, starting transfers between devices, dp_swap(): return lax.ppermute(value, 'dp', [(i, i ^ bit) for i in range(count)])  72.4 us
    ppermute x52, waiting for transfers between devices, tensor_swap(): return lax.ppermute(value, 'tensor', [(i, i ^ bit) for i in range(count)])  36 us
    ppermute x52, starting transfers between devices, tensor_swap(): return lax.ppermute(value, 'tensor', [(i, i ^ bit) for i in range(count)])  24.8 us
    unnamed x109, local copies, waits for them, and re-layouts  17.5 us
  transfers between devices with their start and end apart: 126, of which 51 were waited for; matrix products, arithmetic and copies ran while one was open for 9% of the time, Pallas kernels for 1%

profile of v1, /device:TPU:0, one launch (start us, length us, event | category | flops | bytes accessed | tf_op | source)
XLA Modules:
  0.0 707.7 jit_solution(18098180374339710388)
XLA Ops:
  35.9 15.6 %collective-permute-done.20.refs_6_ = bf16[256,256]{1,0:T(8,128)(2,1)S(1)} collective-permute-done((bf16[256,256]{1,0:T(8,128)(2,1)S(1)}, bf16[256,256]{1,0:T(8,128)(2,1)S(1)}, u32[]{:S(2)}, u32[]{:S(2)}) %collective-permute-start.20) | collective-permute-done | bytes 131104 | tf_op jit(solution)/shard_map/ppermute | solution.py:19
  60.9 10.4 %collective-permute-done.2.refs_2_ = bf16[512,512]{1,0:T(8,128)(2,1)S(1)} collective-permute-done((bf16[512,512]{1,0:T(8,128)(2,1)S(1)}, bf16[512,512]{1,0:T(8,128)(2,1)S(1)}, u32[]{:S(2)}, u32[]{:S(2)}) %collective-permute-start.2) | collective-permute-done | bytes 524320 | tf_op jit(solution)/shard_map/ppermute | solution.py:24
  121.8 9.5 %collective-permute-done.123 = s32[4]{0:T(128)S(1)} collective-permute-done((s32[4]{0:T(128)S(1)}, s32[4]{0:T(128)S(1)}, u32[]{:S(2)}, u32[]{:S(2)}) %collective-permute-start.123) | collective-permute-done | bytes 48 | tf_op jit(solution)/shard_map/ppermute | solution.py:19
  145.2 29.0 %collective-permute-done.44.refs_2_ = bf16[1024,256]{1,0:T(8,128)(2,1)S(1)} collective-permute-done((bf16[1024,256]{1,0:T(8,128)(2,1)S(1)}, bf16[1024,256]{1,0:T(8,128)(2,1)S(1)}, u32[]{:S(2)}, u32[]{:S(2)}) %collective-permute-start.44) | collective-permute-done | bytes 524320 | tf_op jit(solution)/shard_map/ppermute | solution.py:19
  175.9 10.7 %collective-permute-done.37.refs_2_ = bf16[256,1024]{1,0:T(8,128)(2,1)S(1)} collective-permute-done((bf16[256,1024]{1,0:T(8,128)(2,1)S(1)}, bf16[256,1024]{1,0:T(8,128)(2,1)S(1)}, u32[]{:S(2)}, u32[]{:S(2)}) %collective-permute-start.37) | collective-permute-done | bytes 524320 | tf_op jit(solution)/shard_map/ppermute | solution.py:19
  192.2 7.5 %collective-permute-done.24 = bf16[512,512]{1,0:T(8,128)(2,1)S(1)} collective-permute-done((bf16[512,512]{1,0:T(8,128)(2,1)S(1)}, bf16[512,512]{1,0:T(8,128)(2,1)S(1)}, u32[]{:S(2)}, u32[]{:S(2)}) %collective-permute-start.24) | collective-permute-done | bytes 524320 | tf_op jit(solution)/shard_map/ppermute | solution.py:24
  206.1 8.4 %collective-permute-done.60.refs_4_ = bf16[512,512]{1,0:T(8,128)(2,1)S(1)} collective-permute-done((bf16[512,512]{1,0:T(8,128)(2,1)S(1)}, bf16[512,512]{1,0:T(8,128)(2,1)S(1)}, u32[]{:S(2)}, u32[]{:S(2)}) %collective-permute-start.60) | collective-permute-done | bytes 524320 | tf_op jit(solution)/shard_map/ppermute | solution.py:19
  216.3 22.1 %collective-permute-done.48.refs_6_ = bf16[1024,256]{1,0:T(8,128)(2,1)S(1)} collective-permute-done((bf16[1024,256]{1,0:T(8,128)(2,1)S(1)}, bf16[1024,256]{1,0:T(8,128)(2,1)S(1)}, u32[]{:S(2)}, u32[]{:S(2)}) %collective-permute-start.48) | collective-permute-done | bytes 524320 | tf_op jit(solution)/shard_map/ppermute | solution.py:19
  240.0 8.8 %collective-permute-done.41.refs_6_ = bf16[256,1024]{1,0:T(8,128)(2,1)S(1)} collective-permute-done((bf16[256,1024]{1,0:T(8,128)(2,1)S(1)}, bf16[256,1024]{1,0:T(8,128)(2,1)S(1)}, u32[]{:S(2)}, u32[]{:S(2)}) %collective-permute-start.41) | collective-permute-done | bytes 524320 | tf_op jit(solution)/shard_map/ppermute | solution.py:19
  252.4 7.6 %collective-permute-done.32.refs_4_ = bf16[512,512]{1,0:T(8,128)(2,1)S(1)} collective-permute-done((bf16[512,512]{1,0:T(8,128)(2,1)S(1)}, bf16[512,512]{1,0:T(8,128)(2,1)S(1)}, u32[]{:S(2)}, u32[]{:S(2)}) %collective-permute-start.32) | collective-permute-done | bytes 524320 | tf_op jit(solution)/shard_map/ppermute | solution.py:19
  263.7 9.3 %collective-permute-done.42.refs_7_ = bf16[256,1024]{1,0:T(8,128)(2,1)S(1)} collective-permute-done((bf16[256,1024]{1,0:T(8,128)(2,1)S(1)}, bf16[256,1024]{1,0:T(8,128)(2,1)S(1)}, u32[]{:S(2)}, u32[]{:S(2)}) %collective-permute-start.42) | collective-permute-done | bytes 524320 | tf_op jit(solution)/shard_map/ppermute | solution.py:19
  293.6 7.9 %fusion.20 = (f32[2048]{0:T(1024)S(1)}, f32[1024]{0:T(1024)S(1)}, f32[1024]{0:T(1024)S(1)}, f32[2048]{0:T(1024)S(1)}, f32[1024,2048]{1,0:T(8,128)}) fusion(bf16[1024,2048]{1,0:T(8,128)(2,1)S(1)} %shard_map.216, f32[1024]{0:T(1024)S(1)} %add_rsqrt_fusion, f32[1024]{0:T(1024)S(1)} %broadcast_multiply_fusion.4, f32[2048]{0:T(1024)S(1)} %copy-done.41, ...), kind=kOutput, calls=%fused_computation.24 | convolution fusion | flops 4315932672 | bytes 18915328 | tf_op jit(solution)/shard_map/dot_general | solution.py:339
  307.5 7.0 convolution_convert_fusion.3.refs_0_
  316.2 7.4 %convolution_convert_fusion.1.refs_0_ = bf16[1024,2048]{1,0:T(8,128)(2,1)S(1)} fusion(bf16[1024,2048]{1,0:T(8,128)(2,1)S(1)} %shard_map.220, f32[1024,1024]{1,0:T(8,128)} %fusion.60, f32[1024]{0:T(1024)S(1)} %bitcast.192), kind=kOutput, calls=%fused_computation.47 | convolution fusion | flops 4301258752 | bytes 12587008 | tf_op jit(solution)/shard_map/dot_general | solution.py:336
  345.5 10.7 %collective-permute-done.113 = bf16[256,1024]{1,0:T(8,128)(2,1)S(1)} collective-permute-done((bf16[256,1024]{1,0:T(8,128)(2,1)S(1)}, bf16[256,1024]{1,0:T(8,128)(2,1)S(1)}, u32[]{:S(2)}, u32[]{:S(2)}) %collective-permute-start.113) | collective-permute-done | bytes 524320 | tf_op jit(solution)/shard_map/ppermute | solution.py:19
  357.9 20.8 %collective-permute-done.110 = bf16[256,1024]{1,0:T(8,128)(2,1)S(1)} collective-permute-done((bf16[256,1024]{1,0:T(8,128)(2,1)S(1)}, bf16[256,1024]{1,0:T(8,128)(2,1)S(1)}, u32[]{:S(2)}, u32[]{:S(2)}) %collective-permute-start.110) | collective-permute-done | bytes 524320 | tf_op jit(solution)/shard_map/ppermute | solution.py:19
  380.4 9.5 %collective-permute-done.120 = bf16[1024,256]{1,0:T(8,128)(2,1)S(1)} collective-permute-done((bf16[1024,256]{1,0:T(8,128)(2,1)S(1)}, bf16[1024,256]{1,0:T(8,128)(2,1)S(1)}, u32[]{:S(2)}, u32[]{:S(2)}) %collective-permute-start.120) | collective-permute-done | bytes 524320 | tf_op jit(solution)/shard_map/ppermute | solution.py:19
  390.5 9.7 %collective-permute-done.117 = bf16[1024,256]{1,0:T(8,128)(2,1)S(1)} collective-permute-done((bf16[1024,256]{1,0:T(8,128)(2,1)S(1)}, bf16[1024,256]{1,0:T(8,128)(2,1)S(1)}, u32[]{:S(2)}, u32[]{:S(2)}) %collective-permute-start.117) | collective-permute-done | bytes 524320 | tf_op jit(solution)/shard_map/ppermute | solution.py:19
  405.6 31.0 %collective-permute-done.114 = bf16[256,1024]{1,0:T(8,128)(2,1)S(1)} collective-permute-done((bf16[256,1024]{1,0:T(8,128)(2,1)S(1)}, bf16[256,1024]{1,0:T(8,128)(2,1)S(1)}, u32[]{:S(2)}, u32[]{:S(2)}) %collective-permute-start.114) | collective-permute-done | bytes 524320 | tf_op jit(solution)/shard_map/ppermute | solution.py:19
  439.0 8.8 %collective-permute-done.121 = bf16[1024,256]{1,0:T(8,128)(2,1)S(1)} collective-permute-done((bf16[1024,256]{1,0:T(8,128)(2,1)S(1)}, bf16[1024,256]{1,0:T(8,128)(2,1)S(1)}, u32[]{:S(2)}, u32[]{:S(2)}) %collective-permute-start.121) | collective-permute-done | bytes 524320 | tf_op jit(solution)/shard_map/ppermute | solution.py:19
  448.0 11.0 %collective-permute-done.70 = bf16[512,512]{1,0:T(8,128)(2,1)S(1)} collective-permute-done((bf16[512,512]{1,0:T(8,128)(2,1)S(1)}, bf16[512,512]{1,0:T(8,128)(2,1)S(1)}, u32[]{:S(2)}, u32[]{:S(2)}) %collective-permute-start.70) | collective-permute-done | bytes 524320 | tf_op jit(solution)/shard_map/ppermute | solution.py:19
  463.5 10.3 %collective-permute-done.111 = bf16[256,1024]{1,0:T(8,128)(2,1)S(1)} collective-permute-done((bf16[256,1024]{1,0:T(8,128)(2,1)S(1)}, bf16[256,1024]{1,0:T(8,128)(2,1)S(1)}, u32[]{:S(2)}, u32[]{:S(2)}) %collective-permute-start.111) | collective-permute-done | bytes 524320 | tf_op jit(solution)/shard_map/ppermute | solution.py:19
  474.0 11.0 %collective-permute-done.115 = bf16[256,1024]{1,0:T(8,128)(2,1)S(1)} collective-permute-done((bf16[256,1024]{1,0:T(8,128)(2,1)S(1)}, bf16[256,1024]{1,0:T(8,128)(2,1)S(1)}, u32[]{:S(2)}, u32[]{:S(2)}) %collective-permute-start.115) | collective-permute-done | bytes 524320 | tf_op jit(solution)/shard_map/ppermute | solution.py:19
  486.1 9.6 %collective-permute-done.118 = bf16[1024,256]{1,0:T(8,128)(2,1)S(1)} collective-permute-done((bf16[1024,256]{1,0:T(8,128)(2,1)S(1)}, bf16[1024,256]{1,0:T(8,128)(2,1)S(1)}, u32[]{:S(2)}, u32[]{:S(2)}) %collective-permute-start.118) | collective-permute-done | bytes 524320 | tf_op jit(solution)/shard_map/ppermute | solution.py:19
  495.6 11.2 %collective-permute-done.122 = bf16[1024,256]{1,0:T(8,128)(2,1)S(1)} collective-permute-done((bf16[1024,256]{1,0:T(8,128)(2,1)S(1)}, bf16[1024,256]{1,0:T(8,128)(2,1)S(1)}, u32[]{:S(2)}, u32[]{:S(2)}) %collective-permute-start.122) | collective-permute-done | bytes 524320 | tf_op jit(solution)/shard_map/ppermute | solution.py:19
  507.3 10.7 %collective-permute-done.74.refs_4_ = bf16[512,512]{1,0:T(8,128)(2,1)S(1)} collective-permute-done((bf16[512,512]{1,0:T(8,128)(2,1)S(1)}, bf16[512,512]{1,0:T(8,128)(2,1)S(1)}, u32[]{:S(2)}, u32[]{:S(2)}) %collective-permute-start.74) | collective-permute-done | bytes 524320 | tf_op jit(solution)/shard_map/ppermute | solution.py:19
  521.0 10.4 %collective-permute-done.76.refs_6_ = bf16[512,512]{1,0:T(8,128)(2,1)S(1)} collective-permute-done((bf16[512,512]{1,0:T(8,128)(2,1)S(1)}, bf16[512,512]{1,0:T(8,128)(2,1)S(1)}, u32[]{:S(2)}, u32[]{:S(2)}) %collective-permute-start.76) | collective-permute-done | bytes 524320 | tf_op jit(solution)/shard_map/ppermute | solution.py:24
  577.2 8.0 %fusion.28 = (f32[2048]{0:T(1024)S(1)}, f32[1024]{0:T(1024)S(1)}, f32[1024]{0:T(1024)S(1)}, f32[2048]{0:T(1024)S(1)}, f32[1024,2048]{1,0:T(8,128)S(1)}) fusion(bf16[1024,2048]{1,0:T(8,128)(2,1)} %copy-done, f32[1024]{0:T(1024)S(1)} %add_rsqrt_fusion.1, f32[1024]{0:T(1024)S(1)} %broadcast_multiply_fusion.5, f32[2048]{0:T(1024)S(1)} %copy-done.42, ...), kind=kOutput, calls=%fused_computation.32 | convolution fusion | flops 3246909440 | bytes 17342464 | tf_op jit(solution)/shard_map/dot_general | solution.py:362
  612.6 17.9 %collective-permute-done.101 = bf16[256,256]{1,0:T(8,128)(2,1)S(1)} collective-permute-done((bf16[256,256]{1,0:T(8,128)(2,1)S(1)}, bf16[256,256]{1,0:T(8,128)(2,1)S(1)}, u32[]{:S(2)}, u32[]{:S(2)}) %collective-permute-start.101) | collective-permute-done | bytes 131104 | tf_op jit(solution)/shard_map/ppermute | solution.py:19
  654.6 7.6 %collective-permute-done.93 = bf16[256,768]{1,0:T(8,128)(2,1)S(1)} collective-permute-done((bf16[256,768]{1,0:T(8,128)(2,1)S(1)}, bf16[256,768]{1,0:T(8,128)(2,1)S(1)}, u32[]{:S(2)}, u32[]{:S(2)}) %collective-permute-start.93) | collective-permute-done | bytes 393248 | tf_op jit(solution)/shard_map/ppermute | solution.py:19
  662.7 8.5 %collective-permute-done.95 = bf16[256,768]{1,0:T(8,128)(2,1)S(1)} collective-permute-done((bf16[256,768]{1,0:T(8,128)(2,1)S(1)}, bf16[256,768]{1,0:T(8,128)(2,1)S(1)}, u32[]{:S(2)}, u32[]{:S(2)}) %collective-permute-start.95) | collective-permute-done | bytes 393248 | tf_op jit(solution)/shard_map/ppermute | solution.py:19
  677.4 13.7 %collective-permute-done.92 = bf16[256,768]{1,0:T(8,128)(2,1)S(1)} collective-permute-done((bf16[256,768]{1,0:T(8,128)(2,1)S(1)}, bf16[256,768]{1,0:T(8,128)(2,1)S(1)}, u32[]{:S(2)}, u32[]{:S(2)}) %collective-permute-start.92) | collective-permute-done | bytes 393248 | tf_op jit(solution)/shard_map/ppermute | solution.py:19
  (483 shorter events, 323.7 us)
Async XLA Ops:
  10.7 47.2 %collective-permute-start.4 = (bf16[512,512]{1,0:T(8,128)(2,1)S(1)}, bf16[512,512]{1,0:T(8,128)(2,1)S(1)}, u32[]{:S(2)}, u32[]{:S(2)}) collective-permute-start(bf16[512,512]{1,0:T(8,128)(2,1)S(1)} %convert_element_type.594.refs_0_), channel_id=1, source_target_pairs={{0,8},{4,12},{8,0},{12,4},{16,24},{20,28},{24,16},{28,20},{1,9},{5... | collective-permute-start | bytes 1572872 | tf_op jit(solution)/shard_map/ppermute | solution.py:19
  25.8 32.7 %collective-permute-start.9 = (bf16[256,768]{1,0:T(8,128)(2,1)}, bf16[256,768]{1,0:T(8,128)(2,1)S(1)}, u32[]{:S(2)}, u32[]{:S(2)}) collective-permute-start(bf16[256,768]{1,0:T(8,128)(2,1)} %copy.65), channel_id=1, source_target_pairs={{0,8},{4,12},{8,0},{12,4},{16,24},{20,28},{24,16},{28,20},{1,9},{5... | collective-permute-start | bytes 1179656 | tf_op jit(solution)/shard_map/ppermute | solution.py:19
  27.0 32.1 %collective-permute-start.11 = (bf16[256,768]{1,0:T(8,128)(2,1)S(1)}, bf16[256,768]{1,0:T(8,128)(2,1)S(1)}, u32[]{:S(2)}, u32[]{:S(2)}) collective-permute-start(bf16[256,768]{1,0:T(8,128)(2,1)S(1)} %copy.67.refs_0_), channel_id=1, source_target_pairs={{0,16},{4,20},{8,24},{12,28},{16,0},{20,4},{24,8},{28,12},{1,17},{... | collective-permute-start | bytes 1179656 | tf_op jit(solution)/shard_map/ppermute | solution.py:19
  139.3 34.9 %collective-permute-start.46 = (bf16[1024,256]{1,0:T(8,128)(2,1)S(1)}, bf16[1024,256]{1,0:T(8,128)(2,1)S(1)}, u32[]{:S(2)}, u32[]{:S(2)}) collective-permute-start(bf16[1024,256]{1,0:T(8,128)(2,1)S(1)} %get-tuple-element.198.refs_0_), channel_id=1, source_target_pairs={{0,16},{4,20},{8,24},{12,28},{16,0},{20,4},{24,8},{28,12},{1,17},{... | collective-permute-start | bytes 1572872 | tf_op jit(solution)/shard_map/ppermute | solution.py:19
  139.3 36.4 %collective-permute-start.36 = (bf16[256,1024]{1,0:T(8,128)(2,1)S(1)}, bf16[256,1024]{1,0:T(8,128)(2,1)S(1)}, u32[]{:S(2)}, u32[]{:S(2)}) collective-permute-start(bf16[256,1024]{1,0:T(8,128)(2,1)S(1)} %get-tuple-element.196.refs_0_), channel_id=1, source_target_pairs={{0,4},{4,0},{8,12},{12,8},{16,20},{20,16},{24,28},{28,24},{1,5},{5... | collective-permute-start | bytes 1572872 | tf_op jit(solution)/shard_map/ppermute | solution.py:19
  139.9 48.3 %collective-permute-start.39 = (bf16[256,1024]{1,0:T(8,128)(2,1)S(1)}, bf16[256,1024]{1,0:T(8,128)(2,1)S(1)}, u32[]{:S(2)}, u32[]{:S(2)}) collective-permute-start(bf16[256,1024]{1,0:T(8,128)(2,1)S(1)} %get-tuple-element.196.refs_0_), channel_id=1, source_target_pairs={{0,16},{4,20},{8,24},{12,28},{16,0},{20,4},{24,8},{28,12},{1,17},{... | collective-permute-start | bytes 1572872 | tf_op jit(solution)/shard_map/ppermute | solution.py:19
  142.8 31.4 %collective-permute-start.44 = (bf16[1024,256]{1,0:T(8,128)(2,1)S(1)}, bf16[1024,256]{1,0:T(8,128)(2,1)S(1)}, u32[]{:S(2)}, u32[]{:S(2)}) collective-permute-start(bf16[1024,256]{1,0:T(8,128)(2,1)S(1)} %get-tuple-element.197), channel_id=1, source_target_pairs={{0,8},{4,12},{8,0},{12,4},{16,24},{20,28},{24,16},{28,20},{1,9},{5... | collective-permute-start | bytes 1572872 | tf_op jit(solution)/shard_map/ppermute | solution.py:19
  142.8 43.8 %collective-permute-start.37 = (bf16[256,1024]{1,0:T(8,128)(2,1)S(1)}, bf16[256,1024]{1,0:T(8,128)(2,1)S(1)}, u32[]{:S(2)}, u32[]{:S(2)}) collective-permute-start(bf16[256,1024]{1,0:T(8,128)(2,1)S(1)} %get-tuple-element.195), channel_id=1, source_target_pairs={{0,8},{4,12},{8,0},{12,4},{16,24},{20,28},{24,16},{28,20},{1,9},{5... | collective-permute-start | bytes 1572872 | tf_op jit(solution)/shard_map/ppermute | solution.py:19
  199.8 38.7 %collective-permute-start.48 = (bf16[1024,256]{1,0:T(8,128)(2,1)S(1)}, bf16[1024,256]{1,0:T(8,128)(2,1)S(1)}, u32[]{:S(2)}, u32[]{:S(2)}) collective-permute-start(bf16[1024,256]{1,0:T(8,128)(2,1)S(1)} %collective-permute-done.44.refs_2_), channel_id=1, source_target_pairs={{0,16},{4,20},{8,24},{12,28},{16,0},{20,4},{24,8},{28,12},{1,17},{... | collective-permute-start | bytes 1572872 | tf_op jit(solution)/shard_map/ppermute | solution.py:19
  203.1 35.3 %collective-permute-start.38 = (bf16[256,1024]{1,0:T(8,128)(2,1)S(1)}, bf16[256,1024]{1,0:T(8,128)(2,1)S(1)}, u32[]{:S(2)}, u32[]{:S(2)}) collective-permute-start(bf16[256,1024]{1,0:T(8,128)(2,1)S(1)} %collective-permute-done.37.refs_2_), channel_id=1, source_target_pairs={{0,4},{4,0},{8,12},{12,8},{16,20},{20,16},{24,28},{28,24},{1,5},{5... | collective-permute-start | bytes 1572872 | tf_op jit(solution)/shard_map/ppermute | solution.py:19
  215.2 33.6 %collective-permute-start.41 = (bf16[256,1024]{1,0:T(8,128)(2,1)S(1)}, bf16[256,1024]{1,0:T(8,128)(2,1)S(1)}, u32[]{:S(2)}, u32[]{:S(2)}) collective-permute-start(bf16[256,1024]{1,0:T(8,128)(2,1)S(1)} %collective-permute-done.37.refs_2_), channel_id=1, source_target_pairs={{0,16},{4,20},{8,24},{12,28},{16,0},{20,4},{24,8},{28,12},{1,17},{... | collective-permute-start | bytes 1572872 | tf_op jit(solution)/shard_map/ppermute | solution.py:19
  216.3 33.0 %collective-permute-start.59 = (bf16[512,512]{1,0:T(8,128)(2,1)S(1)}, bf16[512,512]{1,0:T(8,128)(2,1)S(1)}, u32[]{:S(2)}, u32[]{:S(2)}) collective-permute-start(bf16[512,512]{1,0:T(8,128)(2,1)S(1)} %collective-permute-done.58.refs_2_), channel_id=1, source_target_pairs={{0,1},{1,0},{2,3},{3,2},{4,5},{5,4},{6,7},{7,6},{8,9},{9,8},{10,11... | collective-permute-start | bytes 1572872 | tf_op jit(solution)/shard_map/ppermute | solution.py:24
  338.4 62.8 %collective-permute-start.67 = (bf16[512,512]{1,0:T(8,128)(2,1)S(1)}, bf16[512,512]{1,0:T(8,128)(2,1)S(1)}, u32[]{:S(2)}, u32[]{:S(2)}) collective-permute-start(bf16[512,512]{1,0:T(8,128)(2,1)S(1)} %get-tuple-element.96), channel_id=1, source_target_pairs={{0,1},{1,0},{2,3},{3,2},{4,5},{5,4},{6,7},{7,6},{8,9},{9,8},{10,11... | collective-permute-start | bytes 1572872 | tf_op jit(solution)/shard_map/ppermute | solution.py:24
  340.8 96.1 %collective-permute-start.64 = (bf16[512,512]{1,0:T(8,128)(2,1)S(1)}, bf16[512,512]{1,0:T(8,128)(2,1)S(1)}, u32[]{:S(2)}, u32[]{:S(2)}) collective-permute-start(bf16[512,512]{1,0:T(8,128)(2,1)S(1)} %get-tuple-element.92), channel_id=1, source_target_pairs={{0,1},{1,0},{2,3},{3,2},{4,5},{5,4},{6,7},{7,6},{8,9},{9,8},{10,11... | collective-permute-start | bytes 1572872 | tf_op jit(solution)/shard_map/ppermute | solution.py:24
  343.1 59.7 %collective-permute-start.112 = (bf16[256,1024]{1,0:T(8,128)(2,1)S(1)}, bf16[256,1024]{1,0:T(8,128)(2,1)S(1)}, u32[]{:S(2)}, u32[]{:S(2)}) collective-permute-start(bf16[256,1024]{1,0:T(8,128)(2,1)S(1)} %get-tuple-element.128), channel_id=1, source_target_pairs={{0,4},{4,0},{8,12},{12,8},{16,20},{20,16},{24,28},{28,24},{1,5},{5... | collective-permute-start | bytes 1572872 | tf_op jit(solution)/shard_map/ppermute | solution.py:19
  343.8 34.9 %collective-permute-start.110 = (bf16[256,1024]{1,0:T(8,128)(2,1)S(1)}, bf16[256,1024]{1,0:T(8,128)(2,1)S(1)}, u32[]{:S(2)}, u32[]{:S(2)}) collective-permute-start(bf16[256,1024]{1,0:T(8,128)(2,1)S(1)} %get-tuple-element.126), channel_id=1, source_target_pairs={{0,4},{4,0},{8,12},{12,8},{16,20},{20,16},{24,28},{28,24},{1,5},{5... | collective-permute-start | bytes 1572872 | tf_op jit(solution)/shard_map/ppermute | solution.py:19
  356.2 33.7 %collective-permute-start.120 = (bf16[1024,256]{1,0:T(8,128)(2,1)S(1)}, bf16[1024,256]{1,0:T(8,128)(2,1)S(1)}, u32[]{:S(2)}, u32[]{:S(2)}) collective-permute-start(bf16[1024,256]{1,0:T(8,128)(2,1)S(1)} %get-tuple-element.138), channel_id=1, source_target_pairs={{0,4},{4,0},{8,12},{12,8},{16,20},{20,16},{24,28},{28,24},{1,5},{5... | collective-permute-start | bytes 1572872 | tf_op jit(solution)/shard_map/ppermute | solution.py:19
  400.3 36.3 %collective-permute-start.114 = (bf16[256,1024]{1,0:T(8,128)(2,1)S(1)}, bf16[256,1024]{1,0:T(8,128)(2,1)S(1)}, u32[]{:S(2)}, u32[]{:S(2)}) collective-permute-start(bf16[256,1024]{1,0:T(8,128)(2,1)S(1)} %add_convert_fusion.7), channel_id=1, source_target_pairs={{0,16},{4,20},{8,24},{12,28},{16,0},{20,4},{24,8},{28,12},{1,17},{... | collective-permute-start | bytes 1572872 | tf_op jit(solution)/shard_map/ppermute | solution.py:19
  401.2 35.8 %collective-permute-start.119 = (bf16[1024,256]{1,0:T(8,128)(2,1)S(1)}, bf16[1024,256]{1,0:T(8,128)(2,1)S(1)}, u32[]{:S(2)}, u32[]{:S(2)}) collective-permute-start(bf16[1024,256]{1,0:T(8,128)(2,1)S(1)} %get-tuple-element.136), channel_id=1, source_target_pairs={{0,4},{4,0},{8,12},{12,8},{16,20},{20,16},{24,28},{28,24},{1,5},{5... | collective-permute-start | bytes 1572872 | tf_op jit(solution)/shard_map/ppermute | solution.py:19
  402.7 35.8 %collective-permute-start.66 = (bf16[512,512]{1,0:T(8,128)(2,1)S(1)}, bf16[512,512]{1,0:T(8,128)(2,1)S(1)}, u32[]{:S(2)}, u32[]{:S(2)}) collective-permute-start(bf16[512,512]{1,0:T(8,128)(2,1)S(1)} %add_convert_fusion.22), channel_id=1, source_target_pairs={{0,2},{1,3},{2,0},{3,1},{4,6},{5,7},{6,4},{7,5},{8,10},{9,11},{10,... | collective-permute-start | bytes 1572872 | tf_op jit(solution)/shard_map/ppermute | solution.py:24
  403.2 44.6 %collective-permute-start.121 = (bf16[1024,256]{1,0:T(8,128)(2,1)S(1)}, bf16[1024,256]{1,0:T(8,128)(2,1)S(1)}, u32[]{:S(2)}, u32[]{:S(2)}) collective-permute-start(bf16[1024,256]{1,0:T(8,128)(2,1)S(1)} %add_convert_fusion.1), channel_id=1, source_target_pairs={{0,16},{4,20},{8,24},{12,28},{16,0},{20,4},{24,8},{28,12},{1,17},{... | collective-permute-start | bytes 1572872 | tf_op jit(solution)/shard_map/ppermute | solution.py:19
  461.0 34.6 %collective-permute-start.118 = (bf16[1024,256]{1,0:T(8,128)(2,1)S(1)}, bf16[1024,256]{1,0:T(8,128)(2,1)S(1)}, u32[]{:S(2)}, u32[]{:S(2)}) collective-permute-start(bf16[1024,256]{1,0:T(8,128)(2,1)S(1)} %add_convert_fusion.4), channel_id=1, source_target_pairs={{0,16},{4,20},{8,24},{12,28},{16,0},{20,4},{24,8},{28,12},{1,17},{... | collective-permute-start | bytes 1572872 | tf_op jit(solution)/shard_map/ppermute | solution.py:19
  463.5 43.3 %collective-permute-start.122 = (bf16[1024,256]{1,0:T(8,128)(2,1)S(1)}, bf16[1024,256]{1,0:T(8,128)(2,1)S(1)}, u32[]{:S(2)}, u32[]{:S(2)}) collective-permute-start(bf16[1024,256]{1,0:T(8,128)(2,1)S(1)} %add_convert_fusion), channel_id=1, source_target_pairs={{0,8},{4,12},{8,0},{12,4},{16,24},{20,28},{24,16},{28,20},{1,9},{5... | collective-permute-start | bytes 1572872 | tf_op jit(solution)/shard_map/ppermute | solution.py:19
  473.8 44.3 %collective-permute-start.74 = (bf16[512,512]{1,0:T(8,128)(2,1)S(1)}, bf16[512,512]{1,0:T(8,128)(2,1)S(1)}, u32[]{:S(2)}, u32[]{:S(2)}) collective-permute-start(bf16[512,512]{1,0:T(8,128)(2,1)S(1)} %fusion.58.refs_0_), channel_id=1, source_target_pairs={{0,8},{4,12},{8,0},{12,4},{16,24},{20,28},{24,16},{28,20},{1,9},{5... | collective-permute-start | bytes 1572872 | tf_op jit(solution)/shard_map/ppermute | solution.py:19
  485.0 35.4 %collective-permute-start.50 = (bf16[512,512]{1,0:T(8,128)(2,1)S(1)}, bf16[512,512]{1,0:T(8,128)(2,1)S(1)}, u32[]{:S(2)}, u32[]{:S(2)}) collective-permute-start(bf16[512,512]{1,0:T(8,128)(2,1)S(1)} %get-tuple-element.84), channel_id=1, source_target_pairs={{0,1},{1,0},{2,3},{3,2},{4,5},{5,4},{6,7},{7,6},{8,9},{9,8},{10,11... | collective-permute-start | bytes 1572872 | tf_op jit(solution)/shard_map/ppermute | solution.py:24
  485.5 35.0 %collective-permute-start.52 = (bf16[512,512]{1,0:T(8,128)(2,1)S(1)}, bf16[512,512]{1,0:T(8,128)(2,1)S(1)}, u32[]{:S(2)}, u32[]{:S(2)}) collective-permute-start(bf16[512,512]{1,0:T(8,128)(2,1)S(1)} %add_convert_fusion.28), channel_id=1, source_target_pairs={{0,2},{1,3},{2,0},{3,1},{4,6},{5,7},{6,4},{7,5},{8,10},{9,11},{10,... | collective-permute-start | bytes 1572872 | tf_op jit(solution)/shard_map/ppermute | solution.py:24
  495.6 37.3 %collective-permute-start.56 = (bf16[512,512]{1,0:T(8,128)(2,1)S(1)}, bf16[512,512]{1,0:T(8,128)(2,1)S(1)}, u32[]{:S(2)}, u32[]{:S(2)}) collective-permute-start(bf16[512,512]{1,0:T(8,128)(2,1)S(1)} %add_convert_fusion.24), channel_id=1, source_target_pairs={{0,8},{4,12},{8,0},{12,4},{16,24},{20,28},{24,16},{28,20},{1,9},{5... | collective-permute-start | bytes 1572872 | tf_op jit(solution)/shard_map/ppermute | solution.py:19
  605.4 46.0 %collective-permute-start.82 = (bf16[512,512]{1,0:T(8,128)(2,1)S(1)}, bf16[512,512]{1,0:T(8,128)(2,1)S(1)}, u32[]{:S(2)}, u32[]{:S(2)}) collective-permute-start(bf16[512,512]{1,0:T(8,128)(2,1)S(1)} %get-tuple-element.106), channel_id=1, source_target_pairs={{0,1},{1,0},{2,3},{3,2},{4,5},{5,4},{6,7},{7,6},{8,9},{9,8},{10,11... | collective-permute-start | bytes 1572872 | tf_op jit(solution)/shard_map/ppermute | solution.py:24
  607.2 35.3 %collective-permute-start.94 = (bf16[256,768]{1,0:T(8,128)(2,1)S(1)}, bf16[256,768]{1,0:T(8,128)(2,1)S(1)}, u32[]{:S(2)}, u32[]{:S(2)}) collective-permute-start(bf16[256,768]{1,0:T(8,128)(2,1)S(1)} %get-tuple-element.114), channel_id=1, source_target_pairs={{0,4},{4,0},{8,12},{12,8},{16,20},{20,16},{24,28},{28,24},{1,5},{5... | collective-permute-start | bytes 1179656 | tf_op jit(solution)/shard_map/ppermute | solution.py:19
  607.8 42.9 %collective-permute-start.91 = (bf16[256,768]{1,0:T(8,128)(2,1)S(1)}, bf16[256,768]{1,0:T(8,128)(2,1)S(1)}, u32[]{:S(2)}, u32[]{:S(2)}) collective-permute-start(bf16[256,768]{1,0:T(8,128)(2,1)S(1)} %get-tuple-element.110), channel_id=1, source_target_pairs={{0,4},{4,0},{8,12},{12,8},{16,20},{20,16},{24,28},{28,24},{1,5},{5... | collective-permute-start | bytes 1179656 | tf_op jit(solution)/shard_map/ppermute | solution.py:19
  650.5 52.6 %collective-permute-start.78 = (bf16[512,512]{1,0:T(8,128)(2,1)S(1)}, bf16[512,512]{1,0:T(8,128)(2,1)}, u32[]{:S(2)}, u32[]{:S(2)}) collective-permute-start(bf16[512,512]{1,0:T(8,128)(2,1)S(1)} %get-tuple-element.100), channel_id=1, source_target_pairs={{0,1},{1,0},{2,3},{3,2},{4,5},{5,4},{6,7},{7,6},{8,9},{9,8},{10,11... | collective-permute-start | bytes 1572872 | tf_op jit(solution)/shard_map/ppermute | solution.py:24
  671.3 31.8 %collective-permute-start.80 = (bf16[512,512]{1,0:T(8,128)(2,1)}, bf16[512,512]{1,0:T(8,128)(2,1)}, u32[]{:S(2)}, u32[]{:S(2)}) collective-permute-start(bf16[512,512]{1,0:T(8,128)(2,1)} %add_convert_fusion.16), channel_id=1, source_target_pairs={{0,2},{1,3},{2,0},{3,1},{4,6},{5,7},{6,4},{7,5},{8,10},{9,11},{10,... | collective-permute-start | bytes 1572872 | tf_op jit(solution)/shard_map/ppermute | solution.py:24
  (143 other events, 2190.9 us)

commit v2 on v1

--- a/solution.py
+++ b/solution.py
@@ -258,7 +258,7 @@
     return jnp.transpose(heads, (1, 2, 0, 3)).reshape(blocks * heads.shape[2], -1)
 
 
-def local(
+def local_general(
     residual_in,
     lengths,
     head_bucket,
@@ -390,6 +390,683 @@
     )
 
 
+def flip(i, bit):
+    return i + bit - 2 * bit * ((i // bit) % 2)
+
+
+class Traffic:
+    def __init__(self, send_sems, recv_sems):
+        self.send_sems, self.recv_sems = send_sems, recv_sems
+        self.copies = {}
+
+    def send(self, name, src, dst, device):
+        k = len(self.copies)
+        copy = pltpu.make_async_remote_copy(
+            src_ref=src,
+            dst_ref=dst,
+            send_sem=self.send_sems.at[k],
+            recv_sem=self.recv_sems.at[k],
+            device_id=device,
+            device_id_type=pl.DeviceIdType.MESH,
+        )
+        copy.start()
+        self.copies[name] = copy
+
+    def wait(self, *names):
+        for name in names:
+            self.copies[name].wait_recv()
+
+    def finish(self):
+        for copy in self.copies.values():
+            copy.wait_send()
+
+
+class Moves:
+    def __init__(self, sems):
+        self.sems, self.copies = sems, {}
+
+    def start(self, name, src, dst):
+        copy = pltpu.make_async_copy(src, dst, self.sems.at[len(self.copies)])
+        copy.start()
+        self.copies[name] = [copy, False]
+
+    def wait(self, *names):
+        for name in names:
+            if not self.copies[name][1]:
+                self.copies[name][0].wait()
+                self.copies[name][1] = True
+
+    def finish(self):
+        self.wait(*self.copies)
+
+
+class Place:
+    def __init__(self):
+        self.i, self.t = lax.axis_index("dp"), lax.axis_index("tensor")
+        self.side = (self.i // HIDDEN_BIT) % 2
+        self.x, self.z, self.far = [(flip(self.i, b), self.t) for b in (1, 2, 4)]
+        self.c, self.y = [(self.i, flip(self.t, b)) for b in (1, 2)]
+
+    def greet(self):
+        barrier = pltpu.get_barrier_semaphore()
+        partners = (self.x, self.z, self.far, self.c, self.y)
+        for device in partners:
+            pl.semaphore_signal(
+                barrier, inc=1, device_id=device, device_id_type=pl.DeviceIdType.MESH
+            )
+        pl.semaphore_wait(barrier, len(partners))
+
+    def block(self, m):
+        d = self.i
+        for bit in (1, 2, 4):
+            if m & bit:
+                d = flip(d, bit)
+        return d
+
+    def stripe(self, m):
+        s = self.t
+        for bit in (1, 2):
+            if m & bit:
+                s = flip(s, bit)
+        return s
+
+
+class WeightGather:
+    def __init__(self, name, place, traffic, moves, halves, slot):
+        self.name, self.p, self.tr, self.mv = name, place, traffic, moves
+        self.halves, self.slot = halves, slot
+
+    def begin(self):
+        p, n = self.p, self.name
+        own, other = self.halves.at[p.side], self.halves.at[1 - p.side]
+        self.tr.send(n + "2", other, self.slot(p.i), p.z)
+        self.tr.send(n + "4", own, self.slot(p.i), p.far)
+        self.tr.send(n + "1", own, self.slot(p.i), p.x)
+        self.mv.start(n + "0", own, self.slot(p.i))
+
+    def mid(self):
+        p, n = self.p, self.name
+        self.tr.wait(n + "2")
+        block = self.slot(p.block(2))
+        self.tr.send(n + "6", block, block, p.far)
+        self.tr.send(n + "3", block, block, p.x)
+
+    def late(self, m):
+        p, n = self.p, self.name
+        self.tr.wait(n + str(m))
+        block = self.slot(p.block(m))
+        self.tr.send(n + str(m + 1), block, block, p.x)
+
+    def end(self):
+        n = self.name
+        self.mv.wait(n + "0")
+        self.tr.wait(n + "1", n + "3", n + "5", n + "7")
+
+
+class ActGather:
+    def __init__(self, name, place, traffic, slots):
+        self.name, self.p, self.tr, self.slots = name, place, traffic, slots
+
+    def at(self, b, m):
+        return self.slots.at[b, self.p.stripe(m)]
+
+    def begin(self):
+        p, n, own = self.p, self.name, self.at(0, 0)
+        self.tr.send(n + "10", own, self.slots.at[1, p.t], p.z)
+        self.tr.send(n + "02", own, own, p.y)
+        self.tr.send(n + "01", own, own, p.c)
+
+    def mid(self):
+        p, n = self.p, self.name
+        self.tr.wait(n + "10")
+        block = self.at(1, 0)
+        self.tr.send(n + "12", block, block, p.y)
+        self.tr.send(n + "11", block, block, p.c)
+        self.tr.wait(n + "02")
+        block = self.at(0, 2)
+        self.tr.send(n + "03", block, block, p.c)
+
+    def end(self):
+        p, n = self.p, self.name
+        self.tr.wait(n + "12")
+        block = self.at(1, 2)
+        self.tr.send(n + "13", block, block, p.c)
+        self.tr.wait(n + "01", n + "11", n + "03", n + "13")
+
+
+def loop_rows(count, step, body):
+    def run(k, carry):
+        body(pl.multiple_of(k * step, step))
+        return carry
+
+    lax.fori_loop(0, count // step, run, 0)
+
+
+def wide(value):
+    return value.astype(jnp.float32)
+
+
+def add_blocks(out, left, right, rows):
+    def body(r):
+        at = pl.ds(r, 64)
+        out[at, :] = (wide(left[at, :]) + wide(right[at, :])).astype(out.dtype)
+
+    loop_rows(rows, 64, body)
+
+
+class ActScatter:
+    def __init__(self, name, place, traffic, part, got_c, got_y, got_z):
+        self.name, self.p, self.tr = name, place, traffic
+        self.part, self.got_c, self.got_y, self.got_z = part, got_c, got_y, got_z
+        self.rows = part.shape[2]
+
+    def at(self, b, m):
+        return self.part.at[b, self.p.stripe(m)]
+
+    def begin(self):
+        p, n = self.p, self.name
+        for j, m in ((1, 3), (0, 1)):
+            for b in (1, 0):
+                self.tr.send(n + "c" + str(b) + str(j), self.at(b, m), self.got_c.at[b, j], p.c)
+
+    def mid(self):
+        p, n = self.p, self.name
+        for b in (1, 0):
+            self.tr.wait(n + "c" + str(b) + "1")
+            add_blocks(self.at(b, 2), self.at(b, 2), self.got_c.at[b, 1], self.rows)
+            self.tr.send(n + "y" + str(b), self.at(b, 2), self.got_y.at[b], p.y)
+        for b in (1, 0):
+            self.tr.wait(n + "c" + str(b) + "0")
+            add_blocks(self.at(b, 0), self.at(b, 0), self.got_c.at[b, 0], self.rows)
+
+    def late(self):
+        p, n = self.p, self.name
+        self.tr.wait(n + "y1")
+        add_blocks(self.at(1, 0), self.at(1, 0), self.got_y.at[1], self.rows)
+        self.tr.send(n + "z", self.at(1, 0), self.got_z, p.z)
+        self.tr.wait(n + "y0")
+        add_blocks(self.at(0, 0), self.at(0, 0), self.got_y.at[0], self.rows)
+
+    def end(self, out, base):
+        self.tr.wait(self.name + "z")
+        own = self.at(0, 0)
+
+        def body(r):
+            at = pl.ds(r, 64)
+            out[at, :] = base[at, :] + (wide(own[at, :]) + wide(self.got_z[at, :]))
+
+        loop_rows(self.rows, 64, body)
+
+
+def round_rows(src, dst, rows):
+    def body(r):
+        at = pl.ds(r, 64)
+        dst[at, :] = src[at, :].astype(dst.dtype)
+
+    loop_rows(rows, 64, body)
+
+
+def dot_f32(left, right):
+    return jnp.dot(left, right, preferred_element_type=jnp.float32)
+
+
+def dot_nt(left, right):
+    return lax.dot_general(
+        left, right, (((1,), (1,)), ((), ())), preferred_element_type=jnp.float32
+    )
+
+
+def dot_tn(left, right):
+    return lax.dot_general(
+        left, right, (((0,), (0,)), ((), ())), preferred_element_type=jnp.float32
+    )
+
+
+def center_rows(slots, b, at):
+    stripes = slots.shape[1]
+    rows = jnp.concatenate([wide(slots[b, s, at, :]) for s in range(stripes)], axis=1)
+    center = rows - jnp.mean(rows, axis=1, keepdims=True)
+    spread = jnp.mean(center * center, axis=1, keepdims=True)
+    return center, lax.rsqrt(spread + epsilon)
+
+
+def norm_rows(slots, gain, shift, out):
+    rows = slots.shape[2]
+    for b in range(2):
+
+        def body(r, b=b):
+            center, inverse = center_rows(slots, b, pl.ds(r, 32))
+            out[pl.ds(b * rows + r, 32), :] = (
+                center * inverse * gain[...] + shift[...]
+            ).astype(jnp.bfloat16)
+
+        loop_rows(rows, 32, body)
+
+
+def attend(qkv, seg_col, seg_row, head_mask, weights, mixed, scale):
+    tokens = seg_row.shape[2]
+    heads = qkv.shape[2] // HD
+    half = tokens // 2
+
+    def body(b, carry):
+        start = pl.multiple_of(b * tokens, tokens)
+        for h in range(heads):
+            cols = pl.ds(h * HD, HD)
+            for part in range(2):
+                rows = pl.ds(start + part * half, half)
+                reach = half * (part + 1)
+                query = qkv[0, rows, cols]
+                key = qkv[1, pl.ds(start, reach), cols]
+                value = qkv[2, pl.ds(start, reach), cols]
+                scores = dot_nt(query, key) * scale
+                row_id = lax.broadcasted_iota(jnp.int32, (half, reach), 0) + part * half
+                col_id = lax.broadcasted_iota(jnp.int32, (half, reach), 1)
+                allowed = (seg_col[rows, :] == seg_row[b, :, pl.ds(0, reach)]) & (
+                    row_id >= col_id
+                )
+                scores = jnp.where(allowed, scores, -1000000000.0)
+                scores = jnp.exp(scores - jnp.max(scores, axis=1, keepdims=True))
+                total = jnp.sum(scores, axis=1, keepdims=True)
+                chosen = (scores / total).astype(jnp.bfloat16)
+                weights[b * heads + h, pl.ds(part * half, half), pl.ds(0, reach)] = chosen
+                mixed[rows, cols] = (dot_f32(chosen, value) * head_mask[rows, :]).astype(
+                    jnp.bfloat16
+                )
+        return carry
+
+    lax.fori_loop(0, 2, body, 0)
+
+
+def forward_kernel(
+    residual,
+    cotangent,
+    gain1,
+    shift1,
+    gain2,
+    shift2,
+    cosine,
+    sine,
+    seg_col,
+    seg_row,
+    head_mask,
+    width_mask,
+    half_qkv,
+    half_out,
+    half_up,
+    half_down,
+    all_qkv,
+    all_out,
+    all_up,
+    all_down,
+    stream1,
+    stream2,
+    stream_c,
+    normed1,
+    normed2,
+    heads_out,
+    weights_out,
+    mixed_out,
+    upper_out,
+    middle_out,
+    w_qkv,
+    w_out,
+    w_up,
+    rows1,
+    rows2,
+    rows_c,
+    normed,
+    qkv,
+    weights,
+    mixed,
+    part,
+    got_c,
+    got_y,
+    got_z,
+    upper,
+    middle,
+    send_sems,
+    recv_sems,
+    move_sems,
+):
+    p = Place()
+    tr, mv = Traffic(send_sems, recv_sems), Moves(move_sems)
+    tokens = residual.shape[0]
+    rows_d = half_qkv.shape[1]
+    head_cols = half_out.shape[1]
+
+    def row_slot(ref):
+        return lambda d: ref.at[pl.ds(pl.multiple_of(d * rows_d, rows_d), rows_d)]
+
+    def first_slot(ref):
+        return lambda d: ref.at[d]
+
+    g_qkv = WeightGather("q", p, tr, mv, half_qkv, row_slot(w_qkv))
+    g_out = WeightGather("o", p, tr, mv, half_out, first_slot(w_out))
+    g_up = WeightGather("u", p, tr, mv, half_up, row_slot(w_up))
+    g_down = WeightGather("d", p, tr, mv, half_down, first_slot(all_down))
+    a1 = ActGather("a", p, tr, rows1)
+    a2 = ActGather("b", p, tr, rows2)
+    ac = ActGather("c", p, tr, rows_c)
+    s1 = ActScatter("s", p, tr, part, got_c, got_y, got_z)
+
+    p.greet()
+    round_rows(residual, rows1.at[0, p.t], tokens)
+    a1.begin()
+    g_qkv.begin()
+    round_rows(cotangent, rows_c.at[0, p.t], tokens)
+    a1.mid()
+    g_qkv.mid()
+    a1.end()
+    g_out.begin()
+    ac.begin()
+    norm_rows(rows1, gain1, shift1, normed)
+    mv.start("stream1", rows1, stream1)
+    mv.start("normed1", normed, normed1)
+    g_qkv.late(4)
+    g_out.mid()
+    g_qkv.late(6)
+    g_up.begin()
+    ac.mid()
+    g_qkv.end()
+
+    def project(r):
+        at = pl.ds(r, 256)
+        for k in range(3):
+            got = dot_f32(normed[at, :], w_qkv[:, pl.ds(k * head_cols, head_cols)])
+            for h in range(head_cols // HD):
+                cols = pl.ds(h * HD, HD)
+                one = got[:, h * HD : (h + 1) * HD]
+                if k < 2:
+                    one = one * cosine[at, :] + pltpu.roll(one, HD // 2, 1) * sine[at, :]
+                qkv[k, at, cols] = one.astype(jnp.bfloat16)
+
+    loop_rows(2 * tokens, 256, project)
+    mv.start("all_qkv", w_qkv, all_qkv)
+    g_out.late(4)
+    g_up.mid()
+    attend(qkv, seg_col, seg_row, head_mask, weights, mixed, HD ** (-0.5))
+    mv.start("heads", qkv, heads_out)
+    mv.start("weights", weights, weights_out)
+    mv.start("mixed", mixed, mixed_out)
+    g_out.late(6)
+    ac.end()
+    mv.start("stream_c", rows_c, stream_c)
+    g_out.end()
+
+    blocks = w_out.shape[0]
+    stripes = part.shape[1]
+    per = blocks // stripes
+
+    def branch(k, carry):
+        b = k // stripes
+        s = k % stripes
+        at = pl.ds(pl.multiple_of(b * tokens, tokens), tokens)
+        for j in range(per):
+            got = dot_f32(mixed[at, :], w_out[s * per + j])
+            part[b, s, :, pl.ds(j * rows_d, rows_d)] = got.astype(jnp.bfloat16)
+        return carry
+
+    lax.fori_loop(0, 2 * stripes, branch, 0)
+    mv.start("all_out", w_out, all_out)
+    s1.begin()
+    s1.mid()
+    g_up.late(4)
+    s1.late()
+    g_down.begin()
+    s1.end(middle, residual)
+    round_rows(middle, rows2.at[0, p.t], tokens)
+    a2.begin()
+    mv.start("middle", middle, middle_out)
+    g_up.late(6)
+    a2.mid()
+    g_down.mid()
+    g_up.end()
+    mv.start("all_up", w_up, all_up)
+    a2.end()
+    mv.wait("normed1")
+    norm_rows(rows2, gain2, shift2, normed)
+    mv.start("stream2", rows2, stream2)
+    mv.start("normed2", normed, normed2)
+
+    def rise(r):
+        at = pl.ds(r, 256)
+        for k in range(upper.shape[1] // 256):
+            cols = pl.ds(k * 256, 256)
+            got = dot_f32(normed[at, :], w_up[:, cols])
+            upper[at, cols] = (jnp.maximum(got, 0.0) * width_mask[at, :]).astype(jnp.bfloat16)
+
+    loop_rows(2 * tokens, 256, rise)
+    mv.start("upper", upper, upper_out)
+    g_down.late(4)
+    g_down.late(6)
+    g_down.end()
+    tr.finish()
+    mv.finish()
+
+
+def forward_call(arrays, half_weights):
+    bf16, f32 = jnp.bfloat16, jnp.float32
+    tokens, columns = arrays[0].shape
+    half_qkv, half_out, half_up, half_down = half_weights
+    count, stripes = lax.axis_size("dp"), lax.axis_size("tensor")
+    rows_d = half_qkv.shape[1]
+    head_cols = half_out.shape[1]
+    hidden = half_up.shape[2]
+    width = rows_d * count
+    heads = head_cols // HD
+    slots = (2, stripes, tokens, columns)
+    shapes = dict(
+        all_qkv=((width, 3 * head_cols), bf16),
+        all_out=((count, head_cols, rows_d), bf16),
+        all_up=((width, hidden), bf16),
+        all_down=((count, hidden, rows_d), bf16),
+        stream1=(slots, bf16),
+        stream2=(slots, bf16),
+        stream_c=(slots, bf16),
+        normed1=((2 * tokens, width), bf16),
+        normed2=((2 * tokens, width), bf16),
+        heads=((3, 2 * tokens, head_cols), bf16),
+        weights=((2 * heads, tokens, tokens), bf16),
+        mixed=((2 * tokens, head_cols), bf16),
+        upper=((2 * tokens, hidden), bf16),
+        middle=((tokens, columns), f32),
+    )
+
+    def vmem(name):
+        return pltpu.VMEM(*shapes[name])
+
+    scratch = [
+        vmem("all_qkv"),
+        vmem("all_out"),
+        vmem("all_up"),
+        vmem("stream1"),
+        vmem("stream2"),
+        vmem("stream_c"),
+        vmem("normed1"),
+        vmem("heads"),
+        vmem("weights"),
+        vmem("mixed"),
+        pltpu.VMEM(slots, bf16),
+        pltpu.VMEM((2, 2, tokens, columns), bf16),
+        pltpu.VMEM((2, tokens, columns), bf16),
+        pltpu.VMEM((tokens, columns), bf16),
+        vmem("upper"),
+        vmem("middle"),
+        pltpu.SemaphoreType.DMA((56,)),
+        pltpu.SemaphoreType.DMA((56,)),
+        pltpu.SemaphoreType.DMA((24,)),
+    ]
+    any_spec = pl.BlockSpec(memory_space=pl.ANY)
+    vmem_spec = pl.BlockSpec(memory_space=pltpu.VMEM)
+    outs = pl.pallas_call(
+        forward_kernel,
+        out_shape=[jax.ShapeDtypeStruct(*s) for s in shapes.values()],
+        in_specs=[vmem_spec] * len(arrays) + [any_spec] * 4,
+        out_specs=[any_spec] * len(shapes),
+        scratch_shapes=scratch,
+        compiler_params=pltpu.CompilerParams(
+            collective_id=0, has_side_effects=True, vmem_limit_bytes=62 << 20
+        ),
+    )(*arrays, *half_weights)
+    return dict(zip(shapes, outs))
+
+def token_tables(lengths, head_bucket, width_bucket, tokens, tensor_index):
+    info = jnp.stack([lengths[0], head_bucket[0], width_bucket[0]])
+    far_info = dp_swap(info, HIDDEN_BIT)
+    pair = [token_info(i[0], i[1], i[2], tokens) for i in (info, far_info)]
+    segment, offset, head_tok, width_tok = [jnp.stack([a, b]) for a, b in zip(*pair)]
+    head_mask = (head_tok.reshape(-1) >= tensor_index).astype(jnp.float32)[:, None]
+    width_mask = (width_tok.reshape(-1) >= tensor_index).astype(jnp.float32)[:, None]
+    cosine, sine_part = [v[:, 0] for v in rotary_tables(offset.reshape(-1), HD)]
+    return (
+        segment,
+        head_mask,
+        width_mask,
+        jnp.concatenate([cosine, cosine], axis=1),
+        jnp.concatenate([-sine_part, sine_part], axis=1),
+    )
+
+
+def count_buckets(lengths, width_bucket, total):
+    matches = (width_bucket[0][:, None] == jnp.arange(total, dtype=jnp.int32)[None, :]).astype(
+        jnp.int32
+    )
+    return sum_all(jnp.sum(lengths[0][:, None] * matches, axis=0), ("dp",))
+
+
+def side_first(weight, axis):
+    shape = weight.shape
+    split = weight.reshape(shape[:axis] + (2, shape[axis] // 2) + shape[axis + 1 :])
+    return jnp.moveaxis(split, axis, 0)
+
+
+def local_fast(
+    residual_in,
+    lengths,
+    head_bucket,
+    width_bucket,
+    norm1_gain,
+    norm1_shift,
+    w_qkv,
+    w_out,
+    norm2_gain,
+    norm2_shift,
+    w_up,
+    w_down,
+    cotangent,
+):
+    f32, bf16 = jnp.float32, jnp.bfloat16
+    dot = functools.partial(jnp.dot, preferred_element_type=f32)
+    tokens = residual_in.shape[0]
+    tensor_index = lax.axis_index("tensor")
+    side = (lax.axis_index("dp") // HIDDEN_BIT) % 2
+    segment, head_mask, width_mask, cosine, sine = token_tables(
+        lengths, head_bucket, width_bucket, tokens, tensor_index
+    )
+    bucket_counts = count_buckets(lengths, width_bucket, lax.axis_size("tensor"))
+    half_qkv = side_first(w_qkv, 2).reshape(2, w_qkv.shape[0], -1)
+    half_weights = (half_qkv, side_first(w_out, 0), side_first(w_up, 1), side_first(w_down, 0))
+    arrays = (
+        residual_in,
+        cotangent,
+        norm1_gain[None],
+        norm1_shift[None],
+        norm2_gain[None],
+        norm2_shift[None],
+        cosine,
+        sine,
+        segment.reshape(-1, 1),
+        segment[:, None, :],
+        head_mask,
+        width_mask,
+    )
+    got = forward_call(arrays, half_weights)
+
+    def rows_of_stream(s):
+        return jnp.swapaxes(s, 1, 2).reshape(2 * tokens, -1)
+
+    full_qkv, full_up = got["all_qkv"], got["all_up"]
+    full_out, full_down = [
+        jnp.swapaxes(got[k], 0, 1).reshape(got[k].shape[1], -1) for k in ("all_out", "all_down")
+    ]
+    normed1, normed2, mixed, middle = [got[k] for k in ("normed1", "normed2", "mixed", "middle")]
+    query, key, value = [heads_of(h, 2) for h in got["heads"]]
+    weights = jnp.where(jnp.tril(jnp.ones((tokens, tokens), bool)), got["weights"], 0)
+    weights = jnp.swapaxes(weights.reshape(2, -1, tokens, tokens), 0, 1).reshape(weights.shape)
+    _, unit1, inverse1 = norm_forward(rows_of_stream(got["stream1"]), norm1_gain, norm1_shift)
+    _, unit2, inverse2 = norm_forward(rows_of_stream(got["stream2"]), norm2_gain, norm2_shift)
+    upper = got["upper"]
+    active = jnp.square(upper.astype(f32)).astype(bf16)
+    width = mixed.shape[1]
+    score_scale = HD ** (-0.5)
+    output = middle + stream_sum(dot(active, full_down))
+    cosine, sine_part = cosine[:, None, : HD // 2], sine[:, None, HD // 2 :]
+
+    grad_top = rows_of_stream(got["stream_c"])
+    grad_down = scatter_weight(cut_weight(dot(active.T, grad_top).astype(bf16), 1))
+    grad_active = dot(grad_top, full_down.T)
+    grad_upper = (grad_active * 2.0 * upper.astype(f32)).astype(bf16)
+    grad_normed2 = dot(grad_upper, full_up.T)
+    part_middle, gain2_grad, shift2_grad = norm_backward(
+        grad_normed2, unit2, inverse2, norm2_gain
+    )
+    grad_middle = cotangent + stream_sum(part_middle)
+    grad_up = scatter_weight(cut_weight(dot(normed2.T, grad_upper).astype(bf16), 0))
+    grad_branch = whole_stream(grad_middle)
+    grad_wout = scatter_weight(cut_weight(dot(mixed.T, grad_branch).astype(bf16), 1))
+    grad_mixed = (dot(grad_branch, full_out.T) * head_mask).astype(bf16)
+    grad_mixed = heads_of(grad_mixed, 2)
+    grad_weights = jnp.einsum("nqd,nkd->nqk", grad_mixed, value, preferred_element_type=f32)
+    grad_value = jnp.einsum("nqk,nqd->nkd", weights, grad_mixed, preferred_element_type=f32)
+    wide = weights.astype(f32)
+    grad_scores = wide * (grad_weights - jnp.sum(grad_weights * wide, axis=-1, keepdims=True))
+    grad_raw = (grad_scores * score_scale).astype(bf16)
+    grad_query = jnp.einsum("nqk,nkd->nqd", grad_raw, key, preferred_element_type=f32)
+    grad_key = jnp.einsum("nqk,nqd->nkd", grad_raw, query, preferred_element_type=f32)
+    grad_query, grad_key = [
+        rotate(rows_of(g, 2).reshape(2 * tokens, -1, HD), cosine, -sine_part).reshape(-1, width)
+        for g in (grad_query, grad_key)
+    ]
+    grad_projected = jnp.concatenate([grad_query, grad_key, rows_of(grad_value, 2)], axis=1)
+    grad_projected = grad_projected.astype(bf16)
+    grad_normed1 = dot(grad_projected, full_qkv.T)
+    part_input, gain1_grad, shift1_grad = norm_backward(
+        grad_normed1, unit1, inverse1, norm1_gain
+    )
+    grad_input = grad_middle + stream_sum(part_input)
+    grad_qkv = scatter_weight(cut_weight(dot(normed1.T, grad_projected).astype(bf16), 0))
+
+    def join(pair, axis):
+        left = jnp.where(side == 0, pair[0], pair[1])
+        right = jnp.where(side == 0, pair[1], pair[0])
+        return jnp.concatenate([left, right], axis=axis).astype(f32)
+
+    grad_qkv = join([g.reshape(g.shape[0], 3, width) for g in grad_qkv], 2)
+    grad_wout, grad_up, grad_down = join(grad_wout, 0), join(grad_up, 1), join(grad_down, 0)
+    gain2_grad, shift2_grad = sum_all(jnp.stack([gain2_grad, shift2_grad]), ("dp", "tensor"))
+    gain1_grad, shift1_grad = sum_all(jnp.stack([gain1_grad, shift1_grad]), ("dp", "tensor"))
+    return (
+        output,
+        grad_input,
+        gain1_grad,
+        shift1_grad,
+        grad_qkv,
+        grad_wout,
+        gain2_grad,
+        shift2_grad,
+        grad_up,
+        grad_down,
+        bucket_counts,
+    )
+
+
+def local(*args):
+    w_out = args[7]
+    if lax.axis_size("dp") == 8 and lax.axis_size("tensor") == 4 and w_out.shape[1] % 128 == 0:
+        return local_fast(*args)
+    return local_general(*args)
+
+
 def solution(mesh):
     placed = (
         P("dp", "tensor"),

time: 712 us -> 725 us (1.018)
  waiting for transfers between devices: 422 us -> 184 us
  Pallas kernels: 12.1 us -> 217 us
  local copies, waits for them, and re-layouts: 38.8 us -> 119 us
  starting transfers between devices: 97.2 us -> 67.2 us
  matrix products: 80.8 us -> 66.3 us
  other arithmetic: 54.3 us -> 61.6 us
    ppermute x74 -> x42, waiting for transfers between devices: 386 us -> 161 us  [dp_swap(): return lax.ppermute(value, 'dp', [(i, i ^ bit) for i in range(count)])]
    pallas_call x0 -> x1, Pallas kernels: none -> 210 us  [forward_call(): pl.pallas_call(forward_kernel, out_shape=[jax.ShapeDtypeStruct(*s) for s...]
    unnamed x109 -> x153, local copies, waits for them, and re-layouts: 17.5 us -> 51.9 us
    convert_element_type x1 -> x2, local copies, waits for them, and re-layouts: 0.27 us -> 24.2 us  [norm_forward(): values = values.astype(jnp.float32)]
    ppermute x74 -> x42, starting transfers between devices: 72.4 us -> 54.7 us  [dp_swap(): return lax.ppermute(value, 'dp', [(i, i ^ bit) for i in range(count)])]
    transpose x1 -> x5, local copies, waits for them, and re-layouts: 0.81 us -> 16.7 us  [the longest x2 8.86 us: local_fast(): jnp.swapaxes(got[k], 0, 1).reshape(got[k].shape[1], -1)]
    dot_general x18 -> x13, matrix products: 80.8 us -> 66.3 us  [the longest x1 9.42 us: local_fast(): grad_normed1 = dot(grad_projected, full_qkv.T)]
    ppermute x52 -> x28, waiting for transfers between devices: 36 us -> 22.9 us  [tensor_swap(): return lax.ppermute(value, 'tensor', [(i, i ^ bit) for i in range(count)])]
  transfers between devices with their start and end apart: 126 -> 70, of which waited for: 51 -> 28; matrix products, arithmetic and copies ran while one was open for 9% -> 18% of each run, Pallas kernels for 1% -> 1%
where the time goes in v2:
time: 725 us; the launch traced here: 718 us
  Pallas kernels  217 us (30%)
  waiting for transfers between devices  184 us (25%)
  local copies, waits for them, and re-layouts  119 us (16%)
  starting transfers between devices  67.2 us (9%)
  matrix products  66.3 us (9%)
  other arithmetic  61.6 us (8%)
    pallas_call x1, Pallas kernels, forward_call(): pl.pallas_call(forward_kernel, out_shape=[jax.ShapeDtypeStruct(*s) for s...  210 us
    ppermute x42, waiting for transfers between devices, dp_swap(): return lax.ppermute(value, 'dp', [(i, i ^ bit) for i in range(count)])  161 us
    ppermute x42, starting transfers between devices, dp_swap(): return lax.ppermute(value, 'dp', [(i, i ^ bit) for i in range(count)])  54.7 us
    unnamed x153, local copies, waits for them, and re-layouts  51.9 us
    convert_element_type x2, local copies, waits for them, and re-layouts, norm_forward(): values = values.astype(jnp.float32)  24.2 us
    ppermute x28, waiting for transfers between devices, tensor_swap(): return lax.ppermute(value, 'tensor', [(i, i ^ bit) for i in range(count)])  22.9 us
  transfers between devices with their start and end apart: 70, of which 28 were waited for; matrix products, arithmetic and copies ran while one was open for 18% of the time, Pallas kernels for 1%

profile of v2, /device:TPU:0, one launch (start us, length us, event | category | flops | bytes accessed | tf_op | source)
XLA Modules:
  0.0 717.8 jit_solution(9280475933855655665)
XLA Ops:
  30.5 209.7 %shard_map.212 = (bf16[2048,768]{1,0:T(8,128)(2,1)}, bf16[8,256,256]{2,1,0:T(8,128)(2,1)}, bf16[2048,1024]{1,0:T(8,128)(2,1)}, bf16[8,1024,256]{2,1,0:T(8,128)(2...) custom-call(f32[512,512]{1,0:T(8,128)} %residual.1, ...), custom_call_target="tpu_custom_call" | custom-call | tf_op jit(solution)/shard_map/pallas_call | solution.py:901
  262.9 6.6 copy.127
  269.5 7.2 convolution_convert_fusion.refs_0_
  276.7 5.2 fusion.2
  281.9 6.2 convolution_convert_fusion.2.refs_0_
  294.0 4.9 convolution_convert_fusion.1.refs_0_
  306.5 12.1 %copy.129 = f32[2,512,4,512]{3,2,1,0:T(4,128)} copy(f32[2,512,4,512]{3,1,2,0:T(8,128)} %convert_bitcast_fusion.1) | data formatting | bytes 16777216 | tf_op jit(solution)/shard_map/convert_element_type | solution.py:233
  318.7 7.7 %copy.163 = f32[128,8,4,512]{3,1,2,0:T(8,128)S(1)} copy(f32[128,8,4,512]{3,2,1,0:T(4,128)} %bitcast.171) | data formatting | bytes 16777216
  326.4 8.4 %multiply_reduce_fusion = (f32[2048]{0:T(1024)S(1)}, f32[1024]{0:T(1024)S(1)}, f32[1024]{0:T(1024)S(1)}, f32[2048]{0:T(1024)S(1)}, f32[1024,2048]{1,0:T(8,128)}) fusion(f32[1024,2048]{1,0:T(8,128)S(1)} %bitcast.169, f32[1024]{0:T(1024)S(1)} %bitcast.241, f32[1024]{0:T(1024)S(1)} %bitcast.239, f32[2048]{0:T(1024)S(1)} %copy-done.55, ...), kind=kOutput, calls=%fused_computation.3 | convolution fusion | flops 4313835520 | bytes 23109632 | tf_op jit(solution)/shard_map/dot_general | solution.py:1009
  346.4 7.7 %collective-permute-start.50 = (f32[2,2048]{1,0:T(2,128)S(1)}, f32[2,2048]{1,0:T(2,128)S(1)}, u32[]{:S(2)}, u32[]{:S(2)}) collective-permute-start(f32[2,2048]{1,0:T(2,128)S(1)} %fusion.61), channel_id=1, source_target_pairs={{0,16},{4,20},{8,24},{12,28},{16,0},{20,4},{24,8},{28,12},{1,17},{... | collective-permute-start | bytes 49160 | tf_op jit(solution)/shard_map/ppermute | solution.py:19
  356.0 7.3 %multiply_convert_fusion.1.refs_0_ = bf16[1024,2048]{1,0:T(8,128)(2,1)S(1)} fusion(f32[1024,2048]{1,0:T(8,128)} %get-tuple-element.248, f32[1024,2048]{1,0:T(8,128)} %bitcast.170, f32[1024]{0:T(1024)S(1)} %broadcast_multiply_fusion.2, f32[1024]{0:T(1024)S(1)} %bitcast.242, f32[1024]{0:T(1024)S(1)} %broadcast_multiply_fusion.3, f32[2048]{0:T(1024)S(1)} %copy-done.55, ...), kind=kLoop, calls=%fused_computation.9 | loop fusion | flops 16777216 | bytes 20996096 | tf_op jit(solution)/shard_map/convert_element_type | solution.py:188
  390.9 12.1 %copy.143 = f32[2,512,4,512]{3,2,1,0:T(4,128)} copy(f32[2,512,4,512]{3,1,2,0:T(8,128)} %convert_bitcast_fusion) | data formatting | bytes 16777216 | tf_op jit(solution)/shard_map/convert_element_type | solution.py:233
  403.1 11.0 %copy.168 = f32[128,8,4,512]{3,1,2,0:T(8,128)} copy(f32[128,8,4,512]{3,2,1,0:T(4,128)} %bitcast.172) | data formatting | bytes 16777216
  422.1 7.8 %collective-permute-done.57 = bf16[256,1024]{1,0:T(8,128)(2,1)S(1)} collective-permute-done((bf16[256,1024]{1,0:T(8,128)(2,1)S(1)}, bf16[256,1024]{1,0:T(8,128)(2,1)S(1)}, u32[]{:S(2)}, u32[]{:S(2)}) %collective-permute-start.57) | collective-permute-done | bytes 524320 | tf_op jit(solution)/shard_map/ppermute | solution.py:19
  436.6 9.9 %collective-permute-done.13 = bf16[512,512]{1,0:T(8,128)(2,1)S(1)} collective-permute-done((bf16[512,512]{1,0:T(8,128)(2,1)S(1)}, bf16[512,512]{1,0:T(8,128)(2,1)S(1)}, u32[]{:S(2)}, u32[]{:S(2)}) %collective-permute-start.13) | collective-permute-done | bytes 524320 | tf_op jit(solution)/shard_map/ppermute | solution.py:24
  447.0 23.4 %collective-permute-done.65 = bf16[1024,256]{1,0:T(8,128)(2,1)S(1)} collective-permute-done((bf16[1024,256]{1,0:T(8,128)(2,1)S(1)}, bf16[1024,256]{1,0:T(8,128)(2,1)S(1)}, u32[]{:S(2)}, u32[]{:S(2)}) %collective-permute-start.65) | collective-permute-done | bytes 524320 | tf_op jit(solution)/shard_map/ppermute | solution.py:19
  473.8 7.9 %collective-permute-done.58 = bf16[256,1024]{1,0:T(8,128)(2,1)S(1)} collective-permute-done((bf16[256,1024]{1,0:T(8,128)(2,1)S(1)}, bf16[256,1024]{1,0:T(8,128)(2,1)S(1)}, u32[]{:S(2)}, u32[]{:S(2)}) %collective-permute-start.58) | collective-permute-done | bytes 524320 | tf_op jit(solution)/shard_map/ppermute | solution.py:19
  483.3 9.6 %collective-permute-done.14 = bf16[512,512]{1,0:T(8,128)(2,1)S(1)} collective-permute-done((bf16[512,512]{1,0:T(8,128)(2,1)S(1)}, bf16[512,512]{1,0:T(8,128)(2,1)S(1)}, u32[]{:S(2)}, u32[]{:S(2)}) %collective-permute-start.14) | collective-permute-done | bytes 524320 | tf_op jit(solution)/shard_map/ppermute | solution.py:19
  497.8 9.3 %collective-permute-done.62 = bf16[1024,256]{1,0:T(8,128)(2,1)S(1)} collective-permute-done((bf16[1024,256]{1,0:T(8,128)(2,1)S(1)}, bf16[1024,256]{1,0:T(8,128)(2,1)S(1)}, u32[]{:S(2)}, u32[]{:S(2)}) %collective-permute-start.62) | collective-permute-done | bytes 524320 | tf_op jit(solution)/shard_map/ppermute | solution.py:19
  509.3 10.3 %collective-permute-done.66 = bf16[1024,256]{1,0:T(8,128)(2,1)S(1)} collective-permute-done((bf16[1024,256]{1,0:T(8,128)(2,1)S(1)}, bf16[1024,256]{1,0:T(8,128)(2,1)S(1)}, u32[]{:S(2)}, u32[]{:S(2)}) %collective-permute-start.66) | collective-permute-done | bytes 524320 | tf_op jit(solution)/shard_map/ppermute | solution.py:19
  521.3 8.2 %collective-permute-done.55 = bf16[256,1024]{1,0:T(8,128)(2,1)S(1)} collective-permute-done((bf16[256,1024]{1,0:T(8,128)(2,1)S(1)}, bf16[256,1024]{1,0:T(8,128)(2,1)S(1)}, u32[]{:S(2)}, u32[]{:S(2)}) %collective-permute-start.55) | collective-permute-done | bytes 524320 | tf_op jit(solution)/shard_map/ppermute | solution.py:19
  529.5 11.2 %collective-permute-done.59 = bf16[256,1024]{1,0:T(8,128)(2,1)S(1)} collective-permute-done((bf16[256,1024]{1,0:T(8,128)(2,1)S(1)}, bf16[256,1024]{1,0:T(8,128)(2,1)S(1)}, u32[]{:S(2)}, u32[]{:S(2)}) %collective-permute-start.59) | collective-permute-done | bytes 524320 | tf_op jit(solution)/shard_map/ppermute | solution.py:19
  541.6 10.3 %collective-permute-done.18.refs_4_ = bf16[512,512]{1,0:T(8,128)(2,1)S(1)} collective-permute-done((bf16[512,512]{1,0:T(8,128)(2,1)S(1)}, bf16[512,512]{1,0:T(8,128)(2,1)S(1)}, u32[]{:S(2)}, u32[]{:S(2)}) %collective-permute-start.18) | collective-permute-done | bytes 524320 | tf_op jit(solution)/shard_map/ppermute | solution.py:19
  555.4 9.9 %collective-permute-done.20.refs_6_ = bf16[512,512]{1,0:T(8,128)(2,1)S(1)} collective-permute-done((bf16[512,512]{1,0:T(8,128)(2,1)S(1)}, bf16[512,512]{1,0:T(8,128)(2,1)S(1)}, u32[]{:S(2)}, u32[]{:S(2)}) %collective-permute-start.20) | collective-permute-done | bytes 524320 | tf_op jit(solution)/shard_map/ppermute | solution.py:24
  576.9 6.0 fusion.8
  587.7 6.6 fusion.9
  603.6 9.4 %multiply_reduce_fusion.1 = (f32[2048]{0:T(1024)S(1)}, f32[1024]{0:T(1024)S(1)}, f32[1024]{0:T(1024)S(1)}, f32[2048]{0:T(1024)S(1)}, f32[1024,2048]{1,0:T(8,128)S(1)}) fusion(f32[1024,2048]{1,0:T(8,128)} %bitcast.165, f32[1024]{0:T(1024)S(1)} %bitcast.237, f32[1024]{0:T(1024)S(1)} %bitcast.235, f32[2048]{0:T(1024)S(1)} %copy-done.56, ...), kind=kOutput, calls=%fused_computation.4 | convolution fusion | flops 3244812288 | bytes 21536768 | tf_op jit(solution)/shard_map/dot_general | solution.py:1032
  632.7 5.8 convolution_convert_fusion.3.refs_0_
  644.6 7.4 %collective-permute-done.46 = bf16[256,256]{1,0:T(8,128)(2,1)S(1)} collective-permute-done((bf16[256,256]{1,0:T(8,128)(2,1)S(1)}, bf16[256,256]{1,0:T(8,128)(2,1)S(1)}, u32[]{:S(2)}, u32[]{:S(2)}) %collective-permute-start.46) | collective-permute-done | bytes 131104 | tf_op jit(solution)/shard_map/ppermute | solution.py:19
  655.8 4.9 collective-permute-done.43
  669.7 12.2 %collective-permute-done.39 = bf16[256,768]{1,0:T(8,128)(2,1)S(1)} collective-permute-done((bf16[256,768]{1,0:T(8,128)(2,1)S(1)}, bf16[256,768]{1,0:T(8,128)(2,1)S(1)}, u32[]{:S(2)}, u32[]{:S(2)}) %collective-permute-start.39) | collective-permute-done | bytes 393248 | tf_op jit(solution)/shard_map/ppermute | solution.py:19
  687.5 14.4 %collective-permute-done.36 = bf16[256,768]{1,0:T(8,128)(2,1)S(1)} collective-permute-done((bf16[256,768]{1,0:T(8,128)(2,1)S(1)}, bf16[256,768]{1,0:T(8,128)(2,1)S(1)}, u32[]{:S(2)}, u32[]{:S(2)}) %collective-permute-start.36) | collective-permute-done | bytes 393248 | tf_op jit(solution)/shard_map/ppermute | solution.py:19
  (401 shorter events, 224.9 us)
Async XLA Ops:
  1.4 20.9 %collective-permute-start = (s32[3,4]{1,0:T(4,128)S(1)}, s32[3,4]{1,0:T(4,128)S(1)}, u32[]{:S(2)}, u32[]{:S(2)}) collective-permute-start(s32[3,4]{1,0:T(4,128)S(1)} %pad_add_fusion.1), channel_id=1, source_target_pairs={{0,8},{4,12},{8,0},{12,4},{16,24},{20,28},{24,16},{28,20},{1,9},{5... | collective-permute-start | bytes 152 | tf_op jit(solution)/shard_map/ppermute | solution.py:19
  291.9 125.0 %collective-permute-start.64 = (bf16[1024,256]{1,0:T(8,128)(2,1)}, bf16[1024,256]{1,0:T(8,128)(2,1)}, u32[]{:S(2)}, u32[]{:S(2)}) collective-permute-start(bf16[1024,256]{1,0:T(8,128)(2,1)} %get-tuple-element.150), channel_id=1, source_target_pairs={{0,4},{4,0},{8,12},{12,8},{16,20},{20,16},{24,28},{28,24},{1,5},{5... | collective-permute-start | bytes 1572872 | tf_op jit(solution)/shard_map/ppermute | solution.py:19
  293.2 143.2 %collective-permute-start.63 = (bf16[1024,256]{1,0:T(8,128)(2,1)}, bf16[1024,256]{1,0:T(8,128)(2,1)}, u32[]{:S(2)}, u32[]{:S(2)}) collective-permute-start(bf16[1024,256]{1,0:T(8,128)(2,1)} %get-tuple-element.148), channel_id=1, source_target_pairs={{0,4},{4,0},{8,12},{12,8},{16,20},{20,16},{24,28},{28,24},{1,5},{5... | collective-permute-start | bytes 1572872 | tf_op jit(solution)/shard_map/ppermute | solution.py:19
  304.0 116.3 %collective-permute-start.54 = (bf16[256,1024]{1,0:T(8,128)(2,1)}, bf16[256,1024]{1,0:T(8,128)(2,1)}, u32[]{:S(2)}, u32[]{:S(2)}) collective-permute-start(bf16[256,1024]{1,0:T(8,128)(2,1)} %get-tuple-element.138), channel_id=1, source_target_pairs={{0,4},{4,0},{8,12},{12,8},{16,20},{20,16},{24,28},{28,24},{1,5},{5... | collective-permute-start | bytes 1572872 | tf_op jit(solution)/shard_map/ppermute | solution.py:19
  339.0 80.0 %collective-permute-start.61 = (bf16[1024,256]{1,0:T(8,128)(2,1)}, bf16[1024,256]{1,0:T(8,128)(2,1)}, u32[]{:S(2)}, u32[]{:S(2)}) collective-permute-start(bf16[1024,256]{1,0:T(8,128)(2,1)} %get-tuple-element.146), channel_id=1, source_target_pairs={{0,4},{4,0},{8,12},{12,8},{16,20},{20,16},{24,28},{28,24},{1,5},{5... | collective-permute-start | bytes 1572872 | tf_op jit(solution)/shard_map/ppermute | solution.py:19
  363.3 51.7 %collective-permute-start.52 = (f32[2,2048]{1,0:T(2,128)S(1)}, f32[2,2048]{1,0:T(2,128)S(1)}, u32[]{:S(2)}, u32[]{:S(2)}) collective-permute-start(f32[2,2048]{1,0:T(2,128)S(1)} %add.261), channel_id=1, source_target_pairs={{0,2},{1,3},{2,0},{3,1},{4,6},{5,7},{6,4},{7,5},{8,10},{9,11},{10,... | collective-permute-start | bytes 49160 | tf_op jit(solution)/shard_map/ppermute | solution.py:24
  416.9 55.3 %collective-permute-start.56 = (bf16[256,1024]{1,0:T(8,128)(2,1)S(1)}, bf16[256,1024]{1,0:T(8,128)(2,1)S(1)}, u32[]{:S(2)}, u32[]{:S(2)}) collective-permute-start(bf16[256,1024]{1,0:T(8,128)(2,1)S(1)} %copy-done.20), channel_id=1, source_target_pairs={{0,4},{4,0},{8,12},{12,8},{16,20},{20,16},{24,28},{28,24},{1,5},{5... | collective-permute-start | bytes 1572872 | tf_op jit(solution)/shard_map/ppermute | solution.py:19
  433.3 37.1 %collective-permute-start.65 = (bf16[1024,256]{1,0:T(8,128)(2,1)S(1)}, bf16[1024,256]{1,0:T(8,128)(2,1)S(1)}, u32[]{:S(2)}, u32[]{:S(2)}) collective-permute-start(bf16[1024,256]{1,0:T(8,128)(2,1)S(1)} %add_convert_fusion.1), channel_id=1, source_target_pairs={{0,16},{4,20},{8,24},{12,28},{16,0},{20,4},{24,8},{28,12},{1,17},{... | collective-permute-start | bytes 1572872 | tf_op jit(solution)/shard_map/ppermute | solution.py:19
  436.4 37.5 %collective-permute-start.8 = (bf16[512,512]{1,0:T(8,128)(2,1)S(1)}, bf16[512,512]{1,0:T(8,128)(2,1)S(1)}, u32[]{:S(2)}, u32[]{:S(2)}) collective-permute-start(bf16[512,512]{1,0:T(8,128)(2,1)S(1)} %copy-done.24), channel_id=1, source_target_pairs={{0,1},{1,0},{2,3},{3,2},{4,5},{5,4},{6,7},{7,6},{8,9},{9,8},{10,11... | collective-permute-start | bytes 1572872 | tf_op jit(solution)/shard_map/ppermute | solution.py:24
  436.5 45.2 %collective-permute-start.58 = (bf16[256,1024]{1,0:T(8,128)(2,1)S(1)}, bf16[256,1024]{1,0:T(8,128)(2,1)S(1)}, u32[]{:S(2)}, u32[]{:S(2)}) collective-permute-start(bf16[256,1024]{1,0:T(8,128)(2,1)S(1)} %add_convert_fusion.7), channel_id=1, source_target_pairs={{0,16},{4,20},{8,24},{12,28},{16,0},{20,4},{24,8},{28,12},{1,17},{... | collective-permute-start | bytes 1572872 | tf_op jit(solution)/shard_map/ppermute | solution.py:19
  446.5 35.2 %collective-permute-start.10 = (bf16[512,512]{1,0:T(8,128)(2,1)S(1)}, bf16[512,512]{1,0:T(8,128)(2,1)S(1)}, u32[]{:S(2)}, u32[]{:S(2)}) collective-permute-start(bf16[512,512]{1,0:T(8,128)(2,1)S(1)} %add_convert_fusion.22), channel_id=1, source_target_pairs={{0,2},{1,3},{2,0},{3,1},{4,6},{5,7},{6,4},{7,5},{8,10},{9,11},{10,... | collective-permute-start | bytes 1572872 | tf_op jit(solution)/shard_map/ppermute | solution.py:24
  470.4 22.5 %collective-permute-start.14 = (bf16[512,512]{1,0:T(8,128)(2,1)S(1)}, bf16[512,512]{1,0:T(8,128)(2,1)S(1)}, u32[]{:S(2)}, u32[]{:S(2)}) collective-permute-start(bf16[512,512]{1,0:T(8,128)(2,1)S(1)} %add_convert_fusion.18), channel_id=1, source_target_pairs={{0,8},{4,12},{8,0},{12,4},{16,24},{20,28},{24,16},{28,20},{1,9},{5... | collective-permute-start | bytes 1572872 | tf_op jit(solution)/shard_map/ppermute | solution.py:19
  472.3 21.1 %collective-permute-start.60 = (bf16[1024,256]{1,0:T(8,128)(2,1)S(1)}, bf16[1024,256]{1,0:T(8,128)(2,1)S(1)}, u32[]{:S(2)}, u32[]{:S(2)}) collective-permute-start(bf16[1024,256]{1,0:T(8,128)(2,1)S(1)} %copy-done.18), channel_id=1, source_target_pairs={{0,4},{4,0},{8,12},{12,8},{16,20},{20,16},{24,28},{28,24},{1,5},{5... | collective-permute-start | bytes 1572872 | tf_op jit(solution)/shard_map/ppermute | solution.py:19
  481.7 25.4 %collective-permute-start.62 = (bf16[1024,256]{1,0:T(8,128)(2,1)S(1)}, bf16[1024,256]{1,0:T(8,128)(2,1)S(1)}, u32[]{:S(2)}, u32[]{:S(2)}) collective-permute-start(bf16[1024,256]{1,0:T(8,128)(2,1)S(1)} %add_convert_fusion.4), channel_id=1, source_target_pairs={{0,16},{4,20},{8,24},{12,28},{16,0},{20,4},{24,8},{28,12},{1,17},{... | collective-permute-start | bytes 1572872 | tf_op jit(solution)/shard_map/ppermute | solution.py:19
  481.7 25.4 %collective-permute-start.6 = (bf16[512,512]{1,0:T(8,128)(2,1)S(1)}, bf16[512,512]{1,0:T(8,128)(2,1)S(1)}, u32[]{:S(2)}, u32[]{:S(2)}) collective-permute-start(bf16[512,512]{1,0:T(8,128)(2,1)S(1)} %add_convert_fusion.25), channel_id=1, source_target_pairs={{0,2},{1,3},{2,0},{3,1},{4,6},{5,7},{6,4},{7,5},{8,10},{9,11},{10,... | collective-permute-start | bytes 1572872 | tf_op jit(solution)/shard_map/ppermute | solution.py:24
  492.9 26.7 %collective-permute-start.66 = (bf16[1024,256]{1,0:T(8,128)(2,1)S(1)}, bf16[1024,256]{1,0:T(8,128)(2,1)S(1)}, u32[]{:S(2)}, u32[]{:S(2)}) collective-permute-start(bf16[1024,256]{1,0:T(8,128)(2,1)S(1)} %add_convert_fusion), channel_id=1, source_target_pairs={{0,8},{4,12},{8,0},{12,4},{16,24},{20,28},{24,16},{28,20},{1,9},{5... | collective-permute-start | bytes 1572872 | tf_op jit(solution)/shard_map/ppermute | solution.py:19
  493.4 26.6 %collective-permute-start.53 = (bf16[256,1024]{1,0:T(8,128)(2,1)S(1)}, bf16[256,1024]{1,0:T(8,128)(2,1)S(1)}, u32[]{:S(2)}, u32[]{:S(2)}) collective-permute-start(bf16[256,1024]{1,0:T(8,128)(2,1)S(1)} %copy-done.16), channel_id=1, source_target_pairs={{0,4},{4,0},{8,12},{12,8},{16,20},{20,16},{24,28},{28,24},{1,5},{5... | collective-permute-start | bytes 1572872 | tf_op jit(solution)/shard_map/ppermute | solution.py:19
  494.6 34.9 %collective-permute-start.55 = (bf16[256,1024]{1,0:T(8,128)(2,1)S(1)}, bf16[256,1024]{1,0:T(8,128)(2,1)S(1)}, u32[]{:S(2)}, u32[]{:S(2)}) collective-permute-start(bf16[256,1024]{1,0:T(8,128)(2,1)S(1)} %add_convert_fusion.10), channel_id=1, source_target_pairs={{0,16},{4,20},{8,24},{12,28},{16,0},{20,4},{24,8},{28,12},{1,17},{... | collective-permute-start | bytes 1572872 | tf_op jit(solution)/shard_map/ppermute | solution.py:19
  507.1 33.6 %collective-permute-start.59 = (bf16[256,1024]{1,0:T(8,128)(2,1)S(1)}, bf16[256,1024]{1,0:T(8,128)(2,1)S(1)}, u32[]{:S(2)}, u32[]{:S(2)}) collective-permute-start(bf16[256,1024]{1,0:T(8,128)(2,1)S(1)} %add_convert_fusion.6), channel_id=1, source_target_pairs={{0,8},{4,12},{8,0},{12,4},{16,24},{20,28},{24,16},{28,20},{1,9},{5... | collective-permute-start | bytes 1572872 | tf_op jit(solution)/shard_map/ppermute | solution.py:19
  507.1 44.8 %collective-permute-start.18 = (bf16[512,512]{1,0:T(8,128)(2,1)S(1)}, bf16[512,512]{1,0:T(8,128)(2,1)S(1)}, u32[]{:S(2)}, u32[]{:S(2)}) collective-permute-start(bf16[512,512]{1,0:T(8,128)(2,1)S(1)} %fusion.34.refs_0_), channel_id=1, source_target_pairs={{0,8},{4,12},{8,0},{12,4},{16,24},{20,28},{24,16},{28,20},{1,9},{5... | collective-permute-start | bytes 1572872 | tf_op jit(solution)/shard_map/ppermute | solution.py:19
  519.6 35.1 %collective-permute-start.1 = (bf16[512,512]{1,0:T(8,128)(2,1)S(1)}, bf16[512,512]{1,0:T(8,128)(2,1)S(1)}, u32[]{:S(2)}, u32[]{:S(2)}) collective-permute-start(bf16[512,512]{1,0:T(8,128)(2,1)S(1)} %get-tuple-element.85), channel_id=1, source_target_pairs={{0,1},{1,0},{2,3},{3,2},{4,5},{5,4},{6,7},{7,6},{8,9},{9,8},{10,11... | collective-permute-start | bytes 1572872 | tf_op jit(solution)/shard_map/ppermute | solution.py:24
  520.0 34.8 %collective-permute-start.3 = (bf16[512,512]{1,0:T(8,128)(2,1)S(1)}, bf16[512,512]{1,0:T(8,128)(2,1)S(1)}, u32[]{:S(2)}, u32[]{:S(2)}) collective-permute-start(bf16[512,512]{1,0:T(8,128)(2,1)S(1)} %add_convert_fusion.28), channel_id=1, source_target_pairs={{0,2},{1,3},{2,0},{3,1},{4,6},{5,7},{6,4},{7,5},{8,10},{9,11},{10,... | collective-permute-start | bytes 1572872 | tf_op jit(solution)/shard_map/ppermute | solution.py:24
  529.5 37.3 %collective-permute-start.7 = (bf16[512,512]{1,0:T(8,128)(2,1)S(1)}, bf16[512,512]{1,0:T(8,128)(2,1)S(1)}, u32[]{:S(2)}, u32[]{:S(2)}) collective-permute-start(bf16[512,512]{1,0:T(8,128)(2,1)S(1)} %add_convert_fusion.24), channel_id=1, source_target_pairs={{0,8},{4,12},{8,0},{12,4},{16,24},{20,28},{24,16},{28,20},{1,9},{5... | collective-permute-start | bytes 1572872 | tf_op jit(solution)/shard_map/ppermute | solution.py:19
  616.0 27.6 %collective-permute-start.42 = (bf16[256,256]{1,0:T(8,128)(2,1)S(1)}, bf16[256,256]{1,0:T(8,128)(2,1)S(1)}, u32[]{:S(2)}, u32[]{:S(2)}) collective-permute-start(bf16[256,256]{1,0:T(8,128)(2,1)S(1)} %get-tuple-element.129), channel_id=1, source_target_pairs={{0,4},{4,0},{8,12},{12,8},{16,20},{20,16},{24,28},{28,24},{1,5},{5... | collective-permute-start | bytes 393224 | tf_op jit(solution)/shard_map/ppermute | solution.py:19
  616.7 25.7 %collective-permute-start.45 = (bf16[256,256]{1,0:T(8,128)(2,1)S(1)}, bf16[256,256]{1,0:T(8,128)(2,1)S(1)}, u32[]{:S(2)}, u32[]{:S(2)}) collective-permute-start(bf16[256,256]{1,0:T(8,128)(2,1)S(1)} %get-tuple-element.133), channel_id=1, source_target_pairs={{0,4},{4,0},{8,12},{12,8},{16,20},{20,16},{24,28},{28,24},{1,5},{5... | collective-permute-start | bytes 393224 | tf_op jit(solution)/shard_map/ppermute | solution.py:19
  618.1 26.4 %collective-permute-start.44 = (bf16[256,256]{1,0:T(8,128)(2,1)S(1)}, bf16[256,256]{1,0:T(8,128)(2,1)S(1)}, u32[]{:S(2)}, u32[]{:S(2)}) collective-permute-start(bf16[256,256]{1,0:T(8,128)(2,1)S(1)} %get-tuple-element.131), channel_id=1, source_target_pairs={{0,4},{4,0},{8,12},{12,8},{16,20},{20,16},{24,28},{28,24},{1,5},{5... | collective-permute-start | bytes 393224 | tf_op jit(solution)/shard_map/ppermute | solution.py:19
  618.8 36.1 %collective-permute-start.41 = (bf16[256,256]{1,0:T(8,128)(2,1)S(1)}, bf16[256,256]{1,0:T(8,128)(2,1)S(1)}, u32[]{:S(2)}, u32[]{:S(2)}) collective-permute-start(bf16[256,256]{1,0:T(8,128)(2,1)S(1)} %get-tuple-element.127), channel_id=1, source_target_pairs={{0,4},{4,0},{8,12},{12,8},{16,20},{20,16},{24,28},{28,24},{1,5},{5... | collective-permute-start | bytes 393224 | tf_op jit(solution)/shard_map/ppermute | solution.py:19
  660.7 25.9 %collective-permute-start.34 = (bf16[256,768]{1,0:T(8,128)(2,1)S(1)}, bf16[256,768]{1,0:T(8,128)(2,1)S(1)}, u32[]{:S(2)}, u32[]{:S(2)}) collective-permute-start(bf16[256,768]{1,0:T(8,128)(2,1)S(1)} %get-tuple-element.118), channel_id=1, source_target_pairs={{0,4},{4,0},{8,12},{12,8},{16,20},{20,16},{24,28},{28,24},{1,5},{5... | collective-permute-start | bytes 1179656 | tf_op jit(solution)/shard_map/ppermute | solution.py:19
  669.7 43.4 %collective-permute-start.22 = (bf16[512,512]{1,0:T(8,128)(2,1)S(1)}, bf16[512,512]{1,0:T(8,128)(2,1)}, u32[]{:S(2)}, u32[]{:S(2)}) collective-permute-start(bf16[512,512]{1,0:T(8,128)(2,1)S(1)} %get-tuple-element.109), channel_id=1, source_target_pairs={{0,1},{1,0},{2,3},{3,2},{4,5},{5,4},{6,7},{7,6},{8,9},{9,8},{10,11... | collective-permute-start | bytes 1572872 | tf_op jit(solution)/shard_map/ppermute | solution.py:24
  682.1 31.1 %collective-permute-start.24 = (bf16[512,512]{1,0:T(8,128)(2,1)}, bf16[512,512]{1,0:T(8,128)(2,1)}, u32[]{:S(2)}, u32[]{:S(2)}) collective-permute-start(bf16[512,512]{1,0:T(8,128)(2,1)} %add_convert_fusion.16), channel_id=1, source_target_pairs={{0,2},{1,3},{2,0},{3,1},{4,6},{5,7},{6,4},{7,5},{8,10},{9,11},{10,... | collective-permute-start | bytes 1572872 | tf_op jit(solution)/shard_map/ppermute | solution.py:24
  683.0 21.0 %collective-permute-start.40 = (bf16[256,768]{1,0:T(8,128)(2,1)S(1)}, bf16[256,768]{1,0:T(8,128)(2,1)S(1)}, u32[]{:S(2)}, u32[]{:S(2)}) collective-permute-start(bf16[256,768]{1,0:T(8,128)(2,1)S(1)} %add_convert_fusion.30), channel_id=1, source_target_pairs={{0,8},{4,12},{8,0},{12,4},{16,24},{20,28},{24,16},{28,20},{1,9},{5... | collective-permute-start | bytes 1179656 | tf_op jit(solution)/shard_map/ppermute | solution.py:19
  686.6 27.5 %collective-permute-start.28 = (bf16[512,512]{1,0:T(8,128)(2,1)}, bf16[512,512]{1,0:T(8,128)(2,1)}, u32[]{:S(2)}, u32[]{:S(2)}) collective-permute-start(bf16[512,512]{1,0:T(8,128)(2,1)} %add_convert_fusion.12), channel_id=1, source_target_pairs={{0,8},{4,12},{8,0},{12,4},{16,24},{20,28},{24,16},{28,20},{1,9},{5... | collective-permute-start | bytes 1572872 | tf_op jit(solution)/shard_map/ppermute | solution.py:19
  (103 other events, 1171.6 us)

commit v3 on v1

--- a/solution.py
+++ b/solution.py
@@ -3,6 +3,7 @@
 
 import jax
 import jax.numpy as jnp
+import numpy as np
 from jax import lax
 from jax.experimental import pallas as pl
 from jax.experimental.pallas import tpu as pltpu
@@ -258,7 +259,7 @@
     return jnp.transpose(heads, (1, 2, 0, 3)).reshape(blocks * heads.shape[2], -1)
 
 
-def local(
+def local_general(
     residual_in,
     lengths,
     head_bucket,
@@ -390,6 +391,1440 @@
     )
 
 
+def flip(i, bit):
+    return i + bit - 2 * bit * ((i // bit) % 2)
+
+
+class Traffic:
+    def __init__(self, send_sems, recv_sems):
+        self.send_sems, self.recv_sems = send_sems, recv_sems
+        self.copies, self.gone, self.come = {}, set(), set()
+
+    def send(self, name, src, dst, device):
+        k = len(self.copies)
+        copy = pltpu.make_async_remote_copy(
+            src_ref=src,
+            dst_ref=dst,
+            send_sem=self.send_sems.at[k],
+            recv_sem=self.recv_sems.at[k],
+            device_id=device,
+            device_id_type=pl.DeviceIdType.MESH,
+        )
+        copy.start()
+        self.copies[name] = copy
+
+    def wait(self, *names):
+        for name in names:
+            if name not in self.come:
+                self.copies[name].wait_recv()
+                self.come.add(name)
+
+    def sent(self, *names):
+        for name in names:
+            if name not in self.gone:
+                self.copies[name].wait_send()
+                self.gone.add(name)
+
+    def finish(self):
+        self.sent(*self.copies)
+
+
+class Moves:
+    def __init__(self, sems):
+        self.sems, self.copies = sems, {}
+
+    def start(self, name, src, dst):
+        copy = pltpu.make_async_copy(src, dst, self.sems.at[len(self.copies)])
+        copy.start()
+        self.copies[name] = [copy, False]
+
+    def wait(self, *names):
+        for name in names:
+            if not self.copies[name][1]:
+                self.copies[name][0].wait()
+                self.copies[name][1] = True
+
+    def finish(self):
+        self.wait(*self.copies)
+
+
+class Place:
+    def __init__(self):
+        self.i, self.t = lax.axis_index("dp"), lax.axis_index("tensor")
+        self.side = (self.i // 2 + self.i // 4) % 2
+        self.x, self.z = [(flip(self.i, b), self.t) for b in (1, 2)]
+        self.far = (self.block(6), self.t)
+        self.c, self.y = [(self.i, flip(self.t, b)) for b in (1, 2)]
+
+    def greet(self):
+        barrier = pltpu.get_barrier_semaphore()
+        partners = (self.x, self.z, self.far, self.c, self.y)
+        for device in partners:
+            pl.semaphore_signal(
+                barrier, inc=1, device_id=device, device_id_type=pl.DeviceIdType.MESH
+            )
+        pl.semaphore_wait(barrier, len(partners))
+
+    def block(self, m):
+        d = self.i
+        for bit in (1, 2, 4):
+            if m & bit:
+                d = flip(d, bit)
+        return d
+
+    def stripe(self, m):
+        s = self.t
+        for bit in (1, 2):
+            if m & bit:
+                s = flip(s, bit)
+        return s
+
+
+class WeightGather:
+    def __init__(self, name, place, traffic, moves, half, slot):
+        self.name, self.p, self.tr, self.mv = name, place, traffic, moves
+        self.half, self.slot = half, slot
+
+    def own(self):
+        self.mv.start(self.name + "0", self.half(self.p.side), self.slot(self.p.i))
+
+    def z(self):
+        self.tr.send(self.name + "2", self.half(1 - self.p.side), self.slot(self.p.i), self.p.z)
+
+    def far(self):
+        self.tr.send(self.name + "6", self.half(self.p.side), self.slot(self.p.i), self.p.far)
+
+    def x(self):
+        self.tr.send(self.name + "1", self.half(self.p.side), self.slot(self.p.i), self.p.x)
+
+    def far_next(self):
+        self.tr.wait(self.name + "2")
+        block = self.slot(self.p.block(2))
+        self.tr.send(self.name + "4", block, block, self.p.far)
+
+    def x_next(self, m):
+        self.tr.wait(self.name + str(m))
+        block = self.slot(self.p.block(m))
+        self.tr.send(self.name + str(m + 1), block, block, self.p.x)
+
+    def take(self, *which):
+        for m in which:
+            if m == 0:
+                self.mv.wait(self.name + "0")
+            else:
+                self.tr.wait(self.name + str(m))
+
+    def end(self):
+        self.take(*range(8))
+
+
+class ActGather:
+    def __init__(self, name, place, traffic, slots):
+        self.name, self.p, self.tr, self.slots = name, place, traffic, slots
+
+    def at(self, b, m):
+        return self.slots.at[b, self.p.stripe(m)]
+
+    def z(self):
+        self.tr.send(self.name + "10", self.at(0, 0), self.slots.at[1, self.p.t], self.p.z)
+
+    def y(self):
+        self.tr.send(self.name + "02", self.at(0, 0), self.at(0, 0), self.p.y)
+
+    def c(self):
+        self.tr.send(self.name + "01", self.at(0, 0), self.at(0, 0), self.p.c)
+
+    def pass_z(self):
+        self.tr.wait(self.name + "10")
+        block = self.at(1, 0)
+        self.tr.send(self.name + "12", block, block, self.p.y)
+        self.tr.send(self.name + "11", block, block, self.p.c)
+
+    def pass_y(self, b):
+        self.tr.wait(self.name + str(b) + "2")
+        block = self.at(b, 2)
+        self.tr.send(self.name + str(b) + "3", block, block, self.p.c)
+
+    def take(self, b):
+        for m in range(1 - b, 4):
+            self.tr.wait(self.name + str(b) + str(m))
+
+
+def loop_rows(count, step, body):
+    def run(k, carry):
+        body(pl.multiple_of(k * step, step))
+        return carry
+
+    lax.fori_loop(0, count // step, run, 0)
+
+
+def wide(value):
+    return value.astype(jnp.float32)
+
+
+def add_blocks(out, left, right, rows):
+    def body(r):
+        at = pl.ds(r, 64)
+        out[at, :] = (wide(left[at, :]) + wide(right[at, :])).astype(out.dtype)
+
+    loop_rows(rows, 64, body)
+
+
+class ActScatter:
+    def __init__(self, name, place, traffic, part, got_c, got_y, got_z):
+        self.name, self.p, self.tr = name, place, traffic
+        self.part, self.got_c, self.got_y, self.got_z = part, got_c, got_y, got_z
+        self.rows = part.shape[2]
+
+    def at(self, b, m):
+        return self.part.at[b, self.p.stripe(m)]
+
+    def c(self, b):
+        for j, m in ((1, 3), (0, 1)):
+            name = self.name + "c" + str(b) + str(j)
+            self.tr.send(name, self.at(b, m), self.got_c.at[b, j], self.p.c)
+
+    def add(self, b, m, name, got):
+        self.tr.wait(self.name + name)
+        add_blocks(self.at(b, m), self.at(b, m), got, self.rows)
+
+    def y(self, b):
+        self.add(b, 2, "c" + str(b) + "1", self.got_c.at[b, 1])
+        self.tr.send(self.name + "y" + str(b), self.at(b, 2), self.got_y.at[b], self.p.y)
+
+    def own(self, b):
+        self.add(b, 0, "c" + str(b) + "0", self.got_c.at[b, 0])
+
+    def z(self):
+        self.add(1, 0, "y1", self.got_y.at[1])
+        self.tr.send(self.name + "z", self.at(1, 0), self.got_z, self.p.z)
+
+    def home(self):
+        self.add(0, 0, "y0", self.got_y.at[0])
+
+    def sent(self):
+        for key in ("c11", "c01", "c10", "c00", "y1", "y0", "z"):
+            self.tr.sent(self.name + key)
+
+    def end(self, out, base):
+        self.tr.wait(self.name + "z")
+        own = self.at(0, 0)
+
+        def body(r):
+            at = pl.ds(r, 64)
+            out[at, :] = base[at, :] + (wide(own[at, :]) + wide(self.got_z[at, :]))
+
+        loop_rows(self.rows, 64, body)
+
+
+def round_rows(src, dst, rows):
+    def body(r):
+        at = pl.ds(r, 64)
+        dst[at, :] = src[at, :].astype(dst.dtype)
+
+    loop_rows(rows, 64, body)
+
+
+def dot_f32(left, right):
+    return jnp.dot(left, right, preferred_element_type=jnp.float32)
+
+
+def dot_nt(left, right):
+    return lax.dot_general(
+        left, right, (((1,), (1,)), ((), ())), preferred_element_type=jnp.float32
+    )
+
+
+def dot_tn(left, right):
+    return lax.dot_general(
+        left, right, (((0,), (0,)), ((), ())), preferred_element_type=jnp.float32
+    )
+
+
+def center_rows(slots, b, at):
+    stripes = slots.shape[1]
+    rows = jnp.concatenate([wide(slots[b, s, at, :]) for s in range(stripes)], axis=1)
+    center = rows - jnp.mean(rows, axis=1, keepdims=True)
+    spread = jnp.mean(center * center, axis=1, keepdims=True)
+    return center, lax.rsqrt(spread + epsilon)
+
+
+def norm_rows(slots, b, gain, shift, out):
+    rows = slots.shape[2]
+
+    def body(r):
+        center, inverse = center_rows(slots, b, pl.ds(r, 32))
+        out[pl.ds(b * rows + r, 32), :] = (center * inverse * gain[...] + shift[...]).astype(
+            jnp.bfloat16
+        )
+
+    loop_rows(rows, 32, body)
+
+
+def attend(b, qkv, seg_col, seg_row, head_mask, weights, mixed, scale):
+    tokens = seg_row.shape[2]
+    heads = qkv.shape[2] // HD
+    half = tokens // 2
+    start = b * tokens
+    for h in range(heads):
+        cols = pl.ds(h * HD, HD)
+        for part in range(2):
+            rows = pl.ds(start + part * half, half)
+            reach = half * (part + 1)
+            query = qkv[0, rows, cols]
+            key = qkv[1, pl.ds(start, reach), cols]
+            value = qkv[2, pl.ds(start, reach), cols]
+            scores = dot_nt(query, key) * scale
+            row_id = lax.broadcasted_iota(jnp.int32, (half, reach), 0) + part * half
+            col_id = lax.broadcasted_iota(jnp.int32, (half, reach), 1)
+            same = seg_col[rows, :] == seg_row[b, :, pl.ds(0, reach)]
+            scores = jnp.where(same & (row_id >= col_id), scores, -1000000000.0)
+            scores = jnp.exp(scores - jnp.max(scores, axis=1, keepdims=True))
+            total = jnp.sum(scores, axis=1, keepdims=True)
+            chosen = (scores / total).astype(jnp.bfloat16)
+            weights[b * heads + h, pl.ds(part * half, half), pl.ds(0, reach)] = chosen
+            mixed[rows, cols] = (dot_f32(chosen, value) * head_mask[rows, :]).astype(jnp.bfloat16)
+
+
+def sequences(lengths):
+    start = 0
+    for s in range(lengths.shape[1]):
+        length = lengths[0, s]
+        yield s, start, length
+        start = start + length
+
+
+def count_row(lengths, width_bucket, lanes):
+    lane = lax.broadcasted_iota(jnp.int32, (1, lanes), 1)
+    row = jnp.zeros((1, lanes), jnp.float32)
+    for s, _, length in sequences(lengths):
+        row = row + jnp.where(lane == width_bucket[0, s], wide(length), 0.0)
+    return row
+
+
+def fill_facts(lengths, head_bucket, width_bucket, place_cosine, place_sine, facts):
+    lanes = facts.shape[1]
+    row = lax.broadcasted_iota(jnp.int32, (8, lanes), 0)
+    lane = lax.broadcasted_iota(jnp.int32, (8, lanes), 1)
+    count = lengths.shape[1]
+    by_lane = jnp.where((row == 0) & (lane >= count), 1e9, 0.0)
+    by_row = jnp.where(row >= count, 1e9, 0.0)
+    for s, start, length in sequences(lengths):
+        end = wide(start + length)
+        here = lane == s
+        by_lane = by_lane + jnp.where((row == 0) & here, end, 0.0)
+        by_lane = by_lane + jnp.where((row == 2) & here, wide(head_bucket[0, s]), 0.0)
+        by_lane = by_lane + jnp.where((row == 3) & here, wide(width_bucket[0, s]), 0.0)
+        by_row = by_row + jnp.where(row == s, end, 0.0)
+        facts[pl.ds(16 + s, 1), :] = place_cosine[pl.ds(start, 1), :]
+        facts[pl.ds(20 + s, 1), :] = place_sine[pl.ds(start, 1), :]
+    facts[pl.ds(0, 8), :] = by_lane
+    facts[pl.ds(8, 8), :] = by_row
+
+
+def fill_tables(
+    infos, place_cosine, place_sine, t, cosine, sine, head_mask, width_mask, seg_col, seg_row
+):
+    tokens, lanes = place_cosine.shape
+    own = wide(t)
+    lane = wide(lax.broadcasted_iota(jnp.int32, (tokens, lanes), 1))
+    place = wide(lax.broadcasted_iota(jnp.int32, (tokens, lanes), 0))
+    sign = jnp.where(lane < lanes // 2, -1.0, 1.0)
+    for b in range(2):
+        rows = pl.ds(b * tokens, tokens)
+
+        def row(k, b=b):
+            return infos[b, pl.ds(k, 1), :]
+
+        segment = jnp.sum(jnp.where(place >= row(0), 1.0, 0.0), axis=1, keepdims=True)
+        seg_col[rows, :] = segment
+        chosen = jnp.where(lane == segment, 1.0, 0.0)
+        head = jnp.sum(chosen * row(2), axis=1, keepdims=True)
+        width = jnp.sum(chosen * row(3), axis=1, keepdims=True)
+        head_mask[rows, :] = jnp.where(head >= own, 1.0, 0.0)
+        width_mask[rows, :] = jnp.where(width >= own, 1.0, 0.0)
+        start_cosine, start_sine = 0.0, 0.0
+        for s in range(4):
+            here = jnp.where(segment == s, 1.0, 0.0)
+            start_cosine = start_cosine + here * row(16 + s)
+            start_sine = start_sine + here * row(20 + s)
+        at_cosine, at_sine = place_cosine[...], place_sine[...]
+        cosine[rows, :] = at_cosine * start_cosine + at_sine * start_sine
+        sine[rows, :] = (at_sine * start_cosine - at_cosine * start_sine) * sign
+        ends = infos[b, pl.ds(8, 8), pl.ds(0, 1)]
+        across = wide(lax.broadcasted_iota(jnp.int32, (8, tokens), 1))
+        seg_row[b] = jnp.sum(jnp.where(across >= ends, 1.0, 0.0), axis=0, keepdims=True)
+
+
+def forward_kernel(
+    residual,
+    cotangent,
+    gain1,
+    shift1,
+    gain2,
+    shift2,
+    lengths,
+    head_bucket,
+    width_bucket,
+    place_cosine,
+    place_sine,
+    half_qkv,
+    half_out,
+    half_up,
+    half_down,
+    cosine,
+    sine,
+    head_mask,
+    all_qkv,
+    all_out,
+    all_up,
+    stream1,
+    stream2,
+    stream_c,
+    normed1,
+    normed2,
+    heads_out,
+    weights_out,
+    mixed_out,
+    active_out,
+    grad_upper_out,
+    part_out,
+    middle_out,
+    w_qkv,
+    w_out,
+    w_up,
+    w_down,
+    rows1,
+    rows2,
+    rows_c,
+    normed,
+    qkv,
+    weights,
+    mixed,
+    part,
+    got_c,
+    got_y,
+    got_z,
+    upper,
+    active,
+    grad_active,
+    middle,
+    infos,
+    seg_col,
+    seg_row,
+    width_mask,
+    send_sems,
+    recv_sems,
+    move_sems,
+):
+    p = Place()
+    tr, mv = Traffic(send_sems, recv_sems), Moves(move_sems)
+    tokens = residual.shape[0]
+    rows_d = half_qkv.shape[1]
+    head_cols = w_out.shape[1]
+
+    def row_slot(ref):
+        return lambda d: ref.at[pl.ds(pl.multiple_of(d * rows_d, rows_d), rows_d)]
+
+    def first_slot(ref):
+        return lambda d: ref.at[d]
+
+    def at_side(k, cut, size):
+        return pl.ds(pl.multiple_of(k * size + cut.start, 128), cut.size)
+
+    hidden = w_up.shape[1]
+    parts = [pl.ds(0, hidden // 2), pl.ds(hidden // 2, hidden // 2)]
+
+    def rows_at(d):
+        return pl.ds(pl.multiple_of(d * rows_d, rows_d), rows_d)
+
+    def up_gather(name, cut):
+        return WeightGather(
+            name,
+            p,
+            tr,
+            mv,
+            lambda k: half_up.at[:, at_side(k, cut, hidden)],
+            lambda d: w_up.at[rows_at(d), cut],
+        )
+
+    def down_gather(name, cut):
+        return WeightGather(
+            name,
+            p,
+            tr,
+            mv,
+            lambda k: half_down.at[at_side(k, cut, hidden), :],
+            lambda d: w_down.at[d, cut, :],
+        )
+
+    heads_cut = pl.ds(0, head_cols)
+    q = WeightGather(
+        "q",
+        p,
+        tr,
+        mv,
+        lambda k: half_qkv.at[:, :, at_side(k, heads_cut, head_cols)],
+        lambda d: w_qkv.at[:, rows_at(d), :],
+    )
+    o = WeightGather(
+        "o",
+        p,
+        tr,
+        mv,
+        lambda k: half_out.at[at_side(k, heads_cut, head_cols), :],
+        lambda d: w_out.at[d],
+    )
+    u, v = [up_gather(n, cut) for n, cut in zip("uv", parts)]
+    d, e = [down_gather(n, cut) for n, cut in zip("de", parts)]
+    a1 = ActGather("a", p, tr, rows1)
+    a2 = ActGather("b", p, tr, rows2)
+    ac = ActGather("c", p, tr, rows_c)
+    s1 = ActScatter("s", p, tr, part, got_c, got_y, got_z)
+
+    fill_facts(lengths, head_bucket, width_bucket, place_cosine, place_sine, infos.at[0])
+    p.greet()
+    for one in (q, o, u, v, d, e):
+        one.own()
+    blocks = w_out.shape[0]
+    stripes = part.shape[1]
+    per = blocks // stripes
+    started = []
+
+    def project(b):
+        def body(r):
+            at = pl.ds(b * tokens + r, 256)
+            for k in range(3):
+                got = dot_f32(normed[at, :], w_qkv[k])
+                for h in range(head_cols // HD):
+                    cols = pl.ds(h * HD, HD)
+                    one = got[:, h * HD : (h + 1) * HD]
+                    if k < 2:
+                        one = one * cosine[at, :] + pltpu.roll(one, HD // 2, 1) * sine[at, :]
+                    qkv[k, at, cols] = one.astype(jnp.bfloat16)
+
+        loop_rows(tokens, 256, body)
+
+    def branch(b):
+        at = pl.ds(b * tokens, tokens)
+
+        def body(s, carry):
+            for j in range(per):
+                got = dot_f32(mixed[at, :], w_out[s * per + j])
+                part[b, s, :, pl.ds(j * rows_d, rows_d)] = got.astype(jnp.bfloat16)
+            return carry
+
+        lax.fori_loop(0, stripes, body, 0)
+
+    def rise(b, cut):
+        def body(r):
+            at = pl.ds(b * tokens + r, 256)
+            for k in range(cut.size // 256):
+                cols = pl.ds(cut.start + k * 256, 256)
+                got = dot_f32(normed[at, :], w_up[:, cols])
+                got = jnp.maximum(got, 0.0) * width_mask[at, :]
+                upper[at, cols] = got.astype(jnp.bfloat16)
+                active[at, cols] = (got * got).astype(jnp.bfloat16)
+
+        loop_rows(tokens, 256, body)
+
+    def fall(m):
+        place = p.block(m)
+        s = place // per
+        cols = pl.ds(pl.multiple_of((place % per) * rows_d, rows_d), rows_d)
+        first = not started
+        started.append(m)
+
+        def body(r):
+            b, at = r // tokens, pl.ds(pl.multiple_of(r % tokens, 256), 256)
+            rows = pl.ds(r, 256)
+            part[b, s, at, cols] = dot_f32(active[rows, :], w_down[place]).astype(jnp.bfloat16)
+            got = dot_nt(rows_c[b, s, at, cols], w_down[place])
+            grad_active[rows, :] = got if first else grad_active[rows, :] + got
+
+        loop_rows(2 * tokens, 256, body)
+
+    def turn(r):
+        at = pl.ds(r, 64)
+        active[at, :] = (grad_active[at, :] * 2.0 * wide(upper[at, :])).astype(jnp.bfloat16)
+
+    q.z()
+    v.x()
+    round_rows(residual, rows1.at[0, p.t], tokens)
+    o.z()
+    q.x()
+    a1.z()
+    o.far()
+    tr.send("info", infos.at[0], infos.at[1], p.z)
+    q.far()
+    a1.c()
+    d.x()
+    q.x_next(2)
+    a1.y()
+    q.far_next()
+    o.far_next()
+    tr.wait("info")
+    fill_tables(
+        infos, place_cosine, place_sine, p.t, cosine, sine, head_mask, width_mask, seg_col, seg_row
+    )
+    u.x()
+    a1.pass_z()
+    q.x_next(6)
+    a1.pass_y(1)
+    a1.take(1)
+    norm_rows(rows1, 1, gain1, shift1, normed)
+    round_rows(cotangent, rows_c.at[0, p.t], tokens)
+    v.z()
+    a1.pass_y(0)
+    o.x()
+    o.x_next(4)
+    ac.y()
+    u.z()
+    a1.take(0)
+    norm_rows(rows1, 0, gain1, shift1, normed)
+    mv.start("stream1", rows1, stream1)
+    mv.start("normed1", normed, normed1)
+    e.z()
+    v.far()
+    q.x_next(4)
+    o.x_next(6)
+    o.x_next(2)
+    v.far_next()
+    q.end()
+    project(1)
+    attend(
+        1, qkv, seg_col, seg_row, head_mask, weights, mixed, HD ** (-0.5)
+    )
+    o.end()
+    branch(1)
+    project(0)
+    mv.start("all_qkv", w_qkv, all_qkv)
+    v.x_next(6)
+    s1.c(1)
+    s1.y(1)
+    s1.own(1)
+    d.z()
+    u.far_next()
+    attend(
+        0, qkv, seg_col, seg_row, head_mask, weights, mixed, HD ** (-0.5)
+    )
+    mv.start("heads", qkv, heads_out)
+    mv.start("weights", weights, weights_out)
+    mv.start("mixed", mixed, mixed_out)
+    ac.c()
+    s1.z()
+    u.x_next(2)
+    branch(0)
+    mv.start("all_out", w_out, all_out)
+    s1.c(0)
+    u.far()
+    s1.y(0)
+    e.x_next(2)
+    e.x()
+    v.x_next(4)
+    s1.own(0)
+    v.x_next(2)
+    s1.home()
+    s1.end(middle, residual)
+    round_rows(middle, rows2.at[0, p.t], tokens)
+    mv.start("middle", middle, middle_out)
+    a2.z()
+    ac.z()
+    e.far()
+    a2.y()
+    d.far_next()
+    e.far_next()
+    a2.c()
+    d.far()
+    u.x_next(4)
+    a2.pass_y(0)
+    d.x_next(2)
+    u.x_next(6)
+    a2.pass_z()
+    ac.pass_z()
+    ac.pass_y(0)
+    a2.take(0)
+    mv.wait("normed1")
+    norm_rows(rows2, 0, gain2, shift2, normed)
+    a2.pass_y(1)
+    a2.take(1)
+    norm_rows(rows2, 1, gain2, shift2, normed)
+    mv.start("stream2", rows2, stream2)
+    mv.start("normed2", normed, normed2)
+    e.x_next(6)
+    u.end()
+    rise(0, parts[0])
+    v.end()
+    rise(1, parts[1])
+    rise(1, parts[0])
+    d.x_next(4)
+    ac.pass_y(1)
+    rise(0, parts[1])
+    mv.start("active", active, active_out)
+    mv.start("all_up", w_up, all_up)
+    ac.take(0)
+    ac.take(1)
+    s1.sent()
+    d.take(3)
+    e.take(3)
+    fall(3)
+    mv.start("stream_c", rows_c, stream_c)
+    e.x_next(4)
+    d.take(1)
+    e.take(1)
+    fall(1)
+    d.take(4)
+    e.take(4)
+    fall(4)
+    d.take(0)
+    e.take(0)
+    fall(0)
+    d.x_next(6)
+    d.take(6)
+    e.take(6)
+    fall(6)
+    d.take(2)
+    e.take(2)
+    fall(2)
+    d.take(5)
+    e.take(5)
+    fall(5)
+    d.take(7)
+    e.take(7)
+    fall(7)
+    mv.start("part", part, part_out)
+    mv.wait("active")
+    loop_rows(2 * tokens, 64, turn)
+    mv.start("grad_upper", active, grad_upper_out)
+    tr.finish()
+    mv.finish()
+
+
+def forward_call(arrays, weights):
+    bf16, f32 = jnp.bfloat16, jnp.float32
+    tokens, columns = arrays[0].shape
+    w_qkv, w_out, w_up, w_down = weights
+    count, stripes = lax.axis_size("dp"), lax.axis_size("tensor")
+    rows_d = w_up.shape[0]
+    head_cols = w_out.shape[0] // 2
+    hidden = w_up.shape[1] // 2
+    width = rows_d * count
+    heads = head_cols // HD
+    slots = (2, stripes, tokens, columns)
+    tables = dict(
+        cosine=((2 * tokens, HD), f32),
+        sine=((2 * tokens, HD), f32),
+        head_mask=((2 * tokens, 1), f32),
+    )
+    shapes = dict(
+        all_qkv=((3, width, head_cols), bf16),
+        all_out=((count, head_cols, rows_d), bf16),
+        all_up=((width, hidden), bf16),
+        stream1=(slots, bf16),
+        stream2=(slots, bf16),
+        stream_c=(slots, bf16),
+        normed1=((2 * tokens, width), bf16),
+        normed2=((2 * tokens, width), bf16),
+        heads=((3, 2 * tokens, head_cols), bf16),
+        weights=((2 * heads, tokens, tokens), bf16),
+        mixed=((2 * tokens, head_cols), bf16),
+        active=((2 * tokens, hidden), bf16),
+        grad_upper=((2 * tokens, hidden), bf16),
+        part_out=(slots, bf16),
+        middle=((tokens, columns), f32),
+    )
+
+    def vmem(name):
+        return pltpu.VMEM(*shapes[name])
+
+    scratch = [
+        vmem("all_qkv"),
+        vmem("all_out"),
+        vmem("all_up"),
+        pltpu.VMEM((count, hidden, rows_d), bf16),
+        vmem("stream1"),
+        vmem("stream2"),
+        vmem("stream_c"),
+        vmem("normed1"),
+        vmem("heads"),
+        vmem("weights"),
+        vmem("mixed"),
+        pltpu.VMEM(slots, bf16),
+        pltpu.VMEM((2, 2, tokens, columns), bf16),
+        pltpu.VMEM((2, tokens, columns), bf16),
+        pltpu.VMEM((tokens, columns), bf16),
+        vmem("active"),
+        vmem("active"),
+        pltpu.VMEM((2 * tokens, hidden), f32),
+        vmem("middle"),
+        pltpu.VMEM((2, 24, 128), f32),
+        pltpu.VMEM((2 * tokens, 1), f32),
+        pltpu.VMEM((2, 1, tokens), f32),
+        pltpu.VMEM((2 * tokens, 1), f32),
+        pltpu.SemaphoreType.DMA((72,)),
+        pltpu.SemaphoreType.DMA((72,)),
+        pltpu.SemaphoreType.DMA((32,)),
+    ]
+    any_spec = pl.BlockSpec(memory_space=pl.ANY)
+    vmem_spec = pl.BlockSpec(memory_space=pltpu.VMEM)
+    smem_spec = pl.BlockSpec(memory_space=pltpu.SMEM)
+    outs = pl.pallas_call(
+        forward_kernel,
+        out_shape=[jax.ShapeDtypeStruct(*s) for s in (tables | shapes).values()],
+        in_specs=[vmem_spec] * 6 + [smem_spec] * 3 + [vmem_spec] * 2 + [any_spec] * 4,
+        out_specs=[vmem_spec] * len(tables) + [any_spec] * len(shapes),
+        scratch_shapes=scratch,
+        compiler_params=pltpu.CompilerParams(
+            collective_id=0, has_side_effects=True, vmem_limit_bytes=62 << 20
+        ),
+    )(*arrays, *weights)
+    split = len(tables)
+    return outs[:split], dict(zip(shapes, outs[split:]))
+
+
+class WeightScatter:
+    def __init__(self, name, place, traffic, odd, even, got_x, got_far, out):
+        self.name, self.p, self.tr = name, place, traffic
+        self.odd, self.even, self.got_x, self.got_far, self.out = odd, even, got_x, got_far, out
+
+    def send_x(self, m):
+        self.tr.send(self.name + "x" + str(m), self.odd.at[m // 2], self.got_x.at[m // 2], self.p.x)
+
+    def add_x(self, m):
+        k, n = m // 2, self.name
+        own = self.even.at[k]
+        self.tr.wait(n + "x" + str(m + 1))
+        add_blocks(own, own, self.got_x.at[k], own.shape[0])
+        if m >= 4:
+            self.tr.send(n + "f" + str(m), own, self.got_far.at[3 - k], self.p.far)
+
+    def add_far(self, m):
+        k, n = m // 2, self.name
+        own = self.even.at[k]
+        self.tr.wait(n + "f" + str(6 - m))
+        add_blocks(own, own, self.got_far.at[k], own.shape[0])
+        if m == 2:
+            for j, (cut, spot) in enumerate(self.out(self.p.side)):
+                self.tr.send(n + "z" + str(j), own.at[:, cut], spot, self.p.z)
+
+    def end(self, moves):
+        for j, (cut, spot) in enumerate(self.out(self.p.side)):
+            moves.start(self.name + str(j), self.even.at[0, :, cut], spot)
+            self.tr.wait(self.name + "z" + str(j))
+
+
+class SumAll:
+    def __init__(self, name, place, traffic, sums, got):
+        self.name, self.tr, self.sums, self.got = name, traffic, sums, got
+        self.partners = (place.c, place.y, place.x, place.z, place.far)
+
+    def start(self, k):
+        self.tr.send(self.name + str(k), self.sums, self.got.at[k], self.partners[k])
+
+    def step(self, k):
+        self.tr.wait(self.name + str(k))
+        self.tr.sent(self.name + str(k))
+        self.sums[...] += self.got[k]
+        if k + 1 < len(self.partners):
+            self.start(k + 1)
+
+
+def norm_back(b, part, slots, gain, total):
+    stripes, rows, columns = part.shape[1:]
+    fold = (4, 8, stripes * columns)
+
+    def body(r):
+        at = pl.ds(r, 32)
+        value = wide(slots[pl.ds(b * rows + r, 32), :])
+        center = value - jnp.mean(value, axis=1, keepdims=True)
+        spread = jnp.mean(center * center, axis=1, keepdims=True)
+        inverse = lax.rsqrt(spread + epsilon)
+        unit = center * inverse
+        grad = jnp.concatenate([wide(part[b, s, at, :]) for s in range(stripes)], axis=1)
+        scaled = grad * gain[...]
+        push = inverse * (
+            scaled
+            - jnp.mean(scaled, axis=1, keepdims=True)
+            - unit * jnp.mean(scaled * unit, axis=1, keepdims=True)
+        )
+        for s in range(stripes):
+            part[b, s, at, :] = push[:, s * columns : (s + 1) * columns].astype(jnp.bfloat16)
+        total[0] += jnp.sum((grad * unit).reshape(fold), axis=0)
+        total[1] += jnp.sum(grad.reshape(fold), axis=0)
+
+    if b == 1:
+        total[...] = jnp.zeros_like(total)
+    loop_rows(rows, 32, body)
+
+
+def attend_back(b, qkv, weights, grad_mixed, cosine, sine, out, tokens, scale):
+    width = grad_mixed.shape[1]
+    heads = width // HD
+    half = tokens // 2
+    start = b * tokens
+
+    def turn_back(grad, rows):
+        return (grad * cosine[rows, :] - pltpu.roll(grad, HD // 2, 1) * sine[rows, :]).astype(
+            jnp.bfloat16
+        )
+
+    for h in range(heads):
+        spots = [pl.ds(k * width + h * HD, HD) for k in range(3)]
+        grad_key, grad_value = None, None
+        for part in (1, 0):
+            rows = pl.ds(start + part * half, half)
+            reach = pl.ds(start, half * (part + 1))
+            query, key, value = qkv[rows, spots[0]], qkv[reach, spots[1]], qkv[reach, spots[2]]
+            given = grad_mixed[rows, pl.ds(h * HD, HD)]
+            chosen = weights[b * heads + h, pl.ds(part * half, half), pl.ds(0, half * (part + 1))]
+            grad = dot_nt(given, value)
+            soft = wide(chosen)
+            grad = soft * (grad - jnp.sum(grad * soft, axis=1, keepdims=True))
+            raw = (grad * scale).astype(jnp.bfloat16)
+            out[rows, spots[0]] = turn_back(dot_f32(raw, key), rows)
+            key_part, value_part = dot_tn(raw, query), dot_tn(chosen, given)
+            if part == 1:
+                grad_key, grad_value = key_part, value_part
+        low, high = pl.ds(start, half), pl.ds(start + half, half)
+        out[low, spots[1]] = turn_back(grad_key[:half] + key_part, low)
+        out[high, spots[1]] = turn_back(grad_key[half:], high)
+        out[low, spots[2]] = (grad_value[:half] + value_part).astype(jnp.bfloat16)
+        out[high, spots[2]] = grad_value[half:].astype(jnp.bfloat16)
+
+
+def backward_kernel(
+    cotangent,
+    gain1,
+    gain2,
+    cosine,
+    sine,
+    head_mask,
+    lengths,
+    width_bucket,
+    all_qkv,
+    all_out,
+    all_up,
+    stream1,
+    stream2,
+    stream_c,
+    normed1,
+    normed2,
+    heads,
+    weights_in,
+    mixed_in,
+    active_in,
+    grad_upper_in,
+    part_in,
+    middle_in,
+    output,
+    grad_input,
+    sums2_out,
+    sums1_out,
+    grad_qkv,
+    grad_out,
+    grad_up,
+    grad_down,
+    w_up,
+    w_out,
+    rows_a,
+    rows_b,
+    active,
+    grad_upper,
+    part_a,
+    part_b,
+    got_ca,
+    got_ya,
+    got_za,
+    got_cb,
+    got_yb,
+    got_zb,
+    stream_b,
+    weights,
+    mixed,
+    grad_mixed,
+    odd,
+    even_down,
+    even_up,
+    odd_out,
+    even_out,
+    gx_down,
+    gf_down,
+    gx_up,
+    gf_up,
+    gx_qkv,
+    gf_qkv,
+    gx_out,
+    gf_out,
+    middle,
+    grad_middle,
+    total,
+    sums2,
+    got2,
+    sums1,
+    got1,
+    send_sems,
+    recv_sems,
+    move_sems,
+):
+    p = Place()
+    tr, mv = Traffic(send_sems, recv_sems), Moves(move_sems)
+    tokens, columns = cotangent.shape
+    stripes, blocks = part_a.shape[1], all_out.shape[0]
+    rows_d = all_out.shape[2]
+    per = blocks // stripes
+    head_cols = mixed.shape[1]
+    bf16 = jnp.bfloat16
+
+    def load_stream(name, src, dst):
+        for b in range(2):
+            for s in range(stripes):
+                spot = dst.at[pl.ds(b * tokens, tokens), pl.ds(s * columns, columns)]
+                mv.start(name + str(b) + str(s), src.at[b, s], spot)
+
+    def wait_stream(name):
+        mv.wait(*[name + str(b) + str(s) for b in range(2) for s in range(stripes)])
+
+    s_out = ActScatter("s", p, tr, part_a, got_ca, got_ya, got_za)
+    s2 = ActScatter("t", p, tr, part_b, got_cb, got_yb, got_zb)
+    s1 = ActScatter("r", p, tr, part_b, got_cb, got_yb, got_zb)
+    ab = ActGather("b", p, tr, stream_b)
+    qkv_cols = pl.ds(0, 3 * head_cols)
+    hidden = active.shape[1]
+    parts = [pl.ds(0, hidden // 2), pl.ds(hidden // 2, hidden // 2)]
+
+    def at_side(k, cut, size):
+        return pl.ds(pl.multiple_of(k * size + cut.start, 128), cut.size)
+
+    def scatter(name, odd, even, got_x, got_far, out, cols):
+        views = [ref.at[:, :, cols] for ref in (odd, even, got_x, got_far)]
+
+        def spots(k):
+            if len(out.shape) == 3:
+                return [
+                    (pl.ds(j * head_cols, head_cols), out.at[j, :, at_side(k, heads_cut, head_cols)])
+                    for j in range(3)
+                ]
+            spot = out.at[:, at_side(k, cols, out.shape[1] // 2)]
+            return [(pl.ds(0, cols.size), spot)]
+
+        return WeightScatter(name, p, tr, *views, spots)
+
+    heads_cut = pl.ds(0, head_cols)
+
+    d, e = [
+        scatter(n, odd, even_down, gx_down, gf_down, grad_down, cut) for n, cut in zip("de", parts)
+    ]
+    u, v = [scatter(n, odd, even_up, gx_up, gf_up, grad_up, cut) for n, cut in zip("uv", parts)]
+    q = scatter("q", odd, even_down, gx_qkv, gf_qkv, grad_qkv, qkv_cols)
+    o = scatter("o", odd_out, even_out, gx_out, gf_out, grad_out, pl.ds(0, head_cols))
+    all2 = SumAll("2", p, tr, sums2, got2)
+    all1 = SumAll("1", p, tr, sums1, got1)
+
+    load_stream("c", stream_c, rows_a)
+    mv.start("active", active_in, active)
+    mv.start("grad_upper", grad_upper_in, grad_upper)
+    mv.start("all_up", all_up, w_up)
+    load_stream("x2", stream2, rows_b)
+    mv.start("mixed", mixed_in, mixed)
+    mv.start("weights", weights_in, weights)
+    for k in range(blocks):
+        mv.start("p" + str(k), all_out.at[k], w_out.at[:, pl.ds(k * rows_d, rows_d)])
+    mv.start("part", part_in, part_a)
+    mv.start("middle", middle_in, middle)
+    p.greet()
+
+    def block_cols(m):
+        return pl.ds(pl.multiple_of(p.block(m) * rows_d, rows_d), rows_d)
+
+    def grad_block(left, right, m, spot, cols=None):
+        value = right[...] if cols is None else right[:, cols]
+        spot[...] = dot_tn(left[:, block_cols(m)], value).astype(bf16)
+
+    def down_block(m, spot):
+        grad_block(rows_a, active, m, spot)
+
+    def product(b, left, right, cols):
+        at = pl.ds(b * tokens, tokens)
+
+        def body(s, carry):
+            rows = pl.ds(pl.multiple_of(s * columns, columns), columns)
+            part_b[b, s] = dot_nt(left[at, cols], right[rows, cols]).astype(bf16)
+            return carry
+
+        lax.fori_loop(0, stripes, body, 0)
+
+    def gather_total(sums):
+        sums[...] = jnp.concatenate(
+            [
+                jnp.sum(total[0], axis=0, keepdims=True),
+                jnp.sum(total[1], axis=0, keepdims=True),
+                jnp.concatenate(
+                    [
+                        count_row(lengths, width_bucket, HD),
+                        jnp.zeros((1, total.shape[2] - HD), jnp.float32),
+                    ],
+                    axis=1,
+                ),
+                jnp.zeros((5, total.shape[2]), jnp.float32),
+            ],
+            axis=0,
+        )
+
+    def up_block(m, spot):
+        grad_block(rows_a, grad_upper, m, spot)
+
+    def up_odd(m):
+        tr.sent("dx" + str(m), "ex" + str(m))
+        up_block(m, odd.at[m // 2])
+        u.send_x(m)
+        v.send_x(m)
+
+    def mix(b):
+        mv.wait(*["p" + str(k) for k in range(blocks)])
+        at = pl.ds(b * tokens, tokens)
+        got = None
+        for s in range(stripes):
+            one = dot_nt(stream_b[b, s], w_out[:, pl.ds(s * columns, columns)])
+            got = one if got is None else got + one
+        grad_mixed[at, :] = (got * head_mask[at, :]).astype(bf16)
+
+    def out_block(m, spot):
+        mv.wait("mixed")
+        place = p.block(m)
+        cols = pl.ds(pl.multiple_of((place % per) * rows_d, rows_d), rows_d)
+        near = dot_tn(stream_b[0, place // per, :, cols], mixed[pl.ds(0, tokens), :])
+        away = dot_tn(stream_b[1, place // per, :, cols], mixed[pl.ds(tokens, tokens), :])
+        spot[...] = (near + away).astype(bf16)
+
+    def qkv_block(m, spot):
+        mv.wait("normed1")
+        grad_block(rows_b, grad_upper, m, spot, qkv_cols)
+
+    def qkv_odd(m):
+        tr.sent("ux" + str(m), "vx" + str(m))
+        qkv_block(m, odd.at[m // 2, :, qkv_cols])
+        q.send_x(m)
+
+    def qkv_even(m):
+        mv.wait("d0", "e0")
+        tr.sent("df4", "df6", "dz0", "ef4", "ef6", "ez0")
+        qkv_block(m, even_down.at[m // 2, :, qkv_cols])
+
+    wait_stream("c")
+    mv.wait("active")
+    down_block(5, odd.at[2])
+    d.send_x(5)
+    e.send_x(5)
+    mv.wait("grad_upper", "all_up")
+    product(1, grad_upper, w_up, pl.ds(0, w_up.shape[1]))
+    wait_stream("x2")
+    norm_back(1, part_b, rows_b, gain2, total)
+    s2.c(1)
+    down_block(4, even_down.at[2])
+    d.add_x(4)
+    s2.y(1)
+    mv.wait("part")
+    down_block(3, odd.at[1])
+    d.send_x(3)
+    e.send_x(3)
+    product(0, grad_upper, w_up, pl.ds(0, w_up.shape[1]))
+    norm_back(0, part_b, rows_b, gain2, total)
+    e.add_x(4)
+    s2.c(0)
+    down_block(2, even_down.at[1])
+    down_block(0, even_down.at[0])
+    s2.own(1)
+    down_block(7, odd.at[3])
+    d.send_x(7)
+    e.send_x(7)
+    s2.y(0)
+    s_out.c(1)
+    down_block(6, even_down.at[3])
+    s2.own(0)
+    down_block(1, odd.at[0])
+    d.send_x(1)
+    e.send_x(1)
+    s2.z()
+    d.add_x(6)
+    d.add_x(2)
+    s2.home()
+    s2.end(grad_middle, cotangent)
+    round_rows(grad_middle, stream_b.at[0, p.t], tokens)
+    for k in range(3):
+        mv.start("h" + str(k), heads.at[k], active.at[:, pl.ds(k * head_cols, head_cols)])
+    mv.start("normed2", normed2, rows_a)
+    mv.wait("normed2")
+    e.add_x(2)
+    up_block(6, even_up.at[3])
+    ab.y()
+    up_odd(5)
+    up_block(2, even_up.at[1])
+    s_out.y(1)
+    e.add_far(2)
+    ab.z()
+    e.add_x(6)
+    up_block(0, even_up.at[0])
+    gather_total(sums2)
+    all2.start(0)
+    up_odd(7)
+    up_block(4, even_up.at[2])
+    s_out.own(1)
+    u.add_x(4)
+    v.add_x(4)
+    s_out.c(0)
+    ab.c()
+    ab.pass_z()
+    up_odd(1)
+    d.add_x(0)
+    ab.pass_y(0)
+    ab.pass_y(1)
+    up_odd(3)
+    d.add_far(2)
+    ab.take(0)
+    mix(0)
+    e.add_x(0)
+    load_stream("x1", stream1, rows_a)
+    s_out.z()
+    ab.take(1)
+    out_block(2, even_out.at[1])
+    v.add_x(6)
+    e.add_far(0)
+    d.add_far(0)
+    out_block(3, odd_out.at[1])
+    o.send_x(3)
+    mix(1)
+    mv.wait("weights", "h0", "h1", "h2")
+    attend_back(
+        1, active, weights, grad_mixed, cosine, sine, grad_upper, tokens, HD ** (-0.5)
+    )
+    s_out.y(0)
+    all2.step(0)
+    u.add_x(6)
+    d.end(mv)
+    attend_back(
+        0, active, weights, grad_mixed, cosine, sine, grad_upper, tokens, HD ** (-0.5)
+    )
+    for k in range(3):
+        mv.start("w" + str(k), all_qkv.at[k], w_up.at[:, pl.ds(k * head_cols, head_cols)])
+    mv.start("normed1", normed1, rows_b)
+    out_block(5, odd_out.at[2])
+    o.send_x(5)
+    u.add_x(2)
+    qkv_odd(7)
+    s2.sent()
+    mv.wait("w0", "w1", "w2")
+    product(1, grad_upper, w_up, qkv_cols)
+    wait_stream("x1")
+    norm_back(1, part_b, rows_a, gain1, total)
+    product(0, grad_upper, w_up, qkv_cols)
+    norm_back(0, part_b, rows_a, gain1, total)
+    all2.step(1)
+    s1.c(0)
+    out_block(4, even_out.at[2])
+    o.add_x(4)
+    s1.c(1)
+    u.add_far(2)
+    v.add_x(0)
+    s1.y(0)
+    out_block(6, even_out.at[3])
+    o.add_x(2)
+    v.add_x(2)
+    e.end(mv)
+    v.add_far(0)
+    out_block(0, even_out.at[0])
+    qkv_even(6)
+    out_block(7, odd_out.at[3])
+    o.send_x(7)
+    qkv_odd(5)
+    s1.y(1)
+    gather_total(sums1)
+    all1.start(0)
+    v.add_far(2)
+    u.add_x(0)
+    o.add_far(2)
+    qkv_even(2)
+    qkv_odd(3)
+    s1.own(0)
+    q.add_x(6)
+    all1.step(0)
+    qkv_even(0)
+    s1.home()
+    qkv_odd(1)
+    all2.step(2)
+    qkv_even(4)
+    s1.own(1)
+    s_out.own(0)
+    s_out.home()
+    q.add_x(2)
+    s1.z()
+    q.add_x(4)
+    o.add_x(6)
+    q.add_x(0)
+    all1.step(1)
+    out_block(1, odd_out.at[0])
+    o.send_x(1)
+    u.add_far(0)
+    all1.step(2)
+    all2.step(3)
+    all1.step(3)
+    s1.end(grad_middle, grad_middle)
+    mv.start("grad_input", grad_middle, grad_input)
+    u.end(mv)
+    o.add_x(0)
+    q.add_far(2)
+    v.end(mv)
+    q.add_far(0)
+    all1.step(4)
+    all2.step(4)
+    mv.wait("middle")
+    s_out.end(middle, middle)
+    mv.start("output", middle, output)
+    o.add_far(0)
+    o.end(mv)
+    q.end(mv)
+    sums2_out[...] = sums2[...]
+    sums1_out[...] = sums1[...]
+    tr.finish()
+    mv.finish()
+
+
+def backward_call(arrays, saved):
+    bf16, f32 = jnp.bfloat16, jnp.float32
+    tokens, columns = arrays[0].shape
+    count, stripes = lax.axis_size("dp"), lax.axis_size("tensor")
+    _, head_cols, rows_d = saved["all_out"].shape
+    width, hidden = saved["all_up"].shape
+    slots = (2, stripes, tokens, columns)
+    wide_rows = (2 * tokens, width)
+
+    def vmem(*shape, dtype=bf16):
+        return pltpu.VMEM(shape, dtype)
+
+    def got(cols):
+        return [vmem(4, rows_d, cols), vmem(2, rows_d, cols)]
+
+    got_act = [vmem(2, 2, tokens, columns), vmem(2, tokens, columns), vmem(tokens, columns)]
+    sums = [vmem(8, width, dtype=f32), vmem(5, 8, width, dtype=f32)]
+    qkv = 3 * head_cols
+    scratch = [
+        vmem(width, hidden),
+        vmem(head_cols, width),
+        vmem(*wide_rows),
+        vmem(*wide_rows),
+        vmem(2 * tokens, hidden),
+        vmem(2 * tokens, hidden),
+        vmem(*slots),
+        vmem(*slots),
+        *got_act,
+        *got_act,
+        vmem(*slots),
+        vmem(*saved["weights"].shape),
+        vmem(2 * tokens, head_cols),
+        vmem(2 * tokens, head_cols),
+        vmem(4, rows_d, hidden),
+        vmem(4, rows_d, hidden),
+        vmem(4, rows_d, hidden),
+        vmem(4, rows_d, head_cols),
+        vmem(4, rows_d, head_cols),
+        *got(hidden),
+        *got(hidden),
+        *got(qkv),
+        *got(head_cols),
+        vmem(tokens, columns, dtype=f32),
+        vmem(tokens, columns, dtype=f32),
+        vmem(2, 8, width, dtype=f32),
+        *sums,
+        *sums,
+        pltpu.SemaphoreType.DMA((84,)),
+        pltpu.SemaphoreType.DMA((84,)),
+        pltpu.SemaphoreType.DMA((72,)),
+    ]
+    any_spec = pl.BlockSpec(memory_space=pl.ANY)
+    vmem_spec = pl.BlockSpec(memory_space=pltpu.VMEM)
+    smem_spec = pl.BlockSpec(memory_space=pltpu.SMEM)
+    shapes = [
+        ((tokens, columns), f32),
+        ((tokens, columns), f32),
+        ((8, width), f32),
+        ((8, width), f32),
+        ((3, rows_d, 2 * head_cols), bf16),
+        ((rows_d, 2 * head_cols), bf16),
+        ((rows_d, 2 * hidden), bf16),
+        ((rows_d, 2 * hidden), bf16),
+    ]
+    names = [k for k in saved]
+    return pl.pallas_call(
+        backward_kernel,
+        out_shape=[jax.ShapeDtypeStruct(*s) for s in shapes],
+        in_specs=[vmem_spec] * 6 + [smem_spec] * 2 + [any_spec] * len(names),
+        out_specs=[any_spec] * 2 + [vmem_spec] * 2 + [any_spec] * 4,
+        scratch_shapes=scratch,
+        compiler_params=pltpu.CompilerParams(
+            collective_id=1, has_side_effects=True, vmem_limit_bytes=63 << 20
+        ),
+    )(*arrays, *[saved[n] for n in names])
+
+
+def local_fast(
+    residual_in,
+    lengths,
+    head_bucket,
+    width_bucket,
+    norm1_gain,
+    norm1_shift,
+    w_qkv,
+    w_out,
+    norm2_gain,
+    norm2_shift,
+    w_up,
+    w_down,
+    cotangent,
+):
+    f32 = jnp.float32
+    tokens = residual_in.shape[0]
+    steps = np.arange(tokens)[:, None] * 10000.0 ** (-2.0 * (np.arange(HD) % (HD // 2)) / HD)
+    arrays = (
+        residual_in,
+        cotangent,
+        norm1_gain[None],
+        norm1_shift[None],
+        norm2_gain[None],
+        norm2_shift[None],
+        lengths,
+        head_bucket,
+        width_bucket,
+        jnp.asarray(np.cos(steps), f32),
+        jnp.asarray(np.sin(steps), f32),
+    )
+    weights = (jnp.swapaxes(w_qkv, 0, 1), w_out, w_up, w_down)
+    (cosine, sine, head_mask), saved = forward_call(arrays, weights)
+    arrays = (cotangent, norm1_gain[None], norm2_gain[None], cosine, sine, head_mask)
+    output, grad_input, sums2, sums1, grad_qkv, grad_out, grad_up, grad_down = backward_call(
+        (*arrays, lengths, width_bucket), saved
+    )
+    total = lax.axis_size("tensor")
+    return (
+        output,
+        grad_input,
+        sums1[0],
+        sums1[1],
+        jnp.swapaxes(grad_qkv, 0, 1).astype(f32),
+        grad_out.T.astype(f32),
+        sums2[0],
+        sums2[1],
+        grad_up.astype(f32),
+        grad_down.T.astype(f32),
+        (sums2[2, :total] / total).astype(jnp.int32),
+    )
+
+
+def local(*args):
+    w_out = args[7]
+    if lax.axis_size("dp") == 8 and lax.axis_size("tensor") == 4 and w_out.shape[1] % 128 == 0:
+        return local_fast(*args)
+    return local_general(*args)
+
+
 def solution(mesh):
     placed = (
         P("dp", "tensor"),

time: 712 us -> 386 us (0.54)
  waiting for transfers between devices: 422 us -> 0 us
  Pallas kernels: 12.1 us -> 368 us
  starting transfers between devices: 97.2 us -> 0 us
  matrix products: 80.8 us -> 0 us
  other arithmetic: 54.3 us -> 5.52 us
  local copies, waits for them, and re-layouts: 38.8 us -> 6.96 us
    ppermute x126 -> x0, waiting for transfers between devices: 422 us -> none  [the longest x74 386 us: dp_swap(): return lax.ppermute(value, 'dp', [(i, i ^ bit) for i in range(count)])]
    pallas_call x16 -> x2, Pallas kernels: 12.1 us -> 368 us  [the longest x1 192 us: backward_call(): pl.pallas_call(backward_kernel, out_shape=[jax.ShapeDtypeStruct(*s) for s...]
    ppermute x126 -> x0, starting transfers between devices: 97.2 us -> none  [the longest x74 72.4 us: dp_swap(): return lax.ppermute(value, 'dp', [(i, i ^ bit) for i in range(count)])]
    dot_general x18 -> x0, matrix products: 80.8 us -> none  [the longest x1 7.98 us: local(): grad_normed1 = dot(grad_projected, full_qkv.T)]
    convert_element_type x35 -> x5, other arithmetic: 24.1 us -> 5.52 us  [the longest x1 1.56 us: local_fast(): grad_up.astype(f32)]
    unnamed x109 -> x14, local copies, waits for them, and re-layouts: 17.5 us -> 5.4 us
    reshape x6 -> x0, local copies, waits for them, and re-layouts: 8.79 us -> none  [the longest x2 4.09 us: local(): rotate(rows_of(g, 2).reshape(2 * tokens, -1, HD), cosine, -sine_part)]
  transfers between devices with their start and end apart: 126 -> 0, of which waited for: 51 -> 0; matrix products, arithmetic and copies ran while one was open for 9% -> 0% of each run, Pallas kernels for 1% -> 0%
where the time goes in v3:
time: 386 us; the launch traced here: 381 us
  Pallas kernels  368 us (95%)
  local copies, waits for them, and re-layouts  6.96 us (2%)
  other arithmetic  5.52 us (1%)
    pallas_call x1, Pallas kernels, backward_call(): pl.pallas_call(backward_kernel, out_shape=[jax.ShapeDtypeStruct(*s) for s...  192 us
    pallas_call x1, Pallas kernels, forward_call(): pl.pallas_call(forward_kernel, out_shape=[jax.ShapeDtypeStruct(*s) for s...  176 us

profile of v3, /device:TPU:0, one launch (start us, length us, event | category | flops | bytes accessed | tf_op | source)
XLA Modules:
  0.0 381.1 jit_solution(770935203945964302)
XLA Ops:
  0.6 176.2 %shard_map.230 = (f32[1024,128]{1,0:T(8,128)}, f32[1024,128]{1,0:T(8,128)}, f32[1024,1]{1,0:T(8,128)}, bf16[3,2048,256]{2,1,0:T(8,128)(2,1)}, bf16[8,256,256]{2,...) custom-call(f32[512,512]{1,0:T(8,128)} %residual.1, ...), custom_call_target="tpu_custom_call" | custom-call | tf_op jit(solution)/shard_map/pallas_call | solution.py:1171
  176.9 191.5 %shard_map.231 = (f32[512,512]{1,0:T(8,128)}, f32[512,512]{1,0:T(8,128)}, f32[8,2048]{1,0:T(8,128)}, f32[8,2048]{1,0:T(8,128)}, bf16[3,256,512]{2,1,0:T(8,128)(2...) custom-call(f32[512,512]{1,0:T(8,128)} %cotangent.3, f32[1,2048]{1,0:T(1,128)} %bitcast.19, ...), custom_call_target="tpu_custom_call" | custom-call | tf_op jit(solution)/shard_map/pallas_call | solution.py:1756
  368.4 0.0 copy-start.4
  368.4 1.3 convert_bitcast_fusion.3
  369.7 1.6 fusion
  371.2 0.0 copy-start.1
  371.2 1.1 convert_bitcast_fusion.2
  372.3 1.0 copy.26
  373.3 0.0 copy-done.4
  373.3 1.4 convert_bitcast_fusion.1
  374.7 0.0 copy-done.1
  374.7 0.0 copy-start
  374.7 1.6 convert_element_type.31
  376.3 0.0 copy-done
  376.3 0.2 convert_bitcast_fusion
  376.5 0.0 copy-start.3
  376.5 1.8 copy.27
  378.3 0.0 copy-done.3
  378.3 0.0 copy-start.2
  378.3 1.0 copy.30
  379.3 0.6 copy-done.2
  379.9 1.0 copy.31
Async XLA Ops:
  368.4 4.9 %copy-start.4 = (bf16[3,256,512]{2,1,0:T(8,128)(2,1)S(1)}, bf16[3,256,512]{2,1,0:T(8,128)(2,1)}, u32[]{:S(2)}) copy-start(bf16[3,256,512]{2,1,0:T(8,128)(2,1)} %get-tuple-element.58) | copy-start | bytes 2359300
  371.2 3.5 copy-start.1
  374.7 1.6 copy-start
  376.5 1.8 copy-start.3
  378.3 1.6 copy-start.2
